TPU v7x, 32 devices: a whole 2x2x4 slice. The times are simulated.
32 devices in a mesh: batch: 16 (over z, y, core), seq: 2 (over x).
Axes of the slice: x: 2, y: 2, z: 4, core: 2. Of those that a mesh axis runs over, the one named last changes fastest.
Arguments:
- tokens_in: bfloat16 [32, 1024, 768], P('batch', 'seq'), may hold values from -6 to 6
- doc_starts: int32 [32, 4], P('batch'), may hold values from 0 to 1023, as said below
- norm1_gain: bfloat16 [768], P(('batch', 'seq')), may hold values from 0.5 to 1.5
- norm1_bias: bfloat16 [768], P(('batch', 'seq')), may hold values from -3 to 3
- qkv_weight: bfloat16 [768, 2304], P(('batch', 'seq')), may hold values from -0.3125 to 0.3125
- query_bias: bfloat16 [768], P(('batch', 'seq')), may hold values from -3 to 3
- value_bias: bfloat16 [768], P(('batch', 'seq')), may hold values from -3 to 3
- attn_weight: bfloat16 [768, 768], P(('batch', 'seq')), may hold values from -1.75 to 1.75
- attn_bias: bfloat16 [768], P(('batch', 'seq')), may hold values from -3 to 3
- norm2_gain: bfloat16 [768], P(('batch', 'seq')), may hold values from 0.5 to 1.5
- norm2_bias: bfloat16 [768], P(('batch', 'seq')), may hold values from -3 to 3
- fc_weight: bfloat16 [768, 3072], P(('batch', 'seq')), may hold values from -0.21875 to 0.21875
- fc_bias: bfloat16 [3072], P(('batch', 'seq')), may hold values from -3 to 3
- proj_weight: bfloat16 [3072, 768], P(('batch', 'seq')), may hold values from -0.109375 to 0.109375
- proj_bias: bfloat16 [768], P(('batch', 'seq')), may hold values from -4 to 4
- out_grad: bfloat16 [32, 1024, 768], P('batch', 'seq'), may hold values from -6 to 6
Outputs:
- block_out: bfloat16 [32, 1024, 768], P('batch', 'seq')
- tokens_grad: float32 [32, 1024, 768], P('batch', 'seq')
- norm1_gain_grad: float32 [768], P(('batch', 'seq'))
- norm1_bias_grad: float32 [768], P(('batch', 'seq'))
- qkv_weight_grad: float32 [768, 2304], P(('batch', 'seq'))
- query_bias_grad: float32 [768], P(('batch', 'seq'))
- value_bias_grad: float32 [768], P(('batch', 'seq'))
- attn_weight_grad: float32 [768, 768], P(('batch', 'seq'))
- attn_bias_grad: float32 [768], P(('batch', 'seq'))
- norm2_gain_grad: float32 [768], P(('batch', 'seq'))
- norm2_bias_grad: float32 [768], P(('batch', 'seq'))
- fc_weight_grad: float32 [768, 3072], P(('batch', 'seq'))
- fc_bias_grad: float32 [3072], P(('batch', 'seq'))
- proj_weight_grad: float32 [3072, 768], P(('batch', 'seq'))
- proj_bias_grad: float32 [768], P(('batch', 'seq'))
Inputs may be any that keep to these rules, and one draw needn't show every extreme that they name: `doc_starts`: in every row the first start is 0 and the starts rise; for j >= 1 start j lies inside part j of the 4 equal parts of the row, counting parts from 0 and never on that part's first position. In one row of every draw the last start is 1023.
All inputs are finite; a program needn't handle non-finite values.
Results may differ from a plain program's by a relative error of at most 0.018.
Values may be sent and summed in bfloat16 or wider, within the bound.
A program may use at most 256 MiB of HBM per device.

v0:
```python
import math

import jax
import jax.numpy as jnp
from jax import lax
from jax.sharding import PartitionSpec as P

H = 12
HD = 64


EPSILON = 1e-05
GELU_SCALE = 0.7978845608028654
NEGATIVE = -1e30


def layer_norm(values, gain, shift):
    average = jnp.mean(values, axis=-1, keepdims=True)
    centered = values - average
    variance = jnp.mean(centered * centered, axis=-1, keepdims=True)
    return centered * lax.rsqrt(variance + EPSILON) * gain + shift


def gelu_tanh(values):
    return (
        0.5 * values * (1.0 + jnp.tanh(GELU_SCALE * (values + 0.044715 * values * values * values)))
    )


def segment_ids(doc_starts, length):
    positions = jnp.arange(length, dtype=jnp.int32)
    return (
        jnp.sum((doc_starts[:, None, :] <= positions[None, :, None]).astype(jnp.int32), axis=-1) - 1
    )


def contract_rows(left, right):
    return lax.dot_general(
        left, right, (((0,), (0,)), ((), ())), preferred_element_type=jnp.float32
    )


def contract_last(left, right):
    return lax.dot_general(
        left, right, (((1,), (1,)), ((), ())), preferred_element_type=jnp.float32
    )


def split_heads(block):
    return block.reshape(block.shape[0], block.shape[1], H, HD)


def merge_heads(block):
    return block.reshape(block.shape[0], block.shape[1], H * HD)


def take_block(values, block, length):
    return lax.dynamic_slice_in_dim(values, block * length, length, 1)


def block_scores(query_block, key_block, query_segments, key_segments, query_start, key_start):
    scores = jnp.einsum(
        "rqhd,rkhd->rhqk",
        split_heads(query_block),
        split_heads(key_block),
        preferred_element_type=jnp.float32,
    ) * (1.0 / math.sqrt(HD))
    query_places = query_start + jnp.arange(query_block.shape[1], dtype=jnp.int32)
    key_places = key_start + jnp.arange(key_block.shape[1], dtype=jnp.int32)
    allowed = (key_places[None, None, :] <= query_places[None, :, None]) & (
        key_segments[:, None, :] == query_segments[:, :, None]
    )
    return (scores, allowed[:, None, :, :])


def pair_grads(
    query_block,
    grad_block,
    log_block,
    delta_block,
    key_block,
    value_block,
    query_segments,
    key_segments,
    query_start,
    key_start,
):
    scores, allowed = block_scores(
        query_block, key_block, query_segments, key_segments, query_start, key_start
    )
    probs = jnp.where(allowed, jnp.exp(scores - log_block[..., None]), 0.0)
    probs_low = probs.astype(jnp.bfloat16)
    value_grad = jnp.einsum(
        "rhqk,rqhd->rkhd", probs_low, split_heads(grad_block), preferred_element_type=jnp.float32
    )
    prob_grad = jnp.einsum(
        "rqhd,rkhd->rhqk",
        split_heads(grad_block),
        split_heads(value_block),
        preferred_element_type=jnp.float32,
    )
    score_grad = (probs * (prob_grad - delta_block[..., None])).astype(jnp.bfloat16)
    query_grad = jnp.einsum(
        "rhqk,rkhd->rqhd", score_grad, split_heads(key_block), preferred_element_type=jnp.float32
    ) * (1.0 / math.sqrt(HD))
    key_grad = jnp.einsum(
        "rhqk,rqhd->rkhd", score_grad, split_heads(query_block), preferred_element_type=jnp.float32
    ) * (1.0 / math.sqrt(HD))
    return (merge_heads(query_grad), merge_heads(key_grad), merge_heads(value_grad))


def shards(
    tokens_in,
    doc_starts,
    norm1_gain,
    norm1_bias,
    qkv_weight,
    query_bias,
    value_bias,
    attn_weight,
    attn_bias,
    norm2_gain,
    norm2_bias,
    fc_weight,
    fc_bias,
    proj_weight,
    proj_bias,
    out_grad,
):
    gathered = (
        lax.all_gather(norm1_gain, ("batch", "seq"), axis=0, tiled=True),
        lax.all_gather(norm1_bias, ("batch", "seq"), axis=0, tiled=True),
        lax.all_gather(qkv_weight, ("batch", "seq"), axis=0, tiled=True),
        lax.all_gather(query_bias, ("batch", "seq"), axis=0, tiled=True),
        lax.all_gather(value_bias, ("batch", "seq"), axis=0, tiled=True),
        lax.all_gather(attn_weight, ("batch", "seq"), axis=0, tiled=True),
        lax.all_gather(attn_bias, ("batch", "seq"), axis=0, tiled=True),
        lax.all_gather(norm2_gain, ("batch", "seq"), axis=0, tiled=True),
        lax.all_gather(norm2_bias, ("batch", "seq"), axis=0, tiled=True),
        lax.all_gather(fc_weight, ("batch", "seq"), axis=0, tiled=True),
        lax.all_gather(fc_bias, ("batch", "seq"), axis=0, tiled=True),
        lax.all_gather(proj_weight, ("batch", "seq"), axis=0, tiled=True),
        lax.all_gather(proj_bias, ("batch", "seq"), axis=0, tiled=True),
    )
    gain_one = gathered[0].astype(jnp.float32)
    shift_one = gathered[1].astype(jnp.float32)
    qkv_full = gathered[2]
    attn_full = gathered[5]
    gain_two = gathered[7].astype(jnp.float32)
    shift_two = gathered[8].astype(jnp.float32)
    fc_full = gathered[9]
    proj_full = gathered[11]
    rows, local, width = tokens_in.shape
    seq_count = lax.axis_size("seq")
    seq_index = lax.axis_index("seq")
    offset = seq_index * local
    segments = segment_ids(doc_starts, local * seq_count)
    query_segments = lax.dynamic_slice_in_dim(segments, offset, local, 1)
    flat = tokens_in.reshape(rows * local, width).astype(jnp.float32)
    normed, norm_back_one = jax.vjp(layer_norm, flat, gain_one, shift_one)
    normed_low = normed.astype(jnp.bfloat16)
    joined_bias = jnp.concatenate([gathered[3], jnp.zeros_like(gathered[3]), gathered[4]]).astype(
        jnp.float32
    )
    projected = jnp.dot(normed_low, qkv_full, preferred_element_type=jnp.float32) + joined_bias
    queries = projected[:, :width].astype(jnp.bfloat16).reshape(rows, local, width)
    keys = projected[:, width : 2 * width].astype(jnp.bfloat16).reshape(rows, local, width)
    values = projected[:, 2 * width :].astype(jnp.bfloat16).reshape(rows, local, width)
    keys_all, values_all = (
        lax.all_gather(keys, "seq", axis=1, tiled=True),
        lax.all_gather(values, "seq", axis=1, tiled=True),
    )

    def max_step(block, carry):
        top, total = carry
        scores, allowed = block_scores(
            queries,
            take_block(keys_all, block, local),
            query_segments,
            take_block(segments, block, local),
            offset,
            block * local,
        )
        masked = jnp.where(allowed, scores, NEGATIVE)
        new_top = jnp.maximum(top, jnp.max(masked, axis=-1))
        added = jnp.sum(jnp.where(allowed, jnp.exp(masked - new_top[..., None]), 0.0), axis=-1)
        return (new_top, total * jnp.exp(top - new_top) + added)

    start_top = jnp.full((rows, H, local), NEGATIVE, jnp.float32)
    top, total = lax.fori_loop(
        0, seq_index + 1, max_step, (start_top, jnp.zeros((rows, H, local), jnp.float32))
    )
    log_total = top + jnp.log(total)

    def value_step(block, mixed):
        scores, allowed = block_scores(
            queries,
            take_block(keys_all, block, local),
            query_segments,
            take_block(segments, block, local),
            offset,
            block * local,
        )
        probs_low = jnp.where(allowed, jnp.exp(scores - log_total[..., None]), 0.0).astype(
            jnp.bfloat16
        )
        return mixed + jnp.einsum(
            "rhqk,rkhd->rqhd",
            probs_low,
            split_heads(take_block(values_all, block, local)),
            preferred_element_type=jnp.float32,
        )

    attended = lax.fori_loop(
        0, seq_index + 1, value_step, jnp.zeros((rows, local, H, HD), jnp.float32)
    )
    attended = attended.reshape(rows * local, width)
    attended_low = attended.astype(jnp.bfloat16)
    middle = (
        flat
        + jnp.dot(attended_low, attn_full, preferred_element_type=jnp.float32)
        + gathered[6].astype(jnp.float32)
    )
    normed_two, norm_back_two = jax.vjp(layer_norm, middle, gain_two, shift_two)
    normed_two_low = normed_two.astype(jnp.bfloat16)
    pre_act = jnp.dot(normed_two_low, fc_full, preferred_element_type=jnp.float32) + gathered[
        10
    ].astype(jnp.float32)
    hidden, gelu_back = jax.vjp(gelu_tanh, pre_act)
    hidden_low = hidden.astype(jnp.bfloat16)
    result = (
        middle
        + jnp.dot(hidden_low, proj_full, preferred_element_type=jnp.float32)
        + gathered[12].astype(jnp.float32)
    )
    block_out = result.astype(jnp.bfloat16).reshape(rows, local, width)
    upstream = out_grad.reshape(rows * local, width)
    upstream_float = upstream.astype(jnp.float32)
    proj_weight_grad = contract_rows(hidden_low, upstream)
    proj_bias_grad = jnp.sum(upstream_float, axis=0)
    hidden_grad = contract_last(upstream, proj_full)
    pre_grad = gelu_back(hidden_grad)[0].astype(jnp.bfloat16)
    fc_weight_grad = contract_rows(normed_two_low, pre_grad)
    fc_bias_grad = jnp.sum(pre_grad.astype(jnp.float32), axis=0)
    norm_two_input = contract_last(pre_grad, fc_full)
    middle_part, norm2_gain_grad, norm2_bias_grad = norm_back_two(norm_two_input)
    middle_grad = upstream_float + middle_part
    branch_grad = middle_grad.astype(jnp.bfloat16)
    attn_weight_grad = contract_rows(attended_low, branch_grad)
    attn_bias_grad = jnp.sum(branch_grad.astype(jnp.float32), axis=0)
    attended_grad = contract_last(branch_grad, attn_full).astype(jnp.bfloat16)
    delta = jnp.sum(
        (attended_grad.astype(jnp.float32) * attended).reshape(rows, local, H, HD), axis=-1
    )
    delta = jnp.swapaxes(delta, 1, 2)
    attended_grad = attended_grad.reshape(rows, local, width)

    def grad_step(block, carry):
        query_grad, key_full, value_full = carry
        part_query, part_key, part_value = pair_grads(
            queries,
            attended_grad,
            log_total,
            delta,
            take_block(keys_all, block, local),
            take_block(values_all, block, local),
            query_segments,
            take_block(segments, block, local),
            offset,
            block * local,
        )
        key_full = lax.dynamic_update_slice_in_dim(
            key_full, take_block(key_full, block, local) + part_key, block * local, 1
        )
        value_full = lax.dynamic_update_slice_in_dim(
            value_full, take_block(value_full, block, local) + part_value, block * local, 1
        )
        return (query_grad + part_query, key_full, value_full)

    empty_full = jnp.zeros((rows, local * seq_count, width), jnp.float32)
    query_grad, key_full, value_full = lax.fori_loop(
        0,
        seq_index + 1,
        grad_step,
        (jnp.zeros((rows, local, width), jnp.float32), empty_full, empty_full),
    )
    key_grad, value_grad = (
        lax.psum_scatter(
            key_full.astype(jnp.bfloat16), "seq", scatter_dimension=1, tiled=True
        ).astype(jnp.float32),
        lax.psum_scatter(
            value_full.astype(jnp.bfloat16), "seq", scatter_dimension=1, tiled=True
        ).astype(jnp.float32),
    )
    qkv_grad = (
        jnp.concatenate([query_grad, key_grad, value_grad], axis=-1)
        .astype(jnp.bfloat16)
        .reshape(rows * local, 3 * width)
    )
    qkv_weight_grad = contract_rows(normed_low, qkv_grad)
    qkv_grad_float = qkv_grad.astype(jnp.float32)
    query_bias_grad = jnp.sum(qkv_grad_float[:, :width], axis=0)
    value_bias_grad = jnp.sum(qkv_grad_float[:, 2 * width :], axis=0)
    normed_grad = contract_last(qkv_grad, qkv_full)
    flat_part, norm1_gain_grad, norm1_bias_grad = norm_back_one(normed_grad)
    tokens_grad = (middle_grad + flat_part).reshape(rows, local, width)
    shares = (
        lax.psum_scatter(norm1_gain_grad, ("batch", "seq"), scatter_dimension=0, tiled=True),
        lax.psum_scatter(norm1_bias_grad, ("batch", "seq"), scatter_dimension=0, tiled=True),
        lax.psum_scatter(qkv_weight_grad, ("batch", "seq"), scatter_dimension=0, tiled=True),
        lax.psum_scatter(query_bias_grad, ("batch", "seq"), scatter_dimension=0, tiled=True),
        lax.psum_scatter(value_bias_grad, ("batch", "seq"), scatter_dimension=0, tiled=True),
        lax.psum_scatter(attn_weight_grad, ("batch", "seq"), scatter_dimension=0, tiled=True),
        lax.psum_scatter(attn_bias_grad, ("batch", "seq"), scatter_dimension=0, tiled=True),
        lax.psum_scatter(norm2_gain_grad, ("batch", "seq"), scatter_dimension=0, tiled=True),
        lax.psum_scatter(norm2_bias_grad, ("batch", "seq"), scatter_dimension=0, tiled=True),
        lax.psum_scatter(fc_weight_grad, ("batch", "seq"), scatter_dimension=0, tiled=True),
        lax.psum_scatter(fc_bias_grad, ("batch", "seq"), scatter_dimension=0, tiled=True),
        lax.psum_scatter(proj_weight_grad, ("batch", "seq"), scatter_dimension=0, tiled=True),
        lax.psum_scatter(proj_bias_grad, ("batch", "seq"), scatter_dimension=0, tiled=True),
    )
    return (block_out, tokens_grad) + tuple(shares)


def solution(mesh):
    return jax.shard_map(
        shards,
        mesh=mesh,
        in_specs=(
            P("batch", "seq", None),
            P("batch", None),
            P(("batch", "seq")),
            P(("batch", "seq")),
            P(("batch", "seq"), None),
            P(("batch", "seq")),
            P(("batch", "seq")),
            P(("batch", "seq"), None),
            P(("batch", "seq")),
            P(("batch", "seq")),
            P(("batch", "seq")),
            P(("batch", "seq"), None),
            P(("batch", "seq")),
            P(("batch", "seq"), None),
            P(("batch", "seq")),
            P("batch", "seq", None),
        ),
        out_specs=(
            P("batch", "seq", None),
            P("batch", "seq", None),
            P(("batch", "seq")),
            P(("batch", "seq")),
            P(("batch", "seq"), None),
            P(("batch", "seq")),
            P(("batch", "seq")),
            P(("batch", "seq"), None),
            P(("batch", "seq")),
            P(("batch", "seq")),
            P(("batch", "seq")),
            P(("batch", "seq"), None),
            P(("batch", "seq")),
            P(("batch", "seq"), None),
            P(("batch", "seq")),
        ),
        check_vma=False,
    )
```

profile of v0, /device:TPU:0, one launch (start us, length us, event | category | flops | bytes accessed | tf_op | source)
XLA Modules:
  0.0 1236.0 jit_solution(13928194495678824608)
XLA Ops:
  14.0 42.8 %all-reduce.19 = (bf16[768]{0:T(1024)(128)(2,1)S(1)}, bf16[768]{0:T(1024)(128)(2,1)S(1)}, bf16[768]{0:T(1024)(128)(2,1)S(1)}, bf16[768]{0:T(1024)(128)(2,1)S(1)}...) all-reduce(bf16[768]{0:T(1024)(128)(2,1)S(1)} %dynamic-update-slice, ...), channel_id=1, replica_groups=mesh['batch'=16,'seq'=2] {'batch','seq'}, use_global_device_ids=true, to_apply=%add.4 | all-reduce | flops 9216 | bytes 36864
  58.0 16.3 %all-gather.7.cloned.1.call-done = bf16[768,2304]{1,0:T(8,128)(2,1)} async-done(((bf16[24,2304]{1,0:T(8,128)(2,1)}), bf16[768,2304]{1,0:T(8,128)(2,1)}) %all-gather.7.cloned.1.call-update) | async-done | bytes 3538960 | tf_op jit(solution)/shard_map/all_gather | solution.py:133
  97.7 30.6 %all-gather.11.cloned.1.call-done = bf16[2,1024,768]{1,2,0:T(8,128)(2,1)} async-done(((bf16[2,512,768]{1,2,0:T(8,128)(2,1)}), bf16[2,1024,768]{1,2,0:T(8,128)(2,1)}) %all-gather.11.cloned.1.call-update) | async-done | bytes 3145744 | tf_op jit(solution)/shard_map/all_gather | solution.py:170
  128.3 25.5 %while.39 = (s32[]{:T(128)}, f32[2,12,512]{2,1,0:T(8,128)S(1)}, f32[2,12,512]{2,1,0:T(8,128)S(1)}, s32[]{:T(128)}, s32[]{:T(128)}, /*index=5*/s32[2,1024]{1,0:T(...) while((s32[]{:T(128)}, f32[2,12,512]{2,1,0:T(8,128)S(1)}, ...), condition=%wide.wide.region_6.7_spmd, body=%wide.wide.region_3.6_spmd.sunk | while | flops 856974336 | bytes 59384000 | solution.py:190
  130.5 11.7 fusion.126
  142.2 11.5 select_reduce_fusion.3
  153.8 21.6 %all-gather.9.cloned.1.call-done = bf16[2,1024,768]{1,2,0:T(8,128)(2,1)} async-done(((bf16[2,512,768]{1,2,0:T(8,128)(2,1)}), bf16[2,1024,768]{1,2,0:T(8,128)(2,1)}) %all-gather.9.cloned.1.call-update) | async-done | bytes 3145744 | tf_op jit(solution)/shard_map/all_gather | solution.py:171
  177.4 16.6 %while.40 = (s32[]{:T(128)}, f32[2,512,12,64]{1,3,2,0:T(8,128)}, s32[]{:T(128)}, bf16[2,1024,768]{1,2,0:T(8,128)(2,1)}, s32[]{:T(128)}, /*index=5*/s32[2,1024]{1...) while((s32[]{:T(128)}, f32[2,512,12,64]{1,3,2,0:T(8,128)}, ...), condition=%wide.wide.region_8.9_spmd, body=%wide.wide.region_7.8_spmd.sunk | while | flops 1637876736 | bytes 18948300 | solution.py:214
  182.3 11.6 bitcast_add_fusion.13
  204.4 27.9 %all-gather.13.cloned.1.call-done = bf16[768,768]{1,0:T(8,128)(2,1)} async-done(((bf16[24,768]{1,0:T(8,128)(2,1)}), bf16[768,768]{1,0:T(8,128)(2,1)}) %all-gather.13.cloned.1.call-update) | async-done | bytes 1179664 | tf_op jit(solution)/shard_map/all_gather | solution.py:136
  238.5 59.2 %all-gather.15.cloned.1.call-done = bf16[768,3072]{1,0:T(8,128)(2,1)} async-done(((bf16[24,3072]{1,0:T(8,128)(2,1)}), bf16[768,3072]{1,0:T(8,128)(2,1)}) %all-gather.15.cloned.1.call-update) | async-done | bytes 4718608 | tf_op jit(solution)/shard_map/all_gather | solution.py:140
  297.7 11.1 fusion.56
  308.8 54.2 %all-gather.17.cloned.1.call-done = bf16[3072,768]{1,0:T(8,128)(2,1)} async-done(((bf16[96,768]{1,0:T(8,128)(2,1)}), bf16[3072,768]{1,0:T(8,128)(2,1)}) %all-gather.17.cloned.1.call-update) | async-done | bytes 4718608 | tf_op jit(solution)/shard_map/all_gather | solution.py:142
  362.9 18.3 %convert_reduce_fusion = (f32[3072]{0:T(1024)}, bf16[1024,3072]{1,0:T(8,128)(2,1)S(1)}) fusion(bf16[1024,768]{1,0:T(8,128)(2,1)S(1)} %bitcast.204, bf16[3072,768]{1,0:T(8,128)(2,1)} %all-gather.17.cloned.1.call-done, f32[1024,3072]{1,0:T(8,128)} %fusion.56, f32[3072]{0:T(1024)S(1)} %copy-done.52), kind=kOutput, calls=%fused_computation.67 | convolution fusion | flops 4916769792 | bytes 25190400 | tf_op jit(solution)/shard_map/dot_general | solution.py:44
  381.3 10.8 multiply_reduce_fusion
  421.5 100.9 %while.41 = (s32[]{:T(128)}, f32[2,512,768]{1,2,0:T(8,128)}, f32[2,1024,768]{2,1,0:T(8,128)}, f32[2,1024,768]{2,1,0:T(8,128)}, s32[]{:T(128)}, /*index=5*/bf16[2...) while((s32[]{:T(128)}, f32[2,512,768]{1,2,0:T(8,128)}, ...), condition=%wide.wide.region_15.16_spmd, body=%wide.wide.region_14.15_spmd.sunk | while | flops 4094690304 | bytes 292200928 | solution.py:281
  441.3 10.1 fusion.141
  451.5 12.4 %fusion.143 = f32[2,12,512,64]{2,3,1,0:T(8,128)} fusion(f32[2,12,512,512]{3,2,1,0:T(8,128)} %fusion.141, f32[2,12,512]{2,1,0:T(8,128)S(1)} %get-tuple-element.956, pred[2,512,512]{1,2,0:T(8,128)(4,1)S(1)} %copy-done.20, bf16[2,512,12,64]{1,0,3,2:T(2,128)(2,1)S(1)} %copy-done.31), kind=kOutput, calls=%fused_computation.32.clone.clone.1 | convolution fusion | flops 830472192 | bytes 30457856 | tf_op jit(solution)/shard_map/while/body/rhqk,rqhd->rkhd/dot_general | solution.py:93
  463.9 16.1 %fusion.142 = bf16[2,12,512,512]{2,3,1,0:T(8,128)(2,1)} fusion(f32[2,12,512,512]{3,2,1,0:T(8,128)} %fusion.141, f32[2,12,512]{2,1,0:T(8,128)S(1)} %get-tuple-element.959, f32[2,12,512]{2,1,0:T(8,128)S(1)} %get-tuple-element.956, pred[2,512,512]{1,2,0:T(8,128)(4,1)} %compare_and_fusion.11, bf16[2,512,12,64]{1,3,2,0:T(8,128)(2,1)} %bitcast.201, ...), kind=kOutput, calls=%fused_computation.29.clone.clone.1 | convolution fusion | flops 843055104 | bytes 41517056 | tf_op jit(solution)/shard_map/while/body/rqhd,rkhd->rhqk/dot_general | solution.py:96
  487.9 7.1 convolution_multiply_fusion.6
  495.0 10.6 convolution_multiply_fusion.7
  537.7 10.7 fusion.55
  549.8 12.8 %fusion.57 = f32[3072,768]{1,0:T(8,128)} fusion(bf16[1024,768]{1,0:T(8,128)(2,1)S(1)} %bitcast.205, f32[1024,3072]{1,0:T(8,128)} %fusion.56, f32[3072]{0:T(1024)S(1)} %copy-done.53), kind=kOutput, calls=%fused_computation.128 | convolution fusion | flops 4863295488 | bytes 23605248 | tf_op jit(solution)/shard_map/dot_general | solution.py:38
  566.3 103.7 %reduce-scatter.9.cloned.1.call-done = bf16[2,512,768]{2,1,0:T(8,128)(2,1)} async-done(((bf16[2,1024,768]{2,1,0:T(8,128)(2,1)}), bf16[2,512,768]{2,1,0:T(8,128)(2,1)}) %reduce-scatter.9.cloned.1.call-update) | async-done | bytes 1572880 | tf_op jit(solution)/shard_map/reduce_scatter | solution.py:291
  670.0 45.7 %reduce-scatter.7.cloned.1.call-done = bf16[2,512,768]{2,1,0:T(8,128)(2,1)} async-done(((bf16[2,1024,768]{2,1,0:T(8,128)(2,1)}), bf16[2,512,768]{2,1,0:T(8,128)(2,1)}) %reduce-scatter.7.cloned.1.call-update) | async-done | bytes 1572880 | tf_op jit(solution)/shard_map/reduce_scatter | solution.py:288
  715.7 9.5 fusion.52
  727.0 13.7 %add_convert_fusion.1 = bf16[1024,768]{1,0:T(8,128)(2,1)} fusion(f32[1024,768]{1,0:T(8,128)} %copy-done.12, bf16[3072,768]{1,0:T(8,128)(2,1)} %all-gather.17.cloned.1.call-done, f32[768]{0:T(1024)S(1)} %convert_element_type.120, f32[1024,3072]{1,0:T(8,128)} %fusion.56, f32[3072]{0:T(1024)S(1)} %copy-done.53), kind=kOutput, calls=%fused_computation.98 | convolution fusion | flops 4865654784 | bytes 22035456 | tf_op jit(solution)/shard_map/dot_general | solution.py:233
  750.5 40.5 %all-reduce.18 = (f32[768]{0:T(1024)S(1)}, f32[768]{0:T(1024)S(1)}, f32[768]{0:T(1024)S(1)}, f32[768]{0:T(1024)S(1)}, f32[768]{0:T(1024)S(1)}, /*index=5*/f32[76...) all-reduce(f32[768]{0:T(1024)S(1)} %get-tuple-element.311, ...), channel_id=4, replica_groups=mesh['batch'=16,'seq'=2] {'batch','seq'}, use_global_device_ids=true, to_apply=%region_21.22.clone | all-reduce | flops 9216 | bytes 73728
  801.0 19.7 %reduce-scatter.13.cloned.1.call-done = f32[24,768]{1,0:T(8,128)} async-done(((f32[768,768]{1,0:T(8,128)}), f32[24,768]{1,0:T(8,128)}) %reduce-scatter.13.cloned.1.call-update) | async-done | bytes 73744 | tf_op jit(solution)/shard_map/reduce_scatter | solution.py:313
  820.7 141.8 %reduce-scatter.15.cloned.1.call-done = f32[24,3072]{1,0:T(8,128)} async-done(((f32[768,3072]{1,0:T(8,128)}), f32[24,3072]{1,0:T(8,128)}) %reduce-scatter.15.cloned.1.call-update) | async-done | bytes 294928 | tf_op jit(solution)/shard_map/reduce_scatter | solution.py:317
  962.5 141.2 %reduce-scatter.17.cloned.1.call-done = f32[96,768]{1,0:T(8,128)} async-done(((f32[3072,768]{1,0:T(8,128)}), f32[96,768]{1,0:T(8,128)}) %reduce-scatter.17.cloned.1.call-update) | async-done | bytes 294928 | tf_op jit(solution)/shard_map/reduce_scatter | solution.py:319
  1103.7 125.2 %reduce-scatter.11.cloned.1.call-done = f32[24,2304]{1,0:T(8,128)} async-done(((f32[768,2304]{1,0:T(8,128)}), f32[24,2304]{1,0:T(8,128)}) %reduce-scatter.11.cloned.1.call-update) | async-done | bytes 221200 | tf_op jit(solution)/shard_map/reduce_scatter | solution.py:310
  (286 shorter events, 171.5 us)
Async XLA Ops:
  7.2 50.2 %copy-start.9 = (bf16[2,512,768]{2,1,0:T(8,128)(2,1)S(1)}, bf16[2,512,768]{2,1,0:T(8,128)(2,1)}, u32[]{:S(2)}) copy-start(bf16[2,512,768]{2,1,0:T(8,128)(2,1)} %param.22) | copy-start | bytes 4718596
  7.3 67.0 %all-gather.7.cloned.1.call-start = ((), (), s32[]{:S(2)}) async-start(), calls=%async_computation.6 | async-start | bytes 3649536 | tf_op jit(solution)/shard_map/all_gather | solution.py:133
  8.0 120.2 %all-gather.11.cloned.1.call-start = ((), (), s32[]{:S(2)}) async-start(), calls=%async_computation.8 | async-start | bytes 4718592 | tf_op jit(solution)/shard_map/all_gather | solution.py:170
  9.8 70.5 %copy-start.39 = (f32[1,4,2,128]{3,1,2,0:T(4,128)}, f32[1,4,2,128]{3,1,2,0:T(4,128)S(1)}, u32[]{:S(2)}) copy-start(f32[1,4,2,128]{3,1,2,0:T(4,128)S(1)} %copy.137) | copy-start | bytes 12292
  11.8 45.0 %copy-start.49 = (f32[1,4,2,128]{3,1,2,0:T(4,128)}, f32[1,4,2,128]{3,1,2,0:T(4,128)S(1)}, u32[]{:S(2)}) copy-start(f32[1,4,2,128]{3,1,2,0:T(4,128)S(1)} %copy.138) | copy-start | bytes 12292
  11.8 68.5 %copy-start.41 = (f32[1024]{0:T(1024)}, f32[1024]{0:T(1024)S(1)}, u32[]{:S(2)}) copy-start(f32[1024]{0:T(1024)S(1)} %rsqrt.20) | copy-start | bytes 12292
  58.0 16.3 %copy-start.30 = (bf16[1024,768]{1,0:T(8,128)(2,1)}, bf16[1024,768]{1,0:T(8,128)(2,1)S(1)}, u32[]{:S(2)}) copy-start(bf16[1024,768]{1,0:T(8,128)(2,1)S(1)} %fusion.39) | copy-start | bytes 4718596
  84.4 91.0 %all-gather.9.cloned.1.call-start = ((), (), s32[]{:S(2)}) async-start(), calls=%async_computation.7 | async-start | bytes 4718592 | tf_op jit(solution)/shard_map/all_gather | solution.py:171
  86.0 146.3 %all-gather.13.cloned.1.call-start = ((), (), s32[]{:S(2)}) async-start(), calls=%async_computation.9 | async-start | bytes 1216512 | tf_op jit(solution)/shard_map/all_gather | solution.py:136
  86.6 211.1 %all-gather.15.cloned.1.call-start = ((), (), s32[]{:S(2)}) async-start(), calls=%async_computation.10 | async-start | bytes 4866048 | tf_op jit(solution)/shard_map/all_gather | solution.py:140
  87.2 275.7 %all-gather.17.cloned.1.call-start = ((), (), s32[]{:S(2)}) async-start(), calls=%async_computation.11 | async-start | bytes 4866048 | tf_op jit(solution)/shard_map/all_gather | solution.py:142
  87.8 582.2 %reduce-scatter.9.cloned.1.call-start = ((), (), s32[]{:S(2)}) async-start(), calls=%async_computation.13 | async-start | bytes 4718592 | tf_op jit(solution)/shard_map/reduce_scatter | solution.py:291
  153.8 23.7 %copy-start.6 = (bf16[2,1024,768]{1,2,0:T(8,128)(2,1)S(1)}, bf16[2,1024,768]{1,2,0:T(8,128)(2,1)}, u32[]{:S(2)}) copy-start(bf16[2,1024,768]{1,2,0:T(8,128)(2,1)} %get-tuple-element.1000) | copy-start | bytes 9437188
  200.8 31.5 %copy-start.10 = (bf16[2,512,768]{2,1,0:T(8,128)(2,1)S(1)}, bf16[2,512,768]{2,1,0:T(8,128)(2,1)}, u32[]{:S(2)}) copy-start(bf16[2,512,768]{2,1,0:T(8,128)(2,1)} %param.22) | copy-start | bytes 4718596
  200.8 31.5 %copy-start.55 = (f32[768]{0:T(1024)S(1)}, f32[768]{0:T(1024)}, u32[]{:S(2)}) copy-start(f32[768]{0:T(1024)} %convert_element_type.114) | copy-start | bytes 9220
  236.2 61.5 %copy-start.37 = (f32[768]{0:T(1024)S(1)}, f32[768]{0:T(1024)}, u32[]{:S(2)}) copy-start(f32[768]{0:T(1024)} %convert_element_type.115) | copy-start | bytes 9220
  236.2 61.5 %copy-start.45 = (f32[768]{0:T(1024)S(1)}, f32[768]{0:T(1024)}, u32[]{:S(2)}) copy-start(f32[768]{0:T(1024)} %convert_element_type.116) | copy-start | bytes 9220
  236.3 155.9 %copy-start.33 = (f32[1024]{0:T(1024)}, f32[1024]{0:T(1024)S(1)}, u32[]{:S(2)}) copy-start(f32[1024]{0:T(1024)S(1)} %broadcast_multiply_fusion) | copy-start | bytes 12292
  238.4 153.7 %copy-start.35 = (f32[1024]{0:T(1024)}, f32[1024]{0:T(1024)S(1)}, u32[]{:S(2)}) copy-start(f32[1024]{0:T(1024)S(1)} %fusion.49) | copy-start | bytes 12292
  238.4 124.5 %copy-start.17 = (bf16[2,512,768]{2,1,0:T(8,128)(2,1)S(1)}, bf16[2,512,768]{2,1,0:T(8,128)(2,1)}, u32[]{:S(2)}) copy-start(bf16[2,512,768]{2,1,0:T(8,128)(2,1)} %param.37) | copy-start | bytes 4718596
  238.4 124.5 %copy-start.52 = (f32[3072]{0:T(1024)S(1)}, f32[3072]{0:T(1024)}, u32[]{:S(2)}) copy-start(f32[3072]{0:T(1024)} %convert_element_type.118) | copy-start | bytes 36868
  362.9 18.4 %copy-start.13 = (f32[1024,768]{1,0:T(8,128)S(1)}, f32[1024,768]{1,0:T(8,128)}, u32[]{:S(2)}) copy-start(f32[1024,768]{1,0:T(8,128)} %copy-done.12) | copy-start | bytes 9437188
  426.1 15.3 %copy-start = (bf16[2,512,768]{1,2,0:T(8,128)(2,1)}, bf16[2,512,768]{1,2,0:T(8,128)(2,1)S(1)}, u32[]{:S(2)}) copy-start(bf16[2,512,768]{1,2,0:T(8,128)(2,1)S(1)} %constant_dynamic-slice_fusion.33) | copy-start | bytes 4718596 | tf_op jit(solution)/shard_map/while
  463.9 16.1 %copy-start.2 = (f32[2,512,768]{1,2,0:T(8,128)S(1)}, f32[2,512,768]{1,2,0:T(8,128)}, u32[]{:S(2)}) copy-start(f32[2,512,768]{1,2,0:T(8,128)} %copy.181) | copy-start | bytes 9437188 | tf_op jit(solution)/shard_map/while
  527.3 188.4 %reduce-scatter.7.cloned.1.call-start = ((), (), s32[]{:S(2)}) async-start(), calls=%async_computation.12 | async-start | bytes 4718592 | tf_op jit(solution)/shard_map/reduce_scatter | solution.py:288
  532.2 288.5 %reduce-scatter.13.cloned.1.call-start = ((), (), s32[]{:S(2)}) async-start(), calls=%async_computation.15 | async-start | bytes 2433024 | tf_op jit(solution)/shard_map/reduce_scatter | solution.py:313
  537.6 424.9 %reduce-scatter.15.cloned.1.call-start = ((), (), s32[]{:S(2)}) async-start(), calls=%async_computation.16 | async-start | bytes 9732096 | tf_op jit(solution)/shard_map/reduce_scatter | solution.py:317
  548.4 555.3 %reduce-scatter.17.cloned.1.call-start = ((), (), s32[]{:S(2)}) async-start(), calls=%async_computation.17 | async-start | bytes 9732096 | tf_op jit(solution)/shard_map/reduce_scatter | solution.py:319
  562.6 666.3 %reduce-scatter.11.cloned.1.call-start = ((), (), s32[]{:S(2)}) async-start(), calls=%async_computation.14 | async-start | bytes 7299072 | tf_op jit(solution)/shard_map/reduce_scatter | solution.py:310
  726.9 13.8 %copy-start.11 = (bf16[2,512,768]{2,1,0:T(8,128)(2,1)S(1)}, bf16[2,512,768]{2,1,0:T(8,128)(2,1)}, u32[]{:S(2)}) copy-start(bf16[2,512,768]{2,1,0:T(8,128)(2,1)} %param.22) | copy-start | bytes 4718596
  726.9 13.8 %copy-start.25 = (bf16[2,512,768]{2,1,0:T(8,128)(2,1)S(1)}, bf16[2,512,768]{2,1,0:T(8,128)(2,1)}, u32[]{:S(2)}) copy-start(bf16[2,512,768]{2,1,0:T(8,128)(2,1)} %copy.106) | copy-start | bytes 4718596
  748.2 48.0 %copy-start.48 = (f32[1024]{0:T(1024)S(1)}, f32[1024]{0:T(1024)}, u32[]{:S(2)}) copy-start(f32[1024]{0:T(1024)} %copy-done.47) | copy-start | bytes 12292
  (50 other events, 256.8 us)
Sparse Core Ops, SparseCore 0:
  11.0 63.1 all-gather.6
  84.5 43.7 all-gather.10
  130.4 44.9 all-gather.8
  178.1 54.1 all-gather.12
  235.1 62.5 all-gather.14
  300.5 62.4 all-gather.16
  527.4 142.5 reduce-scatter.8
  672.3 43.3 reduce-scatter.6
  721.6 99.0 reduce-scatter.12
  828.0 134.4 reduce-scatter.14
  969.0 134.6 reduce-scatter.16
  1110.7 118.1 reduce-scatter.10
where the time goes:
time: 1240 us
  waiting for transfers between devices  789 us (64%)
  matrix products  190 us (15%)
  local copies, waits for them, and re-layouts  95.2 us (8%)
  blocking collectives  83.3 us (7%)
  other arithmetic  61.5 us (5%)
  between operations  15.3 us (1%)
    reduce_scatter x1, waiting for transfers between devices, shards(): lax.psum_scatter(fc_weight_grad, ('batch', 'seq'), scatter_dimension=0, t...  142 us
    reduce_scatter x1, waiting for transfers between devices, shards(): lax.psum_scatter(proj_weight_grad, ('batch', 'seq'), scatter_dimension=0,...  141 us
    reduce_scatter x1, waiting for transfers between devices, shards(): lax.psum_scatter(qkv_weight_grad, ('batch', 'seq'), scatter_dimension=0,...  125 us
    reduce_scatter x1, waiting for transfers between devices, shards(): lax.psum_scatter(value_full.astype(jnp.bfloat16), 'seq', scatter_dimensio...  104 us
    unnamed x2, blocking collectives  83.3 us
    all_gather x1, waiting for transfers between devices, shards(): lax.all_gather(fc_weight, ('batch', 'seq'), axis=0, tiled=True)  59.2 us
    all_gather x1, waiting for transfers between devices, shards(): lax.all_gather(proj_weight, ('batch', 'seq'), axis=0, tiled=True)  54.2 us
    reduce_scatter x1, waiting for transfers between devices, shards(): lax.psum_scatter(key_full.astype(jnp.bfloat16), 'seq', scatter_dimension=...  45.7 us
  transfers between devices with their start and end apart: 12, of which 12 were waited for; matrix products, arithmetic and copies ran while one was open for 13% of the time, Pallas kernels for 0%

commit v1 on v0

--- a/solution.py
+++ b/solution.py
@@ -1,8 +1,11 @@
+import functools
 import math
 
 import jax
 import jax.numpy as jnp
 from jax import lax
+from jax.experimental import pallas as pl
+from jax.experimental.pallas import tpu as pltpu
 from jax.sharding import PartitionSpec as P
 
 H = 12
@@ -12,6 +15,339 @@
 EPSILON = 1e-05
 GELU_SCALE = 0.7978845608028654
 NEGATIVE = -1e30
+
+
+MESH_ID = pl.DeviceIdType.MESH
+VMEM_LIMIT = 60 * 2**20
+
+
+def place():
+    batch, seq = lax.axis_index("batch"), lax.axis_index("seq")
+    return (batch // 4, (batch // 2) % 2, batch % 2, seq)
+
+
+def device(a, y, c, s):
+    return (a * 4 + y * 2 + c, s)
+
+
+def greet(outer):
+    a, y, c, s = place()
+    barrier = pltpu.get_barrier_semaphore()
+    others = [device(lax.rem(a + k, outer), y, c, s) for k in range(1, outer)]
+    others += [device(a, 1 - y, c, s), device(a, y, c, 1 - s), device(a, y, 1 - c, s)]
+    for other in others:
+        pl.semaphore_signal(barrier, inc=1, device_id=other, device_id_type=MESH_ID)
+    pl.semaphore_wait(barrier, len(others))
+
+
+def gather_kernel(outer, pieces, count, *refs):
+    shards, outs = refs[:count], refs[count : 2 * count]
+    own_sem, send_sem, recv_sem = refs[2 * count :]
+    a, y, c, s = place()
+    greet(outer)
+    owns = []
+    for i in range(count):
+        own = pltpu.make_async_copy(shards[i], outs[i].at[a, y, c, s], own_sem.at[i])
+        own.start()
+        owns.append(own)
+
+    def z_copies(p):
+        i, start, width, order = pieces[p]
+        columns = pl.ds(start, width)
+        return [
+            pltpu.make_async_remote_copy(
+                src_ref=shards[i].at[:, columns],
+                dst_ref=outs[i].at[a, y, c, s, :, columns],
+                send_sem=send_sem.at[p, k - 1],
+                recv_sem=recv_sem.at[p, k - 1],
+                device_id=device(lax.rem(a + k, outer), y, c, s),
+                device_id_type=MESH_ID,
+            )
+            for k in range(1, outer)
+        ]
+
+    def later_copy(p, phase):
+        i, start, width, order = pieces[p]
+        columns = pl.ds(start, width)
+        every = slice(None)
+        if phase == 2:
+            index = (every, every, c, every)
+            other = device(a, y, 1 - c, s)
+        elif (phase == 0) == (order == 0):
+            index = (every, y, c, s if phase == 0 else every)
+            other = device(a, 1 - y, c, s)
+        else:
+            index = (every, y if phase == 0 else every, c, s)
+            other = device(a, y, c, 1 - s)
+        block = outs[i].at[index + (every, columns)]
+        return pltpu.make_async_remote_copy(
+            src_ref=block,
+            dst_ref=block,
+            send_sem=send_sem.at[p, outer - 1 + phase],
+            recv_sem=recv_sem.at[p, outer - 1 + phase],
+            device_id=other,
+            device_id_type=MESH_ID,
+        )
+
+    z_all = [z_copies(p) for p in range(len(pieces))]
+    later = [[later_copy(p, phase) for phase in range(3)] for p in range(len(pieces))]
+    lag = (1, 2, 4, 6)
+    for t in range(len(pieces) + lag[3]):
+        if t == 0:
+            for p in range(min(2, len(pieces))):
+                for copy in z_all[p]:
+                    copy.start()
+            for own in owns:
+                own.wait()
+        elif t + 1 < len(pieces):
+            for copy in z_all[t + 1]:
+                copy.start()
+        p = t - lag[0]
+        if 0 <= p < len(pieces):
+            for copy in z_all[p]:
+                copy.wait_recv()
+            later[p][0].start()
+        for phase in range(2):
+            p = t - lag[phase + 1]
+            if 0 <= p < len(pieces):
+                later[p][phase].wait_recv()
+                later[p][phase + 1].start()
+        p = t - lag[3]
+        if 0 <= p < len(pieces):
+            later[p][2].wait_recv()
+    for p in range(len(pieces)):
+        for copy in z_all[p] + later[p]:
+            copy.wait_send()
+
+
+def gather_all(outer, shards, pieces):
+    count = len(shards)
+    return pl.pallas_call(
+        functools.partial(gather_kernel, outer, pieces, count),
+        out_shape=[
+            jax.ShapeDtypeStruct((outer, 2, 2, 2) + shard.shape, shard.dtype) for shard in shards
+        ],
+        in_specs=[pl.BlockSpec(memory_space=pl.ANY)] * count,
+        out_specs=[pl.BlockSpec(memory_space=pl.ANY)] * count,
+        scratch_shapes=[
+            pltpu.SemaphoreType.DMA((count,)),
+            pltpu.SemaphoreType.DMA((len(pieces), outer + 2)),
+            pltpu.SemaphoreType.DMA((len(pieces), outer + 2)),
+        ],
+        compiler_params=pltpu.CompilerParams(collective_id=0, has_side_effects=True),
+    )(*shards)
+
+
+def scatter_kernel(outer, pieces, count, *refs):
+    terms, outs = refs[:count], refs[count : 2 * count]
+    rest = refs[2 * count :]
+    n = len(pieces)
+    held, first, second, third, fourth = (rest[k * n : (k + 1) * n] for k in range(5))
+    own_sem, send_sem, recv_sem = rest[5 * n :]
+    a, y, c, s = place()
+    greet(outer)
+    every = slice(None)
+
+    def remote(p, k, src, dst, other):
+        return pltpu.make_async_remote_copy(
+            src_ref=src,
+            dst_ref=dst,
+            send_sem=send_sem.at[p, k],
+            recv_sem=recv_sem.at[p, k],
+            device_id=other,
+            device_id_type=MESH_ID,
+        )
+
+    started = []
+
+    def core_start(p):
+        i, start, width, order = pieces[p]
+        columns = pl.ds(start, width)
+        own = pltpu.make_async_copy(
+            terms[i].at[:, :, c, :, :, columns], held[p], own_sem.at[p]
+        )
+        own.start()
+        copy = remote(
+            p, 0, terms[i].at[:, :, 1 - c, :, :, columns], first[p], device(a, y, 1 - c, s)
+        )
+        copy.start()
+        started.append(copy)
+        return (own, copy)
+
+    def add(target, other):
+        lead = target.shape[:-2]
+        total = math.prod(lead)
+
+        def body(k, carry):
+            index = []
+            for size in reversed(lead):
+                index.append(lax.rem(k, size))
+                k = k // size
+            index = tuple(reversed(index))
+            value = target[index].astype(jnp.float32) + other[index].astype(jnp.float32)
+            target[index] = value.astype(target.dtype)
+            return carry
+
+        lax.fori_loop(0, total, body, 0)
+
+    def first_half(p):
+        order = pieces[p][3]
+        if order == 0:
+            src, other = held[p].at[:, :, 1 - s], device(a, y, c, 1 - s)
+        else:
+            src, other = held[p].at[:, 1 - y], device(a, 1 - y, c, s)
+        copy = remote(p, 1, src, second[p], other)
+        copy.start()
+        started.append(copy)
+        return copy
+
+    def second_half(p):
+        order = pieces[p][3]
+        if order == 0:
+            src, other = held[p].at[:, 1 - y, s], device(a, 1 - y, c, s)
+        else:
+            src, other = held[p].at[:, y, 1 - s], device(a, y, c, 1 - s)
+        copy = remote(p, 2, src, third[p], other)
+        copy.start()
+        started.append(copy)
+        return copy
+
+    def z_start(p):
+        copies = []
+        for k in range(1, outer):
+            to = lax.rem(a + k, outer)
+            copy = remote(
+                p, 2 + k, held[p].at[to, y, s], fourth[p].at[k - 1], device(to, y, c, s)
+            )
+            copy.start()
+            started.append(copy)
+            copies.append(copy)
+        return copies
+
+    def finish(p):
+        i, start, width, order = pieces[p]
+        value = held[p][a, y, s].astype(jnp.float32)
+        for k in range(1, outer):
+            value = value + fourth[p][k - 1].astype(jnp.float32)
+        outs[i][:, pl.ds(start, width)] = value
+
+    core, one, two, z_all = {}, {}, {}, {}
+    for t in range(n + 6):
+        if t == 0:
+            for p in range(min(2, n)):
+                core[p] = core_start(p)
+        elif t + 1 < n:
+            core[t + 1] = core_start(t + 1)
+        p = t - 1
+        if 0 <= p < n:
+            for copy in core[p][:1]:
+                copy.wait()
+            core[p][1].wait_recv()
+            add(held[p], first[p])
+            one[p] = first_half(p)
+        p = t - 3
+        if 0 <= p < n:
+            one[p].wait_recv()
+            if pieces[p][3] == 0:
+                add(held[p].at[:, :, s], second[p])
+            else:
+                add(held[p].at[:, y], second[p])
+            two[p] = second_half(p)
+        p = t - 4
+        if 0 <= p < n:
+            two[p].wait_recv()
+            add(held[p].at[:, y, s], third[p])
+            z_all[p] = z_start(p)
+        p = t - 5
+        if 0 <= p < n:
+            for copy in z_all[p]:
+                copy.wait_recv()
+            finish(p)
+    for copy in started:
+        copy.wait_send()
+
+
+def scatter_all(outer, terms, pieces):
+    count = len(terms)
+    shape = lambda p, *lead: pltpu.VMEM(
+        lead + (terms[pieces[p][0]].shape[-2], pieces[p][2]), terms[pieces[p][0]].dtype
+    )
+    n = range(len(pieces))
+    return pl.pallas_call(
+        functools.partial(scatter_kernel, outer, pieces, count),
+        out_shape=[jax.ShapeDtypeStruct(term.shape[-2:], jnp.float32) for term in terms],
+        in_specs=[pl.BlockSpec(memory_space=pl.ANY)] * count,
+        out_specs=[pl.BlockSpec(memory_space=pltpu.VMEM)] * count,
+        scratch_shapes=[shape(p, outer, 2, 2) for p in n]
+        + [shape(p, outer, 2, 2) for p in n]
+        + [shape(p, outer, 2) for p in n]
+        + [shape(p, outer) for p in n]
+        + [shape(p, max(outer - 1, 1)) for p in n]
+        + [
+            pltpu.SemaphoreType.DMA((len(pieces),)),
+            pltpu.SemaphoreType.DMA((len(pieces), outer + 2)),
+            pltpu.SemaphoreType.DMA((len(pieces), outer + 2)),
+        ],
+        compiler_params=pltpu.CompilerParams(
+            collective_id=1, has_side_effects=True, vmem_limit_bytes=VMEM_LIMIT
+        ),
+    )(*terms)
+
+
+def cut(shape_list):
+    pieces = []
+    for i, (rows, columns) in enumerate(shape_list):
+        parts, blocks = 1, columns // 128
+        if rows % 8 == 0:
+            fits = [k for k in range(1, blocks + 1) if blocks % k == 0 and rows * columns // k <= 25000]
+            parts = min(fits) if fits else 1
+        width = columns // parts
+        for k in range(parts):
+            pieces.append((i, k * width, width, len(pieces) % 2))
+    return pieces
+
+
+def pack_shape(shape):
+    rows, columns = shape
+    return shape if rows % 8 == 0 else (rows * columns // 128, 128)
+
+
+def pack_vectors(parts):
+    joined = jnp.concatenate([part.astype(jnp.float32) for part in parts], axis=-1)
+    size = -(-joined.shape[-1] // 1024) * 1024
+    pad = [(0, 0)] * (joined.ndim - 1) + [(0, size - joined.shape[-1])]
+    return jnp.pad(joined, pad).reshape(joined.shape[:-1] + (size // 128, 128))
+
+
+def gather_weights(outer, weights, vectors):
+    shards = [pack_vectors(vectors)] + [w.reshape(pack_shape(w.shape)) for w in weights]
+    full = gather_all(outer, shards, cut([shard.shape for shard in shards]))
+    devices = outer * 8
+    packed = full[0].reshape(devices, -1)
+    whole_vectors, at = [], 0
+    for vector in vectors:
+        size = vector.shape[0]
+        whole_vectors.append(packed[:, at : at + size].reshape(devices * size))
+        at += size
+    whole = [f.reshape(devices * w.shape[0], w.shape[1]) for f, w in zip(full[1:], weights)]
+    return whole, whole_vectors
+
+
+def scatter_grads(outer, weight_terms, vector_terms):
+    devices = outer * 8
+    cuts = [term.reshape(devices, -1) for term in vector_terms]
+    packed = pack_vectors(cuts)
+    terms = [packed.reshape((outer, 2, 2, 2) + packed.shape[1:])]
+    shapes = [(term.shape[0] // devices, term.shape[1]) for term in weight_terms]
+    for term, shape in zip(weight_terms, shapes):
+        terms.append(term.astype(jnp.bfloat16).reshape((outer, 2, 2, 2) + pack_shape(shape)))
+    shares = scatter_all(outer, terms, cut([term.shape[-2:] for term in terms]))
+    flat = shares[0].reshape(-1)
+    vectors, at = [], 0
+    for part in cuts:
+        vectors.append(flat[at : at + part.shape[1]])
+        at += part.shape[1]
+    return [share.reshape(shape) for share, shape in zip(shares[1:], shapes)], vectors
 
 
 def layer_norm(values, gain, shift):
@@ -127,21 +463,13 @@
     proj_bias,
     out_grad,
 ):
-    gathered = (
-        lax.all_gather(norm1_gain, ("batch", "seq"), axis=0, tiled=True),
-        lax.all_gather(norm1_bias, ("batch", "seq"), axis=0, tiled=True),
-        lax.all_gather(qkv_weight, ("batch", "seq"), axis=0, tiled=True),
-        lax.all_gather(query_bias, ("batch", "seq"), axis=0, tiled=True),
-        lax.all_gather(value_bias, ("batch", "seq"), axis=0, tiled=True),
-        lax.all_gather(attn_weight, ("batch", "seq"), axis=0, tiled=True),
-        lax.all_gather(attn_bias, ("batch", "seq"), axis=0, tiled=True),
-        lax.all_gather(norm2_gain, ("batch", "seq"), axis=0, tiled=True),
-        lax.all_gather(norm2_bias, ("batch", "seq"), axis=0, tiled=True),
-        lax.all_gather(fc_weight, ("batch", "seq"), axis=0, tiled=True),
-        lax.all_gather(fc_bias, ("batch", "seq"), axis=0, tiled=True),
-        lax.all_gather(proj_weight, ("batch", "seq"), axis=0, tiled=True),
-        lax.all_gather(proj_bias, ("batch", "seq"), axis=0, tiled=True),
-    )
+    outer = lax.axis_size("batch") // 4
+    weights, vectors = gather_weights(
+        outer,
+        [qkv_weight, attn_weight, fc_weight, proj_weight],
+        [norm1_gain, norm1_bias, query_bias, value_bias, attn_bias, norm2_gain, norm2_bias, proj_bias, fc_bias],
+    )
+    gathered = (vectors[0], vectors[1], weights[0], vectors[2], vectors[3], weights[1], vectors[4], vectors[5], vectors[6], weights[2], vectors[8], weights[3], vectors[7])
     gain_one = gathered[0].astype(jnp.float32)
     shift_one = gathered[1].astype(jnp.float32)
     qkv_full = gathered[2]
@@ -304,21 +632,14 @@
     normed_grad = contract_last(qkv_grad, qkv_full)
     flat_part, norm1_gain_grad, norm1_bias_grad = norm_back_one(normed_grad)
     tokens_grad = (middle_grad + flat_part).reshape(rows, local, width)
-    shares = (
-        lax.psum_scatter(norm1_gain_grad, ("batch", "seq"), scatter_dimension=0, tiled=True),
-        lax.psum_scatter(norm1_bias_grad, ("batch", "seq"), scatter_dimension=0, tiled=True),
-        lax.psum_scatter(qkv_weight_grad, ("batch", "seq"), scatter_dimension=0, tiled=True),
-        lax.psum_scatter(query_bias_grad, ("batch", "seq"), scatter_dimension=0, tiled=True),
-        lax.psum_scatter(value_bias_grad, ("batch", "seq"), scatter_dimension=0, tiled=True),
-        lax.psum_scatter(attn_weight_grad, ("batch", "seq"), scatter_dimension=0, tiled=True),
-        lax.psum_scatter(attn_bias_grad, ("batch", "seq"), scatter_dimension=0, tiled=True),
-        lax.psum_scatter(norm2_gain_grad, ("batch", "seq"), scatter_dimension=0, tiled=True),
-        lax.psum_scatter(norm2_bias_grad, ("batch", "seq"), scatter_dimension=0, tiled=True),
-        lax.psum_scatter(fc_weight_grad, ("batch", "seq"), scatter_dimension=0, tiled=True),
-        lax.psum_scatter(fc_bias_grad, ("batch", "seq"), scatter_dimension=0, tiled=True),
-        lax.psum_scatter(proj_weight_grad, ("batch", "seq"), scatter_dimension=0, tiled=True),
-        lax.psum_scatter(proj_bias_grad, ("batch", "seq"), scatter_dimension=0, tiled=True),
-    )
+    weight_shares, vector_shares = scatter_grads(
+        outer,
+        [qkv_weight_grad, attn_weight_grad, fc_weight_grad, proj_weight_grad],
+        [norm1_gain_grad, norm1_bias_grad, query_bias_grad, value_bias_grad, attn_bias_grad, norm2_gain_grad, norm2_bias_grad, proj_bias_grad, fc_bias_grad],
+    )
+    qkv_share, attn_share, fc_share, proj_share = weight_shares
+    g1, b1, qb, vb, ab, g2, b2, pb, fb = vector_shares
+    shares = (g1, b1, qkv_share, qb, vb, attn_share, ab, g2, b2, fc_share, fb, proj_share, pb)
     return (block_out, tokens_grad) + tuple(shares)
 
 

time: 1240 us -> 755 us (0.61)
  waiting for transfers between devices: 789 us -> 217 us
  Pallas kernels: 0 us -> 165 us
  blocking collectives: 83.3 us -> 0 us
  matrix products: 190 us -> 175 us
    reduce_scatter x4 -> x0, waiting for transfers between devices: 428 us -> none  [the longest x1 142 us: shards(): lax.psum_scatter(fc_weight_grad, ('batch', 'seq'), scatter_dimension=0, t...]
    pallas_call x0 -> x2, Pallas kernels: none -> 165 us  [the longest x1 86.6 us: gather_all(): pl.pallas_call(functools.partial(gather_kernel, outer, pieces, count), ou...]
    all_gather x4 -> x0, waiting for transfers between devices: 158 us -> none  [the longest x1 59.2 us: shards(): lax.all_gather(fc_weight, ('batch', 'seq'), axis=0, tiled=True)]
    unnamed x2 -> x0, blocking collectives: 83.3 us -> none
    reduce_scatter x1, waiting for transfers between devices: 104 us -> 116 us  [shards(): lax.psum_scatter(value_full.astype(jnp.bfloat16), 'seq', scatter_dimensio...]
  transfers between devices with their start and end apart: 12 -> 4, of which waited for: 12 -> 4; matrix products, arithmetic and copies ran while one was open for 13% -> 11% of each run, Pallas kernels for 0% -> 0%
where the time goes in v1:
time: 755 us; the launch traced here: 749 us
  waiting for transfers between devices  217 us (29%)
  matrix products  175 us (23%)
  Pallas kernels  165 us (22%)
  local copies, waits for them, and re-layouts  106 us (14%)
  other arithmetic  69.6 us (9%)
  between operations  14.9 us (2%)
    reduce_scatter x1, waiting for transfers between devices, shards(): lax.psum_scatter(value_full.astype(jnp.bfloat16), 'seq', scatter_dimensio...  116 us
    pallas_call x1, Pallas kernels, gather_all(): pl.pallas_call(functools.partial(gather_kernel, outer, pieces, count), ou...  86.6 us
    pallas_call x1, Pallas kernels, scatter_all(): pl.pallas_call(functools.partial(scatter_kernel, outer, pieces, count), o...  78.8 us
    reduce_scatter x1, waiting for transfers between devices, shards(): lax.psum_scatter(key_full.astype(jnp.bfloat16), 'seq', scatter_dimension=...  45.6 us
    all_gather x1, waiting for transfers between devices, shards(): lax.all_gather(keys, 'seq', axis=1, tiled=True)  33 us
    dot_general x4, matrix products, contract_last(): lax.dot_general(left, right, (((1,), (1,)), ((), ())), preferred_element_...  32.2 us
    dot_general x4, matrix products, contract_rows(): lax.dot_general(left, right, (((0,), (0,)), ((), ())), preferred_element_...  31.3 us
    dynamic_slice x11, local copies, waits for them, and re-layouts, take_block(): return lax.dynamic_slice_in_dim(values, block * length, length, 1)  23 us
  transfers between devices with their start and end apart: 4, of which 4 were waited for; matrix products, arithmetic and copies ran while one was open for 11% of the time, Pallas kernels for 0%

profile of v1, /device:TPU:0, one launch (start us, length us, event | category | flops | bytes accessed | tf_op | source)
XLA Modules:
  0.0 748.8 jit_solution(17848883293741886442)
XLA Ops:
  7.2 6.2 concatenate.21
  18.9 86.6 %shard_map.271 = (f32[4,2,2,2,8,128]{5,4,3,2,1,0:T(8,128)}, bf16[4,2,2,2,24,2304]{5,4,3,2,1,0:T(8,128)(2,1)}, bf16[4,2,2,2,24,768]{5,4,3,2,1,0:T(8,128)(2,1)}, b...) custom-call(f32[8,128]{1,0:T(8,128)} %bitcast_convert_fusion.refs_0_, bf16[24,2304]{1,0:T(8,128)(2,1)} %refs_1_.1, ...), custom_call_target="tpu_custom_call" | custom-call | tf_op jit(solution)/shard_map/pallas_call | solution.py:125
  108.2 6.1 add_convert_fusion
  130.3 33.0 %all-gather.5.cloned.1.call-done = bf16[2,1024,768]{1,2,0:T(8,128)(2,1)} async-done(((bf16[2,512,768]{1,2,0:T(8,128)(2,1)}), bf16[2,1024,768]{1,2,0:T(8,128)(2,1)}) %all-gather.5.cloned.1.call-update) | async-done | bytes 3145744 | tf_op jit(solution)/shard_map/all_gather | solution.py:498
  163.3 25.5 %while.39 = (s32[]{:T(128)}, f32[2,12,512]{2,1,0:T(8,128)S(1)}, f32[2,12,512]{2,1,0:T(8,128)S(1)}, s32[]{:T(128)}, s32[]{:T(128)}, /*index=5*/s32[2,1024]{1,0:T(...) while((s32[]{:T(128)}, f32[2,12,512]{2,1,0:T(8,128)S(1)}, ...), condition=%wide.wide.region_6.7_spmd, body=%wide.wide.region_3.6_spmd.sunk | while | flops 856974336 | bytes 59384000 | solution.py:518
  165.6 11.7 %fusion.137 = (f32[2,12,512]{2,1,0:T(8,128)S(1)}, f32[2,12,512,512]{3,2,1,0:T(8,128)}) fusion(pred[2,512,512]{1,2,0:T(8,128)(4,1)S(1)} %compare_and_fusion.9, bf16[2,512,12,64]{1,3,2,0:T(8,128)(2,1)S(1)} %bitcast.241, bf16[2,512,12,64]{1,0,3,2:T(2,128)(2,1)S(1)} %get-tuple-element.880), kind=kOutput, calls=%fused_computation.2.clone.clone.1 | convolution fusion | flops 824168448 | bytes 28884992 | tf_op jit(solution)/shard_map/while/body/rqhd,rkhd->rhqk/dot_general | solution.py:398
  177.3 11.5 %select_reduce_fusion.3 = f32[2,12,512]{2,1,0:T(8,128)S(1)} fusion(f32[2,12,512,512]{3,2,1,0:T(8,128)} %get-tuple-element.809, f32[2,12,512]{2,1,0:T(8,128)S(1)} %max.5, pred[2,512,512]{1,2,0:T(8,128)(4,1)S(1)} %compare_and_fusion.9), kind=kLoop, calls=%fused_computation.1.clone.clone.1 | loop fusion | flops 31444992 | bytes 25788416 | tf_op jit(solution)/shard_map/while/body/reduce_sum | solution.py:514
  188.8 21.6 %all-gather.3.cloned.1.call-done = bf16[2,1024,768]{1,2,0:T(8,128)(2,1)} async-done(((bf16[2,512,768]{1,2,0:T(8,128)(2,1)}), bf16[2,1024,768]{1,2,0:T(8,128)(2,1)}) %all-gather.3.cloned.1.call-update) | async-done | bytes 3145744 | tf_op jit(solution)/shard_map/all_gather | solution.py:499
  212.5 16.6 %while.40 = (s32[]{:T(128)}, f32[2,512,12,64]{1,3,2,0:T(8,128)}, s32[]{:T(128)}, bf16[2,1024,768]{1,2,0:T(8,128)(2,1)}, s32[]{:T(128)}, /*index=5*/s32[2,1024]{1...) while((s32[]{:T(128)}, f32[2,512,12,64]{1,3,2,0:T(8,128)}, ...), condition=%wide.wide.region_8.9_spmd, body=%wide.wide.region_7.8_spmd.sunk | while | flops 1637876736 | bytes 18948300 | solution.py:542
  217.3 11.6 %bitcast_add_fusion.13 = f32[2,512,12,64]{1,3,2,0:T(8,128)} fusion(f32[2,512,12,64]{1,3,2,0:T(8,128)} %get-tuple-element.901, bf16[2,512,12,64]{1,3,2,0:T(8,128)(2,1)} %bitcast.244, f32[2,12,512]{2,1,0:T(8,128)S(1)} %get-tuple-element.924, pred[2,512,512]{1,2,0:T(8,128)(4,1)} %compare_and_fusion.10, bf16[2,512,12,64]{1,3,2,0:T(8,128)(2,1)} %bitcast.243, ...), kind=kOutput, calls=%fused_computation.17.clone.clone.1 | convolution fusion | flops 1636564992 | bytes 11583488 | tf_op jit(solution)/shard_map/while/body/rhqk,rkhd->rqhd/dot_general | solution.py:535
  244.3 11.3 %fusion.65 = f32[1024,3072]{1,0:T(8,128)} fusion(bf16[768,3072]{1,0:T(8,128)(2,1)} %bitcast.284, f32[1024,768]{1,0:T(8,128)} %copy-done.21, f32[768]{0:T(1024)S(1)} %copy-done.54, f32[768]{0:T(1024)S(1)} %copy-done.44, f32[1024]{0:T(1024)S(1)} %fusion.58, f32[1024]{0:T(1024)S(1)} %broadcast_multiply_fusion), kind=kOutput, calls=%fused_computation.142 | convolution fusion | flops 4835770368 | bytes 20461568 | tf_op jit(solution)/shard_map/dot_general | solution.py:554
  255.6 18.4 %convert_reduce_fusion = (f32[3072]{0:T(1024)}, bf16[1024,3072]{1,0:T(8,128)(2,1)S(1)}) fusion(bf16[3072,768]{1,0:T(8,128)(2,1)} %bitcast.282, bf16[1024,768]{1,0:T(8,128)(2,1)S(1)} %bitcast.245, f32[1024,3072]{1,0:T(8,128)} %fusion.65, f32[3072]{0:T(1024)S(1)} %copy-done.51), kind=kOutput, calls=%fused_computation.72 | convolution fusion | flops 4916769792 | bytes 25190400 | tf_op jit(solution)/shard_map/dot_general | solution.py:380
  274.0 6.2 multiply_reduce_fusion
  309.5 100.9 %while.41 = (s32[]{:T(128)}, f32[2,512,768]{1,2,0:T(8,128)}, f32[2,1024,768]{2,1,0:T(8,128)}, f32[2,1024,768]{2,1,0:T(8,128)}, s32[]{:T(128)}, /*index=5*/bf16[2...) while((s32[]{:T(128)}, f32[2,512,768]{1,2,0:T(8,128)}, ...), condition=%wide.wide.region_15.16_spmd, body=%wide.wide.region_14.15_spmd.sunk | while | flops 4094690304 | bytes 292200928 | solution.py:609
  314.0 4.4 constant_dynamic-slice_fusion.36
  329.3 10.2 %fusion.152 = f32[2,12,512,512]{3,2,1,0:T(8,128)} fusion(bf16[2,512,12,64]{1,3,2,0:T(8,128)(2,1)S(1)} %bitcast.239, bf16[2,512,12,64]{1,0,3,2:T(2,128)(2,1)S(1)} %get-tuple-element.984), kind=kOutput, calls=%fused_computation.43.clone.clone.1 | convolution fusion | flops 805306368 | bytes 28311552 | tf_op jit(solution)/shard_map/while/body/rqhd,rkhd->rhqk/dot_general | solution.py:398
  339.4 12.4 %fusion.154 = f32[2,12,512,64]{2,3,1,0:T(8,128)} fusion(f32[2,12,512,512]{3,2,1,0:T(8,128)} %fusion.152, f32[2,12,512]{2,1,0:T(8,128)S(1)} %get-tuple-element.980, pred[2,512,512]{1,2,0:T(8,128)(4,1)S(1)} %copy-done.18, bf16[2,512,12,64]{1,0,3,2:T(2,128)(2,1)S(1)} %copy-done.32), kind=kOutput, calls=%fused_computation.32.clone.clone.1 | convolution fusion | flops 830472192 | bytes 30457856 | tf_op jit(solution)/shard_map/while/body/rhqk,rqhd->rkhd/dot_general | solution.py:429
  351.9 16.1 %fusion.153 = bf16[2,12,512,512]{2,3,1,0:T(8,128)(2,1)} fusion(f32[2,12,512,512]{3,2,1,0:T(8,128)} %fusion.152, f32[2,12,512]{2,1,0:T(8,128)S(1)} %get-tuple-element.983, f32[2,12,512]{2,1,0:T(8,128)S(1)} %get-tuple-element.980, pred[2,512,512]{1,2,0:T(8,128)(4,1)} %compare_and_fusion.11, bf16[2,512,12,64]{1,3,2,0:T(8,128)(2,1)} %bitcast.242, ...), kind=kOutput, calls=%fused_computation.29.clone.clone.1 | convolution fusion | flops 843055104 | bytes 41517056 | tf_op jit(solution)/shard_map/while/body/rqhd,rkhd->rhqk/dot_general | solution.py:432
  368.0 4.3 bitcast_add_fusion.15
  375.8 7.1 convolution_multiply_fusion.6
  382.9 10.6 %convolution_multiply_fusion.7 = f32[2,12,512,64]{2,3,1,0:T(8,128)} fusion(bf16[2,12,512,512]{2,3,1,0:T(8,128)(2,1)} %fusion.153, bf16[2,512,12,64]{1,0,3,2:T(2,128)(2,1)} %get-tuple-element.1044), kind=kOutput, calls=%fused_computation.39.clone.clone.1 | convolution fusion | flops 806092800 | bytes 17301504 | tf_op jit(solution)/shard_map/while/body/rhqk,rqhd->rkhd/dot_general | solution.py:442
  393.5 5.3 bitcast_add_fusion.16
  410.5 4.7 convert_element_type.130
  419.4 4.9 convert_element_type.129
  430.0 10.0 %convolution_convert_fusion.1 = bf16[768,3072]{1,0:T(8,128)(2,1)} fusion(bf16[1024,3072]{1,0:T(8,128)(2,1)} %copy-done.61, f32[1024,768]{1,0:T(8,128)S(1)} %copy-done.23, f32[768]{0:T(1024)S(1)} %copy-done.55, f32[768]{0:T(1024)S(1)} %copy-done.45, f32[1024]{0:T(1024)S(1)} %copy-done.48, f32[1024]{0:T(1024)S(1)} %copy-done.43), kind=kOutput, calls=%fused_computation.76 | convolution fusion | flops 4838129664 | bytes 14170112 | tf_op jit(solution)/shard_map/dot_general | solution.py:374
  440.1 13.1 %add_convert_fusion.1 = bf16[1024,768]{1,0:T(8,128)(2,1)} fusion(f32[1024,768]{1,0:T(8,128)S(1)} %copy-done.24, bf16[3072,768]{1,0:T(8,128)(2,1)} %bitcast.283, f32[768]{0:T(1024)S(1)} %add.251, f32[1024,3072]{1,0:T(8,128)} %fusion.65, f32[3072]{0:T(1024)S(1)} %copy-done.52), kind=kOutput, calls=%fused_computation.110 | convolution fusion | flops 4865654784 | bytes 22035456 | tf_op jit(solution)/shard_map/dot_general | solution.py:561
  453.3 9.4 %convolution_convert_fusion = bf16[3072,768]{1,0:T(8,128)(2,1)} fusion(bf16[1024,768]{1,0:T(8,128)(2,1)S(1)} %bitcast.246, f32[1024,3072]{1,0:T(8,128)S(1)} %bitcast.292, f32[3072]{0:T(1024)S(1)} %copy-done.52), kind=kOutput, calls=%fused_computation.75 | convolution fusion | flops 4865654784 | bytes 18886656 | tf_op jit(solution)/shard_map/dot_general | solution.py:374
  462.7 116.4 %reduce-scatter.5.cloned.1.call-done = bf16[2,512,768]{2,1,0:T(8,128)(2,1)} async-done(((bf16[2,1024,768]{2,1,0:T(8,128)(2,1)}), bf16[2,512,768]{2,1,0:T(8,128)(2,1)}) %reduce-scatter.5.cloned.1.call-update) | async-done | bytes 1572880 | tf_op jit(solution)/shard_map/reduce_scatter | solution.py:619
  579.1 45.6 %reduce-scatter.3.cloned.1.call-done = bf16[2,512,768]{2,1,0:T(8,128)(2,1)} async-done(((bf16[2,1024,768]{2,1,0:T(8,128)(2,1)}), bf16[2,512,768]{2,1,0:T(8,128)(2,1)}) %reduce-scatter.3.cloned.1.call-update) | async-done | bytes 1572880 | tf_op jit(solution)/shard_map/reduce_scatter | solution.py:616
  624.7 6.6 fusion.62
  641.8 8.0 %convolution_convert_fusion.2 = bf16[768,2304]{1,0:T(8,128)(2,1)} fusion(bf16[1024,768]{1,0:T(8,128)(2,1)} %get-tuple-element.419, bf16[1024,768]{1,0:T(8,128)(2,1)} %bitcast.261, bf16[1024,768]{1,0:T(8,128)(2,1)} %bitcast.264, bf16[1024,768]{1,0:T(8,128)(2,1)S(1)} %bitcast.252), kind=kOutput, calls=%fused_computation.77 | convolution fusion | flops 3639803904 | bytes 9830400 | tf_op jit(solution)/shard_map/dot_general | solution.py:374
  653.9 78.8 %shard_map.272 = (f32[8,128]{1,0:T(8,128)}, f32[24,2304]{1,0:T(8,128)}, f32[24,768]{1,0:T(8,128)}, f32[24,3072]{1,0:T(8,128)}, f32[96,768]{1,0:T(8,128)}) custom-call(f32[4,2,2,2,8,128]{5,4,3,2,1,0:T(8,128)} %bitcast.273, bf16[4,2,2,2,24,2304]{5,4,3,2,1,0:T(8,128)(2,1)} %bitcast.258, bf16[4,2,2,2,24,768]{5,4,3,2,1,0:T(8,128)(2,1)} %bitcast.268, ...), custom_call_target="tpu_custom_call" | custom-call | tf_op jit(solution)/shard_map/pallas_call | solution.py:276
  (258 shorter events, 141.2 us)
Async XLA Ops:
  7.2 100.4 %copy-start.9 = (bf16[2,512,768]{2,1,0:T(8,128)(2,1)S(1)}, bf16[2,512,768]{2,1,0:T(8,128)(2,1)}, u32[]{:S(2)}) copy-start(bf16[2,512,768]{2,1,0:T(8,128)(2,1)} %param.22) | copy-start | bytes 4718596
  7.2 156.1 %all-gather.5.cloned.1.call-start = ((), (), s32[]{:S(2)}) async-start(), calls=%async_computation.3 | async-start | bytes 4718592 | tf_op jit(solution)/shard_map/all_gather | solution.py:498
  107.4 7.0 copy-start.38
  118.4 92.0 %all-gather.3.cloned.1.call-start = ((), (), s32[]{:S(2)}) async-start(), calls=%async_computation.2 | async-start | bytes 4718592 | tf_op jit(solution)/shard_map/all_gather | solution.py:499
  120.0 459.1 %reduce-scatter.5.cloned.1.call-start = ((), (), s32[]{:S(2)}) async-start(), calls=%async_computation.5 | async-start | bytes 4718592 | tf_op jit(solution)/shard_map/reduce_scatter | solution.py:619
  188.8 23.7 %copy-start.6 = (bf16[2,1024,768]{1,2,0:T(8,128)(2,1)S(1)}, bf16[2,1024,768]{1,2,0:T(8,128)(2,1)}, u32[]{:S(2)}) copy-start(bf16[2,1024,768]{1,2,0:T(8,128)(2,1)} %get-tuple-element.1046) | copy-start | bytes 9437188
  235.1 6.8 copy-start.19
  239.7 40.5 %copy-start.42 = (f32[1024]{0:T(1024)}, f32[1024]{0:T(1024)S(1)}, u32[]{:S(2)}) copy-start(f32[1024]{0:T(1024)S(1)} %broadcast_multiply_fusion) | copy-start | bytes 12292
  241.9 38.3 %copy-start.47 = (f32[1024]{0:T(1024)}, f32[1024]{0:T(1024)S(1)}, u32[]{:S(2)}) copy-start(f32[1024]{0:T(1024)S(1)} %fusion.58) | copy-start | bytes 12292
  244.3 11.3 %copy-start.16 = (bf16[2,512,768]{2,1,0:T(8,128)(2,1)S(1)}, bf16[2,512,768]{2,1,0:T(8,128)(2,1)}, u32[]{:S(2)}) copy-start(bf16[2,512,768]{2,1,0:T(8,128)(2,1)} %param.37) | copy-start | bytes 4718596
  244.3 11.3 %copy-start.51 = (f32[3072]{0:T(1024)S(1)}, f32[3072]{0:T(1024)}, u32[]{:S(2)}) copy-start(f32[3072]{0:T(1024)} %add.245) | copy-start | bytes 36868
  244.3 29.7 %slice-start = ((s8[4718592]{0:T(1024)(128)(4,1)}), s8[4194304]{0:T(1024)(128)(4,1)S(1)}, s32[]{:S(2)}) async-start(s8[4718592]{0:T(1024)(128)(4,1)} %bitcast.285), calls=%async_computation.6 | async-start | bytes 8388608
  255.5 18.4 %copy-start.22 = (f32[1024,768]{1,0:T(8,128)S(1)}, f32[1024,768]{1,0:T(8,128)}, u32[]{:S(2)}) copy-start(f32[1024,768]{1,0:T(8,128)} %copy-done.21) | copy-start | bytes 9437188
  255.6 18.4 %slice-start.1 = ((s8[4718592]{0:T(1024)(128)(4,1)}), s8[524288]{0:T(1024)(128)(4,1)S(1)}, s32[]{:S(2)}) async-start(s8[4718592]{0:T(1024)(128)(4,1)} %bitcast.285), calls=%async_computation.7 | async-start | bytes 1048576
  274.0 6.2 copy-start.61
  314.0 15.3 %copy-start = (bf16[2,512,768]{1,2,0:T(8,128)(2,1)}, bf16[2,512,768]{1,2,0:T(8,128)(2,1)S(1)}, u32[]{:S(2)}) copy-start(bf16[2,512,768]{1,2,0:T(8,128)(2,1)S(1)} %constant_dynamic-slice_fusion.33) | copy-start | bytes 4718596 | tf_op jit(solution)/shard_map/while
  329.3 10.2 %copy-start.18 = (pred[2,512,512]{1,2,0:T(8,128)(4,1)S(1)}, pred[2,512,512]{1,2,0:T(8,128)(4,1)}, u32[]{:S(2)}) copy-start(pred[2,512,512]{1,2,0:T(8,128)(4,1)} %compare_and_fusion.11) | copy-start | bytes 1572868 | tf_op jit(solution)/shard_map/while
  329.3 10.2 %copy-start.32 = (bf16[2,512,12,64]{1,0,3,2:T(2,128)(2,1)S(1)}, bf16[2,512,12,64]{1,0,3,2:T(2,128)(2,1)}, u32[]{:S(2)}) copy-start(bf16[2,512,12,64]{1,0,3,2:T(2,128)(2,1)} %get-tuple-element.985) | copy-start | bytes 4718596 | tf_op jit(solution)/shard_map/while
  351.9 16.1 %copy-start.2 = (f32[2,512,768]{1,2,0:T(8,128)S(1)}, f32[2,512,768]{1,2,0:T(8,128)}, u32[]{:S(2)}) copy-start(f32[2,512,768]{1,2,0:T(8,128)} %copy.190) | copy-start | bytes 9437188 | tf_op jit(solution)/shard_map/while
  415.2 209.5 %reduce-scatter.3.cloned.1.call-start = ((), (), s32[]{:S(2)}) async-start(), calls=%async_computation.4 | async-start | bytes 4718592 | tf_op jit(solution)/shard_map/reduce_scatter | solution.py:616
  430.0 10.1 %copy-start.24 = (f32[1024,768]{1,0:T(8,128)S(1)}, f32[1024,768]{1,0:T(8,128)}, u32[]{:S(2)}) copy-start(f32[1024,768]{1,0:T(8,128)} %copy-done.21) | copy-start | bytes 9437188
  430.0 10.1 %copy-start.52 = (f32[3072]{0:T(1024)S(1)}, f32[3072]{0:T(1024)}, u32[]{:S(2)}) copy-start(f32[3072]{0:T(1024)} %add.245) | copy-start | bytes 36868
  430.0 23.2 %slice-start.2 = ((s8[12582912]{0:T(1024)(128)(4,1)}), s8[4194304]{0:T(1024)(128)(4,1)S(1)}, s32[]{:S(2)}) async-start(s8[12582912]{0:T(1024)(128)(4,1)} %bitcast.291), calls=%async_computation.8 | async-start | bytes 8388608
  440.1 13.2 %copy-start.17 = (bf16[2,512,768]{2,1,0:T(8,128)(2,1)S(1)}, bf16[2,512,768]{2,1,0:T(8,128)(2,1)}, u32[]{:S(2)}) copy-start(bf16[2,512,768]{2,1,0:T(8,128)(2,1)} %param.37) | copy-start | bytes 4718596
  440.1 13.2 %slice-start.3 = ((s8[12582912]{0:T(1024)(128)(4,1)}), s8[4194304]{0:T(1024)(128)(4,1)S(1)}, s32[]{:S(2)}) async-start(s8[12582912]{0:T(1024)(128)(4,1)} %bitcast.291), calls=%async_computation.9 | async-start | bytes 8388608
  440.1 13.2 %slice-start.4 = ((s8[12582912]{0:T(1024)(128)(4,1)}), s8[4194304]{0:T(1024)(128)(4,1)S(1)}, s32[]{:S(2)}) async-start(s8[12582912]{0:T(1024)(128)(4,1)} %bitcast.291), calls=%async_computation.10 | async-start | bytes 8388608
  453.3 171.4 %copy-start.27 = (bf16[2,512,768]{2,1,0:T(8,128)(2,1)S(1)}, bf16[2,512,768]{2,1,0:T(8,128)(2,1)}, u32[]{:S(2)}) copy-start(bf16[2,512,768]{2,1,0:T(8,128)(2,1)} %copy.109) | copy-start | bytes 4718596
  624.7 6.6 copy-start.11
  624.7 6.6 copy-start.30
  624.7 6.6 copy-start.31
  624.7 6.6 copy-start.36
  624.7 7.5 %copy-start.60 = (bf16[4,2,2,2,24,2304]{5,4,3,2,1,0:T(8,128)(2,1)S(1)}, bf16[4,2,2,2,24,2304]{5,4,3,2,1,0:T(8,128)(2,1)}, u32[]{:S(2)}) copy-start(bf16[4,2,2,2,24,2304]{5,4,3,2,1,0:T(8,128)(2,1)} %get-tuple-element.203) | copy-start | bytes 10616836
  (39 other events, 120.4 us)
Sparse Core Ops, SparseCore 0:
  118.5 44.7 all-gather.4
  165.4 44.9 all-gather.2
  415.4 163.7 reduce-scatter.4
  581.3 43.3 reduce-scatter.2

commit v2 on v1

v2 whole, which is shorter than its diff:
```python
import functools
import math

import jax
import jax.numpy as jnp
from jax import lax
from jax.experimental import pallas as pl
from jax.experimental.pallas import tpu as pltpu
from jax.sharding import PartitionSpec as P

HD = 64
EPSILON = 1e-05
GELU_SCALE = 0.7978845608028654
MESH_ID = pl.DeviceIdType.MESH
VMEM_LIMIT = 60 * 2**20


def place():
    batch, seq = lax.axis_index("batch"), lax.axis_index("seq")
    return (batch // 4, (batch // 2) % 2, batch % 2, seq)


def device(a, y, c, s):
    return (a * 4 + y * 2 + c, s)


def greet(outer):
    a, y, c, s = place()
    barrier = pltpu.get_barrier_semaphore()
    others = [device(lax.rem(a + k, outer), y, c, s) for k in range(1, outer)]
    others += [device(a, 1 - y, c, s), device(a, y, c, 1 - s), device(a, y, 1 - c, s)]
    for other in others:
        pl.semaphore_signal(barrier, inc=1, device_id=other, device_id_type=MESH_ID)
    pl.semaphore_wait(barrier, len(others))


def gather_kernel(outer, pieces, count, *refs):
    shards, outs = refs[:count], refs[count : 2 * count]
    own_sem, send_sem, recv_sem = refs[2 * count :]
    a, y, c, s = place()
    greet(outer)
    owns = []
    for i in range(count):
        own = pltpu.make_async_copy(shards[i], outs[i].at[a, y, c, s], own_sem.at[i])
        own.start()
        owns.append(own)

    def z_copies(p):
        i, start, width, order = pieces[p]
        columns = pl.ds(start, width)
        return [
            pltpu.make_async_remote_copy(
                src_ref=shards[i].at[:, columns],
                dst_ref=outs[i].at[a, y, c, s, :, columns],
                send_sem=send_sem.at[p, k - 1],
                recv_sem=recv_sem.at[p, k - 1],
                device_id=device(lax.rem(a + k, outer), y, c, s),
                device_id_type=MESH_ID,
            )
            for k in range(1, outer)
        ]

    def later_copy(p, phase):
        i, start, width, order = pieces[p]
        columns = pl.ds(start, width)
        every = slice(None)
        if phase == 2:
            index = (every, every, c, every)
            other = device(a, y, 1 - c, s)
        elif (phase == 0) == (order == 0):
            index = (every, y, c, s if phase == 0 else every)
            other = device(a, 1 - y, c, s)
        else:
            index = (every, y if phase == 0 else every, c, s)
            other = device(a, y, c, 1 - s)
        block = outs[i].at[index + (every, columns)]
        return pltpu.make_async_remote_copy(
            src_ref=block,
            dst_ref=block,
            send_sem=send_sem.at[p, outer - 1 + phase],
            recv_sem=recv_sem.at[p, outer - 1 + phase],
            device_id=other,
            device_id_type=MESH_ID,
        )

    z_all = [z_copies(p) for p in range(len(pieces))]
    later = [[later_copy(p, phase) for phase in range(3)] for p in range(len(pieces))]
    lag = (1, 2, 4, 6)
    for t in range(len(pieces) + lag[3]):
        if t == 0:
            for p in range(min(2, len(pieces))):
                for copy in z_all[p]:
                    copy.start()
            for own in owns:
                own.wait()
        elif t + 1 < len(pieces):
            for copy in z_all[t + 1]:
                copy.start()
        p = t - lag[0]
        if 0 <= p < len(pieces):
            for copy in z_all[p]:
                copy.wait_recv()
            later[p][0].start()
        for phase in range(2):
            p = t - lag[phase + 1]
            if 0 <= p < len(pieces):
                later[p][phase].wait_recv()
                later[p][phase + 1].start()
        p = t - lag[3]
        if 0 <= p < len(pieces):
            later[p][2].wait_recv()
    for p in range(len(pieces)):
        for copy in z_all[p] + later[p]:
            copy.wait_send()


def gather_all(outer, shards, pieces):
    count = len(shards)
    return pl.pallas_call(
        functools.partial(gather_kernel, outer, pieces, count),
        out_shape=[
            jax.ShapeDtypeStruct((outer, 2, 2, 2) + shard.shape, shard.dtype) for shard in shards
        ],
        in_specs=[pl.BlockSpec(memory_space=pl.ANY)] * count,
        out_specs=[pl.BlockSpec(memory_space=pl.ANY)] * count,
        scratch_shapes=[
            pltpu.SemaphoreType.DMA((count,)),
            pltpu.SemaphoreType.DMA((len(pieces), outer + 2)),
            pltpu.SemaphoreType.DMA((len(pieces), outer + 2)),
        ],
        compiler_params=pltpu.CompilerParams(collective_id=0, has_side_effects=True),
    )(*shards)


def scatter_kernel(outer, pieces, count, *refs):
    terms, outs = refs[:count], refs[count : 2 * count]
    rest = refs[2 * count :]
    n = len(pieces)
    held, first, second, third, fourth = (rest[k * n : (k + 1) * n] for k in range(5))
    own_sem, send_sem, recv_sem = rest[5 * n :]
    a, y, c, s = place()
    greet(outer)
    every = slice(None)

    def remote(p, k, src, dst, other):
        return pltpu.make_async_remote_copy(
            src_ref=src,
            dst_ref=dst,
            send_sem=send_sem.at[p, k],
            recv_sem=recv_sem.at[p, k],
            device_id=other,
            device_id_type=MESH_ID,
        )

    started = []

    def core_start(p):
        i, start, width, order = pieces[p]
        columns = pl.ds(start, width)
        own = pltpu.make_async_copy(
            terms[i].at[:, :, c, :, :, columns], held[p], own_sem.at[p]
        )
        own.start()
        copy = remote(
            p, 0, terms[i].at[:, :, 1 - c, :, :, columns], first[p], device(a, y, 1 - c, s)
        )
        copy.start()
        started.append(copy)
        return (own, copy)

    def add(target, other):
        lead = target.shape[:-2]
        total = math.prod(lead)

        def body(k, carry):
            index = []
            for size in reversed(lead):
                index.append(lax.rem(k, size))
                k = k // size
            index = tuple(reversed(index))
            value = target[index].astype(jnp.float32) + other[index].astype(jnp.float32)
            target[index] = value.astype(target.dtype)
            return carry

        lax.fori_loop(0, total, body, 0)

    def first_half(p):
        order = pieces[p][3]
        if order == 0:
            src, other = held[p].at[:, :, 1 - s], device(a, y, c, 1 - s)
        else:
            src, other = held[p].at[:, 1 - y], device(a, 1 - y, c, s)
        copy = remote(p, 1, src, second[p], other)
        copy.start()
        started.append(copy)
        return copy

    def second_half(p):
        order = pieces[p][3]
        if order == 0:
            src, other = held[p].at[:, 1 - y, s], device(a, 1 - y, c, s)
        else:
            src, other = held[p].at[:, y, 1 - s], device(a, y, c, 1 - s)
        copy = remote(p, 2, src, third[p], other)
        copy.start()
        started.append(copy)
        return copy

    def z_start(p):
        copies = []
        for k in range(1, outer):
            to = lax.rem(a + k, outer)
            copy = remote(
                p, 2 + k, held[p].at[to, y, s], fourth[p].at[k - 1], device(to, y, c, s)
            )
            copy.start()
            started.append(copy)
            copies.append(copy)
        return copies

    def finish(p):
        i, start, width, order = pieces[p]
        value = held[p][a, y, s].astype(jnp.float32)
        for k in range(1, outer):
            value = value + fourth[p][k - 1].astype(jnp.float32)
        outs[i][:, pl.ds(start, width)] = value

    core, one, two, z_all = {}, {}, {}, {}
    for t in range(n + 6):
        if t == 0:
            for p in range(min(2, n)):
                core[p] = core_start(p)
        elif t + 1 < n:
            core[t + 1] = core_start(t + 1)
        p = t - 1
        if 0 <= p < n:
            for copy in core[p][:1]:
                copy.wait()
            core[p][1].wait_recv()
            add(held[p], first[p])
            one[p] = first_half(p)
        p = t - 3
        if 0 <= p < n:
            one[p].wait_recv()
            if pieces[p][3] == 0:
                add(held[p].at[:, :, s], second[p])
            else:
                add(held[p].at[:, y], second[p])
            two[p] = second_half(p)
        p = t - 4
        if 0 <= p < n:
            two[p].wait_recv()
            add(held[p].at[:, y, s], third[p])
            z_all[p] = z_start(p)
        p = t - 5
        if 0 <= p < n:
            for copy in z_all[p]:
                copy.wait_recv()
            finish(p)
    for copy in started:
        copy.wait_send()


def scatter_all(outer, terms, pieces):
    count = len(terms)
    shape = lambda p, *lead: pltpu.VMEM(
        lead + (terms[pieces[p][0]].shape[-2], pieces[p][2]), terms[pieces[p][0]].dtype
    )
    n = range(len(pieces))
    return pl.pallas_call(
        functools.partial(scatter_kernel, outer, pieces, count),
        out_shape=[jax.ShapeDtypeStruct(term.shape[-2:], jnp.float32) for term in terms],
        in_specs=[pl.BlockSpec(memory_space=pl.ANY)] * count,
        out_specs=[pl.BlockSpec(memory_space=pltpu.VMEM)] * count,
        scratch_shapes=[shape(p, outer, 2, 2) for p in n]
        + [shape(p, outer, 2, 2) for p in n]
        + [shape(p, outer, 2) for p in n]
        + [shape(p, outer) for p in n]
        + [shape(p, max(outer - 1, 1)) for p in n]
        + [
            pltpu.SemaphoreType.DMA((len(pieces),)),
            pltpu.SemaphoreType.DMA((len(pieces), outer + 2)),
            pltpu.SemaphoreType.DMA((len(pieces), outer + 2)),
        ],
        compiler_params=pltpu.CompilerParams(
            collective_id=1, has_side_effects=True, vmem_limit_bytes=VMEM_LIMIT
        ),
    )(*terms)


def cut(shape_list):
    pieces = []
    for i, (rows, columns) in enumerate(shape_list):
        parts, blocks = 1, columns // 128
        if rows % 8 == 0:
            fits = [k for k in range(1, blocks + 1) if blocks % k == 0 and rows * columns // k <= 25000]
            parts = min(fits) if fits else 1
        width = columns // parts
        for k in range(parts):
            pieces.append((i, k * width, width, len(pieces) % 2))
    return pieces


def pack_shape(shape):
    rows, columns = shape
    return shape if rows % 8 == 0 else (rows * columns // 128, 128)


def pack_vectors(parts):
    joined = jnp.concatenate([part.astype(jnp.float32) for part in parts], axis=-1)
    size = -(-joined.shape[-1] // 1024) * 1024
    pad = [(0, 0)] * (joined.ndim - 1) + [(0, size - joined.shape[-1])]
    return jnp.pad(joined, pad).reshape(joined.shape[:-1] + (size // 128, 128))


TILE = 256
PAIR = 128
FIRM = 1e30


def dot_nn(left, right):
    return lax.dot_general(left, right, (((1,), (0,)), ((), ())), preferred_element_type=jnp.float32)


def dot_nt(left, right):
    return lax.dot_general(left, right, (((1,), (1,)), ((), ())), preferred_element_type=jnp.float32)


def dot_tn(left, right):
    return lax.dot_general(left, right, (((0,), (0,)), ((), ())), preferred_element_type=jnp.float32)


def normalize(values):
    average = jnp.mean(values, axis=-1, keepdims=True)
    centered = values - average
    variance = jnp.mean(centered * centered, axis=-1, keepdims=True)
    scale = lax.rsqrt(variance + EPSILON)
    return centered * scale, scale


def norm_grad(upstream, gain, normal, scale):
    inner = upstream * gain
    first = jnp.mean(inner, axis=-1, keepdims=True)
    second = jnp.mean(inner * normal, axis=-1, keepdims=True)
    return scale * (inner - first - normal * second)


def column_sum(values):
    return jnp.sum(values, axis=0, keepdims=True)


def project_kernel(x_ref, prev_ref, weight_ref, vectors_ref, normed_ref, q_ref, k_ref, v_ref):
    tile = pl.program_id(1)
    width = x_ref.shape[-1]
    x = jnp.where(tile == 0, prev_ref[0], x_ref[0]).astype(jnp.float32)
    normal, _ = normalize(x)
    normed = (normal * vectors_ref[0:1] + vectors_ref[1:2]).astype(jnp.bfloat16)
    normed_ref[0] = normed

    @pl.when(tile > 0)
    def _():
        queries = dot_nn(normed, weight_ref[:, :width]) + vectors_ref[2:3]
        q_ref[0] = queries.astype(jnp.bfloat16) * jnp.bfloat16(1.0 / math.sqrt(HD))

    k_ref[0] = dot_nn(normed, weight_ref[:, width : 2 * width]).astype(jnp.bfloat16)
    values = dot_nn(normed, weight_ref[:, 2 * width :]) + vectors_ref[3:4]
    v_ref[0] = values.astype(jnp.bfloat16)


def project(tokens, prev, weight, vectors):
    rows, local, width = tokens.shape
    tiles = local // TILE
    here = lambda r, t: (r, jnp.maximum(t - 1, 0), 0)
    extended = jax.ShapeDtypeStruct((rows, local + TILE, width), jnp.bfloat16)
    return pl.pallas_call(
        project_kernel,
        grid=(rows, tiles + 1),
        in_specs=[
            pl.BlockSpec((1, TILE, width), here),
            pl.BlockSpec((1, TILE, width), lambda r, t: (r, 0, 0)),
            pl.BlockSpec(weight.shape, lambda r, t: (0, 0)),
            pl.BlockSpec(vectors.shape, lambda r, t: (0, 0)),
        ],
        out_specs=[
            pl.BlockSpec((1, TILE, width), lambda r, t: (r, t, 0)),
            pl.BlockSpec((1, TILE, width), here),
            pl.BlockSpec((1, TILE, width), lambda r, t: (r, t, 0)),
            pl.BlockSpec((1, TILE, width), lambda r, t: (r, t, 0)),
        ],
        out_shape=[extended, jax.ShapeDtypeStruct(tokens.shape, jnp.bfloat16), extended, extended],
        compiler_params=pltpu.CompilerParams(vmem_limit_bytes=VMEM_LIMIT),
    )(tokens, prev, weight, vectors)


def lane_index(rows):
    return lax.broadcasted_iota(jnp.int32, (rows, PAIR), 1)


def mask_columns(starts_ref, row, q_cols, k_cols):
    place = lax.broadcasted_iota(jnp.int32, (TILE, PAIR), 0)
    lane = lane_index(TILE)
    for tile in range(2):
        before, start = starts_ref[row, tile], starts_ref[row, tile + 1]
        late = jnp.where(place >= start, 1.0, 0.0)
        q_cols[tile] = jnp.where(lane == 0, late, jnp.where(lane == 1, 1.0, 0.0)).astype(jnp.bfloat16)
        early = jnp.where(place < before, -FIRM, 0.0)
        k_cols[tile, 0] = jnp.where(
            lane == 0, -FIRM, jnp.where(lane == 1, early, 0.0)
        ).astype(jnp.bfloat16)
        early = jnp.where(place < start, -FIRM, 0.0)
        k_cols[tile, 1] = jnp.where(lane == 0, early, 0.0).astype(jnp.bfloat16)


def attend_kernel(starts_ref, q_ref, k_ref, v_ref, probs_ref, out_ref, inverse_ref, q_cols, k_cols):
    row = pl.program_id(0)

    @pl.when(pl.program_id(1) == 0)
    def _():
        mask_columns(starts_ref, row, q_cols, k_cols)

    lane = lane_index(TILE)
    causal = lax.broadcasted_iota(jnp.int32, (TILE, TILE), 1) <= lax.broadcasted_iota(
        jnp.int32, (TILE, TILE), 0
    )
    ones = jnp.ones((TILE, PAIR), jnp.bfloat16)
    for tile in range(2):
        queries = q_ref[0, pl.ds(tile * TILE, TILE)]
        keys = [
            jnp.concatenate([k_ref[0, pl.ds((tile + w) * TILE, TILE)], k_cols[tile, w]], axis=1)
            for w in range(2)
        ]
        values = [
            jnp.concatenate([v_ref[0, pl.ds((tile + w) * TILE, TILE)], ones], axis=1)
            for w in range(2)
        ]
        mixed, inverse = [], []
        for head in range(2):
            mine = (lane < HD) if head == 0 else (lane >= HD)
            left = jnp.concatenate([jnp.where(mine, queries, jnp.bfloat16(0)), q_cols[tile]], axis=1)
            far = dot_nt(left, keys[0])
            near = jnp.where(causal, dot_nt(left, keys[1]), -FIRM)
            top = jnp.max(jnp.maximum(far, near), axis=-1, keepdims=True)
            far = jnp.exp(far - top).astype(jnp.bfloat16)
            near = jnp.exp(near - top).astype(jnp.bfloat16)
            probs_ref[0, 0, tile, head, 0] = far
            probs_ref[0, 0, tile, head, 1] = near
            total = dot_nn(far, values[0]) + dot_nn(near, values[1])
            share = 1.0 / total[:, PAIR:]
            mixed.append(total[:, :PAIR] * share)
            inverse.append(share)
        out_ref[0, pl.ds(tile * TILE, TILE)] = jnp.where(lane < HD, mixed[0], mixed[1]).astype(
            jnp.bfloat16
        )
        inverse_ref[0, pl.ds(tile * TILE, TILE)] = jnp.where(lane < HD, inverse[0], inverse[1])


def attend(starts, q, k, v):
    rows, local, width = q.shape
    pairs = width // PAIR
    by_pair = lambda r, j: (r, 0, j)
    return pl.pallas_call(
        attend_kernel,
        grid=(rows, pairs),
        in_specs=[
            pl.BlockSpec(memory_space=pltpu.SMEM),
            pl.BlockSpec((1, local, PAIR), by_pair),
            pl.BlockSpec((1, local + TILE, PAIR), by_pair),
            pl.BlockSpec((1, local + TILE, PAIR), by_pair),
        ],
        out_specs=[
            pl.BlockSpec((1, 1, 2, 2, 2, TILE, TILE), lambda r, j: (r, j, 0, 0, 0, 0, 0)),
            pl.BlockSpec((1, local, PAIR), by_pair),
            pl.BlockSpec((1, local, PAIR), by_pair),
        ],
        out_shape=[
            jax.ShapeDtypeStruct((rows, pairs, 2, 2, 2, TILE, TILE), jnp.bfloat16),
            jax.ShapeDtypeStruct((rows, local, width), jnp.bfloat16),
            jax.ShapeDtypeStruct((rows, local, width), jnp.float32),
        ],
        scratch_shapes=[
            pltpu.VMEM((2, TILE, PAIR), jnp.bfloat16),
            pltpu.VMEM((2, 2, TILE, PAIR), jnp.bfloat16),
        ],
        compiler_params=pltpu.CompilerParams(vmem_limit_bytes=VMEM_LIMIT),
    )(starts, q, k, v)


def attend_grad_kernel(
    probs_ref, q_ref, k_ref, v_ref, grad_ref, out_ref, inverse_ref, dq_ref, dk_ref, dv_ref, dk_sum, dv_sum
):
    lane = lane_index(TILE)
    ones = jnp.ones((TILE, PAIR), jnp.bfloat16)
    for tile in range(2):
        span = pl.ds(tile * TILE, TILE)
        queries = q_ref[0, span]
        scaled = (grad_ref[0, span].astype(jnp.float32) * inverse_ref[0, span]).astype(jnp.bfloat16)
        product = scaled.astype(jnp.float32) * out_ref[0, span].astype(jnp.float32)
        d_queries = []
        for head in range(2):
            mine = (lane < HD) if head == 0 else (lane >= HD)
            delta = -jnp.sum(jnp.where(mine, product, 0.0), axis=-1, keepdims=True)
            high = delta.astype(jnp.bfloat16).astype(jnp.float32)
            extra = jnp.where(lane == 0, high, jnp.where(lane == 1, delta - high, 0.0))
            grads = jnp.where(mine, scaled, jnp.bfloat16(0))
            mine_queries = jnp.where(mine, queries, jnp.bfloat16(0))
            left = jnp.concatenate([grads, extra.astype(jnp.bfloat16)], axis=1)
            d_query = None
            for w in range(2):
                at = pl.ds((tile + w) * TILE, TILE)
                right = jnp.concatenate([v_ref[0, at], ones], axis=1)
                probs = probs_ref[0, 0, tile, head, w]
                d_score = (probs.astype(jnp.float32) * dot_nt(left, right)).astype(jnp.bfloat16)
                part = dot_nn(d_score, k_ref[0, at])
                d_query = part if w == 0 else d_query + part
                d_key = dot_tn(d_score, mine_queries)
                d_value = dot_tn(probs, grads)
                if head == 0 and (w == 1 or tile == 0):
                    dk_sum[at] = d_key
                    dv_sum[at] = d_value
                else:
                    dk_sum[at] += d_key
                    dv_sum[at] += d_value
            d_queries.append(d_query)
        dq = jnp.where(lane < HD, d_queries[0], d_queries[1]) * (1.0 / math.sqrt(HD))
        dq_ref[0, span] = dq.astype(jnp.bfloat16)
    dk_ref[0] = dk_sum[...].astype(jnp.bfloat16)
    dv_ref[0] = dv_sum[...].astype(jnp.bfloat16)


def attend_grad(probs, q, k, v, grad, out, inverse):
    rows, local, width = q.shape
    pairs = width // PAIR
    by_pair = lambda r, j: (r, 0, j)
    small = pl.BlockSpec((1, local, PAIR), by_pair)
    large = pl.BlockSpec((1, local + TILE, PAIR), by_pair)
    return pl.pallas_call(
        attend_grad_kernel,
        grid=(rows, pairs),
        in_specs=[
            pl.BlockSpec((1, 1, 2, 2, 2, TILE, TILE), lambda r, j: (r, j, 0, 0, 0, 0, 0)),
            small,
            large,
            large,
            small,
            small,
            small,
        ],
        out_specs=[small, large, large],
        out_shape=[
            jax.ShapeDtypeStruct(q.shape, jnp.bfloat16),
            jax.ShapeDtypeStruct(k.shape, jnp.bfloat16),
            jax.ShapeDtypeStruct(k.shape, jnp.bfloat16),
        ],
        scratch_shapes=[
            pltpu.VMEM((local + TILE, PAIR), jnp.float32),
            pltpu.VMEM((local + TILE, PAIR), jnp.float32),
        ],
        compiler_params=pltpu.CompilerParams(vmem_limit_bytes=VMEM_LIMIT),
    )(probs, q, k, v, grad, out, inverse)


def gelu_pair(v):
    square = v * v
    half = 0.5 + 0.5 * jnp.tanh(v * (GELU_SCALE + (GELU_SCALE * 0.044715) * square))
    hidden = v * half
    slope = half + hidden * (1.0 - half) * (2.0 * GELU_SCALE + (6.0 * GELU_SCALE * 0.044715) * square)
    return hidden, slope


MLP_TILE = 256
CHUNK = 768


def mlp_kernel(
    x_hbm, att_hbm, dy_hbm, attn_hbm, fc_hbm, proj_hbm, vectors,
    out_hbm, middle_grad_hbm, att_grad_hbm, attn_grad_hbm, fc_grad_hbm, proj_grad_hbm, sums_ref,
    x, att, dy, attn, fc, proj, hidden, pre_grad, normed, branch, out, middle_grad, att_grad,
    attn_grad, fc_grad, proj_grad, in_sem, out_sem,
):
    tokens, width = x.shape
    chunks = fc.shape[1] // CHUNK
    tiles = tokens // MLP_TILE
    loads = [
        pltpu.make_async_copy(src, dst, in_sem.at[i])
        for i, (src, dst) in enumerate(
            ((att_hbm, att), (attn_hbm, attn), (x_hbm, x), (fc_hbm, fc), (dy_hbm, dy), (proj_hbm, proj))
        )
    ]
    for load in loads:
        load.start()
    sums_ref[...] = jnp.zeros_like(sums_ref)
    for load in loads[:3]:
        load.wait()

    def tile_step(t, carry):
        span = pl.ds(pl.multiple_of(t * MLP_TILE, MLP_TILE), MLP_TILE)
        middle = x[span].astype(jnp.float32) + dot_nn(att[span], attn[...]) + vectors[4:5]
        normal, scale = normalize(middle)
        low = (normal * vectors[5:6] + vectors[6:7]).astype(jnp.bfloat16)
        normed[span] = low

        @pl.when(t == 0)
        def _():
            for load in loads[3:]:
                load.wait()

        upstream = dy[span]
        result = middle + vectors[7:8]
        back = None
        for j in range(chunks):
            columns = pl.ds(j * CHUNK, CHUNK)
            pre = dot_nn(low, fc[:, columns]) + vectors[8 + j : 9 + j]
            value, slope = gelu_pair(pre)
            value = value.astype(jnp.bfloat16)
            hidden[span, columns] = value
            grad = dot_nt(upstream, proj[columns]) * slope
            grad = grad.astype(jnp.bfloat16)
            pre_grad[span, columns] = grad
            sums_ref[4 + j : 5 + j] += column_sum(grad.astype(jnp.float32))
            result = result + dot_nn(value, proj[columns])
            part = dot_nt(grad, fc[:, columns])
            back = part if back is None else back + part
        out[span] = result.astype(jnp.bfloat16)
        upstream = upstream.astype(jnp.float32)
        sums_ref[0:1] += column_sum(upstream)
        sums_ref[1:2] += column_sum(back * normal)
        sums_ref[2:3] += column_sum(back)
        total = upstream + norm_grad(back, vectors[5:6], normal, scale)
        middle_grad[span] = total
        total = total.astype(jnp.bfloat16)
        branch[span] = total
        sums_ref[3:4] += column_sum(total.astype(jnp.float32))
        att_grad[span] = dot_nt(total, attn[...]).astype(jnp.bfloat16)
        return carry

    lax.fori_loop(0, tiles, tile_step, 0)
    stores = []

    def store(src, dst):
        copy = pltpu.make_async_copy(src, dst, out_sem.at[len(stores)])
        copy.start()
        stores.append(copy)

    store(out, out_hbm)
    store(middle_grad, middle_grad_hbm)
    store(att_grad, att_grad_hbm)
    for j in range(chunks):
        columns = pl.ds(j * CHUNK, CHUNK)
        proj_grad[columns] = dot_tn(hidden[:, columns], dy[...]).astype(jnp.bfloat16)
        store(proj_grad.at[columns], proj_grad_hbm.at[columns])
    for j in range(chunks):
        columns = pl.ds(j * CHUNK, CHUNK)
        fc_grad[:, columns] = dot_tn(normed[...], pre_grad[:, columns]).astype(jnp.bfloat16)
        store(fc_grad.at[:, columns], fc_grad_hbm.at[:, columns])
    attn_grad[...] = dot_tn(att[...], branch[...]).astype(jnp.bfloat16)
    store(attn_grad, attn_grad_hbm)
    for copy in stores:
        copy.wait()


def mlp(x, att, dy, attn, fc, proj, vectors):
    tokens, width = x.shape
    hidden = fc.shape[1]
    low, full = jnp.bfloat16, jnp.float32
    anywhere = pl.BlockSpec(memory_space=pl.ANY)
    vmem = pl.BlockSpec(memory_space=pltpu.VMEM)
    return pl.pallas_call(
        mlp_kernel,
        in_specs=[anywhere] * 6 + [vmem],
        out_specs=[anywhere] * 6 + [vmem],
        out_shape=[
            jax.ShapeDtypeStruct((tokens, width), low),
            jax.ShapeDtypeStruct((tokens, width), full),
            jax.ShapeDtypeStruct((tokens, width), low),
            jax.ShapeDtypeStruct(attn.shape, low),
            jax.ShapeDtypeStruct(fc.shape, low),
            jax.ShapeDtypeStruct(proj.shape, low),
            jax.ShapeDtypeStruct((8, width), full),
        ],
        scratch_shapes=[
            pltpu.VMEM((tokens, width), low),
            pltpu.VMEM((tokens, width), low),
            pltpu.VMEM((tokens, width), low),
            pltpu.VMEM(attn.shape, low),
            pltpu.VMEM(fc.shape, low),
            pltpu.VMEM(proj.shape, low),
            pltpu.VMEM((tokens, hidden), low),
            pltpu.VMEM((tokens, hidden), low),
            pltpu.VMEM((tokens, width), low),
            pltpu.VMEM((tokens, width), low),
            pltpu.VMEM((tokens, width), low),
            pltpu.VMEM((tokens, width), full),
            pltpu.VMEM((tokens, width), low),
            pltpu.VMEM(attn.shape, low),
            pltpu.VMEM(fc.shape, low),
            pltpu.VMEM(proj.shape, low),
            pltpu.SemaphoreType.DMA((6,)),
            pltpu.SemaphoreType.DMA((12,)),
        ],
        compiler_params=pltpu.CompilerParams(vmem_limit_bytes=VMEM_LIMIT),
    )(x, att, dy, attn, fc, proj, vectors)


def project_grad_kernel(normed, dq, dk, dv, weight, weight_grad, prev_grad, sums):
    rows, extended, width = normed.shape
    local = dq.shape[1]
    third = [pl.ds(i * width, width) for i in range(3)]
    for r in range(rows):
        head = pl.ds(0, TILE)
        prev_grad[r] = (
            dot_nt(dk[r, head], weight[:, third[1]]) + dot_nt(dv[r, head], weight[:, third[2]])
        ).astype(jnp.bfloat16)
    total = None
    for i, grads in enumerate((dq, dk, dv)):
        total = None
        for r in range(rows):
            left = normed[r, TILE:] if i == 0 else normed[r]
            part = dot_tn(left, grads[r])
            total = part if total is None else total + part
        weight_grad[:, third[i]] = total.astype(jnp.bfloat16)
    sums[...] = jnp.zeros_like(sums)
    for r in range(rows):
        sums[0:1] += column_sum(dq[r].astype(jnp.float32))
        sums[1:2] += column_sum(dv[r].astype(jnp.float32))


def project_grad(normed, dq, dk, dv, weight):
    rows, extended, width = normed.shape
    vmem = pl.BlockSpec(memory_space=pltpu.VMEM)
    return pl.pallas_call(
        project_grad_kernel,
        in_specs=[vmem] * 5,
        out_specs=[vmem] * 3,
        out_shape=[
            jax.ShapeDtypeStruct(weight.shape, jnp.bfloat16),
            jax.ShapeDtypeStruct((rows, TILE, width), jnp.bfloat16),
            jax.ShapeDtypeStruct((8, width), jnp.float32),
        ],
        compiler_params=pltpu.CompilerParams(vmem_limit_bytes=VMEM_LIMIT),
    )(normed, dq, dk, dv, weight)


def tokens_grad_kernel(x_ref, dq, dk, dv, weight, late, middle_grad, vectors, out_ref, sums):
    row, tile = pl.program_id(0), pl.program_id(1)
    width = x_ref.shape[-1]

    @pl.when((row == 0) & (tile == 0))
    def _():
        sums[...] = jnp.zeros_like(sums)

    back = dot_nt(dq[0], weight[:, :width])
    back = back + dot_nt(dk[0], weight[:, width : 2 * width])
    back = back + dot_nt(dv[0], weight[:, 2 * width :])
    back = back + jnp.where(tile == pl.num_programs(1) - 1, late[0].astype(jnp.float32), 0.0)
    normal, scale = normalize(x_ref[0].astype(jnp.float32))
    sums[0:1] += column_sum(back * normal)
    sums[1:2] += column_sum(back)
    out_ref[0] = middle_grad[0] + norm_grad(back, vectors[0:1], normal, scale)


def tokens_grad_of(x, dq, dk, dv, weight, late, middle_grad, vectors):
    rows, local, width = x.shape
    block = lambda shift: pl.BlockSpec((1, TILE, width), lambda r, t: (r, t + shift, 0))
    whole = lambda v: pl.BlockSpec(v.shape, lambda r, t: (0, 0))
    return pl.pallas_call(
        tokens_grad_kernel,
        grid=(rows, local // TILE),
        in_specs=[
            block(0),
            block(0),
            block(1),
            block(1),
            whole(weight),
            pl.BlockSpec((1, TILE, width), lambda r, t: (r, 0, 0)),
            block(0),
            whole(vectors),
        ],
        out_specs=[block(0), pl.BlockSpec((8, width), lambda r, t: (0, 0))],
        out_shape=[
            jax.ShapeDtypeStruct(x.shape, jnp.float32),
            jax.ShapeDtypeStruct((8, width), jnp.float32),
        ],
        compiler_params=pltpu.CompilerParams(vmem_limit_bytes=VMEM_LIMIT),
    )(x, dq, dk, dv, weight, late, middle_grad, vectors)


def gather_weights(outer, weights, vectors, fc_bias):
    devices = outer * 8
    shards = [pack_vectors(vectors + [fc_bias])]
    shards += [w.reshape(pack_shape(w.shape)) for w in weights]
    full = gather_all(outer, shards, cut([shard.shape for shard in shards]))
    packed = full[0].reshape(devices, -1)
    count, size = len(vectors), vectors[0].shape[0]
    first = packed[:, : count * size].reshape(devices, count, size)
    first = jnp.swapaxes(first, 0, 1).reshape(count, devices * size)
    second = packed[:, count * size : count * size + fc_bias.shape[0]].reshape(-1, devices * size)
    whole = [f.reshape(devices * w.shape[0], w.shape[1]) for f, w in zip(full[1:], weights)]
    return whole, jnp.concatenate([first, second], axis=0)


def scatter_grads(outer, weight_terms, vector_terms, fc_bias_term):
    devices = outer * 8
    count, width = vector_terms.shape
    first = jnp.swapaxes(vector_terms.reshape(count, devices, width // devices), 0, 1)
    first = first.reshape(devices, -1)
    second = fc_bias_term.reshape(devices, -1)
    packed = pack_vectors([first, second])
    terms = [packed.reshape((outer, 2, 2, 2) + packed.shape[1:])]
    shapes = [(term.shape[0] // devices, term.shape[1]) for term in weight_terms]
    for term, shape in zip(weight_terms, shapes):
        terms.append(term.reshape((outer, 2, 2, 2) + pack_shape(shape)))
    shares = scatter_all(outer, terms, cut([term.shape[-2:] for term in terms]))
    flat = shares[0].reshape(-1)
    size = width // devices
    vectors = [flat[i * size : (i + 1) * size] for i in range(count)]
    fc_bias = flat[count * size : count * size + second.shape[1]]
    return [share.reshape(shape) for share, shape in zip(shares[1:], shapes)], vectors, fc_bias


def shards(
    tokens_in,
    doc_starts,
    norm1_gain,
    norm1_bias,
    qkv_weight,
    query_bias,
    value_bias,
    attn_weight,
    attn_bias,
    norm2_gain,
    norm2_bias,
    fc_weight,
    fc_bias,
    proj_weight,
    proj_bias,
    out_grad,
):
    outer = lax.axis_size("batch") // 4
    rows, local, width = tokens_in.shape
    seq = lax.axis_index("seq")
    prev = lax.ppermute(tokens_in[:, local - TILE :], "seq", [(0, 1)])
    (qkv, attn, fc, proj), vectors = gather_weights(
        outer,
        [qkv_weight, attn_weight, fc_weight, proj_weight],
        [norm1_gain, norm1_bias, query_bias, value_bias, attn_bias, norm2_gain, norm2_bias, proj_bias],
        fc_bias,
    )
    first = 2 * seq
    padded = jnp.pad(doc_starts, ((0, 0), (1, 0)))
    starts = lax.dynamic_slice_in_dim(padded, first, 3, 1)
    starts = starts - TILE * (first - 1 + jnp.arange(3, dtype=jnp.int32))
    normed, q, k, v = project(tokens_in, prev, qkv, vectors)
    probs, att, inverse = attend(starts, q, k, v)
    flat = lambda value: value.reshape(rows * local, width)
    out, middle_grad, att_grad, attn_grad, fc_grad, proj_grad, mlp_sums = mlp(
        flat(tokens_in), flat(att), flat(out_grad), attn, fc, proj, vectors
    )
    block = lambda value: value.reshape(rows, local, width)
    dq, dk, dv = attend_grad(probs, q, k, v, block(att_grad), att, inverse)
    qkv_grad, prev_grad, project_sums = project_grad(normed, dq, dk, dv, qkv)
    late = lax.ppermute(prev_grad, "seq", [(1, 0)])
    tokens_grad, norm_sums = tokens_grad_of(
        tokens_in, dq, dk, dv, qkv, late, block(middle_grad), vectors
    )
    sums = jnp.concatenate([norm_sums[:2], project_sums[:2], mlp_sums[:4]], axis=0)
    weights, shares, fc_share = scatter_grads(
        outer, [qkv_grad, attn_grad, fc_grad, proj_grad], sums, mlp_sums[4:]
    )
    gain1, bias1, query, value, proj_b, gain2, bias2, attn_b = shares
    return (
        out.reshape(rows, local, width),
        tokens_grad,
        gain1,
        bias1,
        weights[0],
        query,
        value,
        weights[1],
        attn_b,
        gain2,
        bias2,
        weights[2],
        fc_share,
        weights[3],
        proj_b,
    )


def solution(mesh):
    return jax.shard_map(
        shards,
        mesh=mesh,
        in_specs=(
            P("batch", "seq", None),
            P("batch", None),
            P(("batch", "seq")),
            P(("batch", "seq")),
            P(("batch", "seq"), None),
            P(("batch", "seq")),
            P(("batch", "seq")),
            P(("batch", "seq"), None),
            P(("batch", "seq")),
            P(("batch", "seq")),
            P(("batch", "seq")),
            P(("batch", "seq"), None),
            P(("batch", "seq")),
            P(("batch", "seq"), None),
            P(("batch", "seq")),
            P("batch", "seq", None),
        ),
        out_specs=(
            P("batch", "seq", None),
            P("batch", "seq", None),
            P(("batch", "seq")),
            P(("batch", "seq")),
            P(("batch", "seq"), None),
            P(("batch", "seq")),
            P(("batch", "seq")),
            P(("batch", "seq"), None),
            P(("batch", "seq")),
            P(("batch", "seq")),
            P(("batch", "seq")),
            P(("batch", "seq"), None),
            P(("batch", "seq")),
            P(("batch", "seq"), None),
            P(("batch", "seq")),
        ),
        check_vma=False,
    )
```

time: 755 us -> 348 us (0.46)
  waiting for transfers between devices: 217 us -> 19.9 us
  matrix products: 175 us -> 0 us
  Pallas kernels: 165 us -> 296 us
  local copies, waits for them, and re-layouts: 106 us -> 22.3 us
  other arithmetic: 69.6 us -> 1.34 us
  between operations: 14.9 us -> 0.81 us
    dot_general x19 -> x0, matrix products: 175 us -> none  [the longest x4 32.2 us: contract_last(): lax.dot_general(left, right, (((1,), (1,)), ((), ())), preferred_element_...]
    reduce_scatter x2 -> x0, waiting for transfers between devices: 162 us -> none  [the longest x1 116 us: shards(): lax.psum_scatter(value_full.astype(jnp.bfloat16), 'seq', scatter_dimensio...]
    pallas_call x0 -> x6, Pallas kernels: none -> 134 us  [the longest x1 47.5 us: mlp(): pl.pallas_call(mlp_kernel, in_specs=[anywhere] * 6 + [vmem], out_specs=[a...]
    all_gather x2 -> x0, waiting for transfers between devices: 54.6 us -> none  [the longest x1 33 us: shards(): lax.all_gather(keys, 'seq', axis=1, tiled=True)]
    reduce_sum x11 -> x0, other arithmetic: 28 us -> none  [the longest x1 11.5 us: max_step(): jnp.sum(jnp.where(allowed, jnp.exp(masked - new_top[..., None]), 0.0), ax...]
    dynamic_slice x12 -> x0, local copies, waits for them, and re-layouts: 23 us -> none  [the longest x11 23 us: take_block(): return lax.dynamic_slice_in_dim(values, block * length, length, 1)]
    convert_element_type x6 -> x0, other arithmetic: 22.4 us -> none  [the longest x1 6.61 us: shards(): qkv_grad_float = qkv_grad.astype(jnp.float32)]
    ppermute x0 -> x2, waiting for transfers between devices: none -> 19.9 us  [the longest x1 19.9 us: shards(): late = lax.ppermute(prev_grad, 'seq', [(1, 0)])]
  transfers between devices with their start and end apart: 4 -> 2, of which waited for: 4 -> 1; matrix products, arithmetic and copies ran while one was open for 11% -> 3% of each run, Pallas kernels for 0% -> 24%
where the time goes in v2:
time: 348 us; the launch traced here: 346 us
  Pallas kernels  296 us (85%)
  local copies, waits for them, and re-layouts  22.3 us (6%)
  waiting for transfers between devices  19.9 us (6%)
  starting transfers between devices  6.17 us (2%)
    pallas_call x1, Pallas kernels, gather_all(): pl.pallas_call(functools.partial(gather_kernel, outer, pieces, count), ou...  84.7 us
    pallas_call x1, Pallas kernels, scatter_all(): pl.pallas_call(functools.partial(scatter_kernel, outer, pieces, count), o...  77.3 us
    pallas_call x1, Pallas kernels, mlp(): pl.pallas_call(mlp_kernel, in_specs=[anywhere] * 6 + [vmem], out_specs=[a...  47.5 us
    pallas_call x1, Pallas kernels, attend_grad(): pl.pallas_call(attend_grad_kernel, grid=(rows, pairs), in_specs=[pl.Block...  34.7 us
    ppermute x1, waiting for transfers between devices, shards(): late = lax.ppermute(prev_grad, 'seq', [(1, 0)])  19.9 us
    pallas_call x1, Pallas kernels, attend(): pl.pallas_call(attend_kernel, grid=(rows, pairs), in_specs=[pl.BlockSpec(...  16.7 us
    pallas_call x1, Pallas kernels, project_grad(): pl.pallas_call(project_grad_kernel, in_specs=[vmem] * 5, out_specs=[vmem]...  12.7 us
    pallas_call x1, Pallas kernels, project(): pl.pallas_call(project_kernel, grid=(rows, tiles + 1), in_specs=[pl.Block...  11.9 us
  transfers between devices with their start and end apart: 2, of which 1 were waited for; matrix products, arithmetic and copies ran while one was open for 3% of the time, Pallas kernels for 24%

profile of v2, /device:TPU:0, one launch (start us, length us, event | category | flops | bytes accessed | tf_op | source)
XLA Modules:
  0.0 346.4 jit_solution(16528663864076963866)
XLA Ops:
  0.7 1.2 slice.48
  1.8 4.9 %collective-permute-start = (bf16[2,256,768]{2,1,0:T(8,128)(2,1)S(1)}, bf16[2,256,768]{2,1,0:T(8,128)(2,1)S(1)}, u32[]{:S(2)}, u32[]{:S(2)}) collective-permute-start(bf16[2,256,768]{2,1,0:T(8,128)(2,1)S(1)} %slice.48), channel_id=1, source_target_pairs={{0,1},{2,3},{4,5},{6,7},{8,9},{10,11},{12,13},{14,15},{16,17},{18,... | collective-permute-start | bytes 2359304 | tf_op jit(solution)/shard_map/ppermute | solution.py:841
  6.8 6.1 %concatenate.13 = bf16[288]{0:T(512)(128)(2,1)S(1)} concatenate(bf16[24]{0:T(256)(128)(2,1)} %param.18, bf16[24]{0:T(256)(128)(2,1)} %param.19, bf16[24]{0:T(256)(128)(2,1)} %param.21, bf16[24]{0:T(256)(128)(2,1)} %param.22, bf16[24]{0:T(256)(128)(2,1)} %param.24, bf16[24]{0:T(256)(128)(2,1)} %param.25, bf16[24]{0:T(256)(128)(2,1)} %param.26, bf16[24]{0:T(256)(128)(2,1)} %param.30, ...), dimensions={0} | concatenate | bytes 1152 | tf_op jit(solution)/shard_map/concatenate | solution.py:310
  12.9 0.6 bitcast_convert_fusion.refs_0_
  13.5 84.7 %shard_map.271 = (f32[4,2,2,2,8,128]{5,4,3,2,1,0:T(8,128)}, bf16[4,2,2,2,24,2304]{5,4,3,2,1,0:T(8,128)(2,1)}, bf16[4,2,2,2,24,768]{5,4,3,2,1,0:T(8,128)(2,1)}, b...) custom-call(f32[8,128]{1,0:T(8,128)} %bitcast_convert_fusion.refs_0_, bf16[24,2304]{1,0:T(8,128)(2,1)} %refs_1_.1, ...), custom_call_target="tpu_custom_call" | custom-call | tf_op jit(solution)/shard_map/pallas_call | solution.py:119
  98.2 0.9 copy.38
  99.3 0.1 reshape.111
  99.4 0.1 reshape.112
  99.6 0.6 dynamic-slice_subtract_fusion.starts_ref
  100.3 0.9 copy-done.1
  101.1 11.9 %shard_map.272 = (bf16[2,768,768]{2,1,0:T(8,128)(2,1)}, bf16[2,512,768]{2,1,0:T(8,128)(2,1)}, bf16[2,768,768]{2,1,0:T(8,128)(2,1)}, bf16[2,768,768]{2,1,0:T(8,128)(2,1)}) custom-call(bf16[2,512,768]{2,1,0:T(8,128)(2,1)} %x_ref.3, bf16[2,256,768]{2,1,0:T(8,128)(2,1)} %copy-done.1, bf16[768,2304]{1,0:T(8,128)(2,1)} %bitcast.29, f32[12,768]{1,0:T(8,128)} %copy-done.2), custom_call_target="tpu_custom_call" | custom-call | tf_op jit(solution)/shard_map/pallas_call | solution.py:375
  113.1 16.7 %shard_map.273 = (bf16[2,6,2,2,2,256,256]{6,5,4,3,2,1,0:T(8,128)(2,1)}, bf16[2,512,768]{2,1,0:T(8,128)(2,1)}, f32[2,512,768]{2,1,0:T(8,128)}) custom-call(s32[2,3]{1,0:T(2,128)} %dynamic-slice_subtract_fusion.starts_ref, bf16[2,512,768]{2,1,0:T(8,128)(2,1)} %get-tuple-element.49.q_ref, bf16[2,768,768]{2,1,0:T(8,128)(2,1)} %get-tuple-element.50.k_ref, ...), custom_call_target="tpu_custom_call" | custom-call | tf_op jit(solution)/shard_map/pallas_call | solution.py:461
  129.7 47.5 %shard_map.274 = (bf16[1024,768]{1,0:T(8,128)(2,1)}, f32[1024,768]{1,0:T(8,128)}, bf16[1024,768]{1,0:T(8,128)(2,1)}, bf16[768,768]{1,0:T(8,128)(2,1)}, bf16[768,...) custom-call(bf16[1024,768]{1,0:T(8,128)(2,1)} %bitcast.32, bf16[1024,768]{1,0:T(8,128)(2,1)} %bitcast.33, ...), custom_call_target="tpu_custom_call" | custom-call | tf_op jit(solution)/shard_map/pallas_call | solution.py:667
  177.3 34.7 %shard_map.275 = (bf16[2,512,768]{2,1,0:T(8,128)(2,1)}, bf16[2,768,768]{2,1,0:T(8,128)(2,1)}, bf16[2,768,768]{2,1,0:T(8,128)(2,1)}) custom-call(bf16[2,6,2,2,2,256,256]{6,5,4,3,2,1,0:T(8,128)(2,1)} %get-tuple-element.57.probs_ref, bf16[2,512,768]{2,1,0:T(8,128)(2,1)} %get-tuple-element.49.q_ref, bf16[2,768,768]{2,1,0:T(8,128)(2,1)} %get-tuple-element.50.k_ref, ...), custom_call_target="tpu_custom_call" | custom-call | tf_op jit(solution)/shard_map/pallas_call | solution.py:536
  211.9 12.7 %shard_map.276 = (bf16[768,2304]{1,0:T(8,128)(2,1)}, bf16[2,256,768]{2,1,0:T(8,128)(2,1)}, f32[8,768]{1,0:T(8,128)}) custom-call(bf16[2,768,768]{2,1,0:T(8,128)(2,1)} %get-tuple-element.63.normed, bf16[2,512,768]{2,1,0:T(8,128)(2,1)} %get-tuple-element.60.dq, bf16[2,768,768]{2,1,0:T(8,128)(2,1)} %get-tuple-element.61.dk, ...), custom_call_target="tpu_custom_call" | custom-call | tf_op jit(solution)/shard_map/pallas_call | solution.py:730
  224.7 1.3 collective-permute-start.1
  226.1 0.7 slice.52
  226.8 19.9 %collective-permute-done.1.late = bf16[2,256,768]{2,1,0:T(8,128)(2,1)S(1)} collective-permute-done((bf16[2,256,768]{2,1,0:T(8,128)(2,1)}, bf16[2,256,768]{2,1,0:T(8,128)(2,1)S(1)}, u32[]{:S(2)}, u32[]{:S(2)}) %collective-permute-start.1) | collective-permute-done | bytes 786464 | tf_op jit(solution)/shard_map/ppermute | solution.py:861
  246.7 0.9 copy-done
  247.6 10.3 %shard_map.277 = (f32[2,512,768]{2,1,0:T(8,128)}, f32[8,768]{1,0:T(8,128)}) custom-call(bf16[2,512,768]{2,1,0:T(8,128)(2,1)} %x_ref.3, bf16[2,512,768]{2,1,0:T(8,128)(2,1)} %get-tuple-element.60.dq, bf16[2,768,768]{2,1,0:T(8,128)(2,1)} %get-tuple-element.61.dk, bf16[2,768,768]{2,1,0:T(8,128)(2,1)} %get-tuple-element.62.dv, bf16[768,2304]{1,0:T(8,128)(2,1)} %bitcast.31, ...), custom_call_target="tpu_custom_call" | custom-call | tf_op jit(solution)/shard_map/pallas_call | solution.py:765
  257.9 0.7 slice.51
  258.6 0.1 reshape.122
  258.8 0.1 copy.34
  258.8 0.1 reshape.123
  259.0 0.7 copy.36
  259.7 77.3 %shard_map.278 = (f32[8,128]{1,0:T(8,128)}, f32[24,2304]{1,0:T(8,128)}, f32[24,768]{1,0:T(8,128)}, f32[24,3072]{1,0:T(8,128)}, f32[96,768]{1,0:T(8,128)}) custom-call(f32[4,2,2,2,8,128]{5,4,3,2,1,0:T(8,128)} %bitcast.44, bf16[4,2,2,2,24,2304]{5,4,3,2,1,0:T(8,128)(2,1)} %bitcast.38, bf16[4,2,2,2,24,768]{5,4,3,2,1,0:T(8,128)(2,1)} %bitcast.42, ...), custom_call_target="tpu_custom_call" | custom-call | tf_op jit(solution)/shard_map/pallas_call | solution.py:270
  337.1 1.3 slice.62
  338.3 1.6 fusion.2
  339.9 1.6 copy.44
  341.5 1.5 copy.45
  343.0 1.7 copy.46
  344.7 1.7 copy.47
  (20 shorter events, 0.4 us)
Async XLA Ops:
  0.6 98.9 %copy-start.4 = (s32[2,4]{1,0:T(2,128)S(1)}, s32[2,4]{1,0:T(2,128)}, u32[]{:S(2)}) copy-start(s32[2,4]{1,0:T(2,128)} %param.17) | copy-start | bytes 100
  1.8 98.4 %collective-permute-start = (bf16[2,256,768]{2,1,0:T(8,128)(2,1)S(1)}, bf16[2,256,768]{2,1,0:T(8,128)(2,1)S(1)}, u32[]{:S(2)}, u32[]{:S(2)}) collective-permute-start(bf16[2,256,768]{2,1,0:T(8,128)(2,1)S(1)} %slice.48), channel_id=1, source_target_pairs={{0,1},{2,3},{4,5},{6,7},{8,9},{10,11},{12,13},{14,15},{16,17},{18,... | collective-permute-start | bytes 2359304 | tf_op jit(solution)/shard_map/ppermute | solution.py:841
  99.6 0.7 copy-start.2
  100.3 0.9 copy-start.1
  211.9 14.0 %copy-start.3 = (f32[8,768]{1,0:T(8,128)S(1)}, f32[8,768]{1,0:T(8,128)}, u32[]{:S(2)}) copy-start(f32[8,768]{1,0:T(8,128)} %get-tuple-element.69) | copy-start | bytes 73732
  224.7 22.0 %collective-permute-start.1 = (bf16[2,256,768]{2,1,0:T(8,128)(2,1)}, bf16[2,256,768]{2,1,0:T(8,128)(2,1)S(1)}, u32[]{:S(2)}, u32[]{:S(2)}) collective-permute-start(bf16[2,256,768]{2,1,0:T(8,128)(2,1)} %get-tuple-element.64), channel_id=1, source_target_pairs={{1,0},{3,2},{5,4},{7,6},{9,8},{11,10},{13,12},{15,14},{17,16},{19,... | collective-permute-start | bytes 2359304 | tf_op jit(solution)/shard_map/ppermute | solution.py:861
  246.7 0.9 copy-start

commit v3 on v2

--- a/solution.py
+++ b/solution.py
@@ -13,6 +13,7 @@
 GELU_SCALE = 0.7978845608028654
 MESH_ID = pl.DeviceIdType.MESH
 VMEM_LIMIT = 60 * 2**20
+EVERY = slice(None)
 
 
 def place():
@@ -34,84 +35,243 @@
     pl.semaphore_wait(barrier, len(others))
 
 
+def remote(src, dst, send_sem, recv_sem, other):
+    return pltpu.make_async_remote_copy(
+        src_ref=src,
+        dst_ref=dst,
+        send_sem=send_sem,
+        recv_sem=recv_sem,
+        device_id=other,
+        device_id_type=MESH_ID,
+    )
+
+
+class Gather:
+    lags, ahead = (1, 2, 4, 6), 2
+
+    def __init__(self, outer, pieces, shards, outs, own_sem, send_sem, recv_sem):
+        self.outer, self.pieces, self.shards, self.outs = outer, pieces, shards, outs
+        self.own_sem, self.send_sem, self.recv_sem = own_sem, send_sem, recv_sem
+        self.steps = len(pieces) + self.lags[3]
+        self.place = place()
+
+    def sems(self, p, k):
+        return self.send_sem.at[p, k], self.recv_sem.at[p, k]
+
+    def own(self, i):
+        return pltpu.make_async_copy(
+            self.shards[i], self.outs[i].at[self.place], self.own_sem.at[i]
+        )
+
+    def first(self, p, k):
+        i, start, width, order = self.pieces[p]
+        a, y, c, s = self.place
+        columns = pl.ds(start, width)
+        src = self.shards[i].at[:, columns]
+        dst = self.outs[i].at[a, y, c, s, :, columns]
+        if k == 0:
+            return remote(src, dst, *self.sems(p, 0), self.near(order))
+        return remote(src, dst, *self.sems(p, k), device(lax.rem(a + k, self.outer), y, c, s))
+
+    def near(self, order):
+        a, y, c, s = self.place
+        return device(a, 1 - y, c, s) if order == 0 else device(a, y, c, 1 - s)
+
+    def second(self, p, k):
+        i, start, width, order = self.pieces[p]
+        a, y, c, s = self.place
+        source = lax.rem(a + self.outer - k, self.outer)
+        block = self.outs[i].at[source, y, c, s, :, pl.ds(start, width)]
+        return remote(block, block, *self.sems(p, self.outer - 1 + k), self.near(order))
+
+    def third(self, p):
+        i, start, width, order = self.pieces[p]
+        a, y, c, s = self.place
+        index = (EVERY, EVERY, c, s) if order == 0 else (EVERY, y, c, EVERY)
+        block = self.outs[i].at[index + (EVERY, pl.ds(start, width))]
+        return remote(block, block, *self.sems(p, 2 * self.outer - 1), self.near(1 - order))
+
+    def fourth(self, p):
+        i, start, width, order = self.pieces[p]
+        a, y, c, s = self.place
+        block = self.outs[i].at[EVERY, EVERY, c, EVERY, EVERY, pl.ds(start, width)]
+        return remote(block, block, *self.sems(p, 2 * self.outer), device(a, y, 1 - c, s))
+
+    def step(self, t):
+        outer, count, lags = self.outer, len(self.pieces), self.lags
+        for p in range(self.ahead + 1) if t == 0 else (t + self.ahead,):
+            if p < count:
+                for k in range(outer):
+                    self.first(p, k).start()
+        if t == 0:
+            for i in range(len(self.shards)):
+                self.own(i).start()
+        p = t - lags[0]
+        if 0 <= p < count:
+            for k in range(1, outer):
+                self.first(p, k).wait_recv()
+                self.second(p, k).start()
+        p = t - lags[1]
+        if 0 <= p < count:
+            if p == 0:
+                for i in range(len(self.shards)):
+                    self.own(i).wait()
+            self.first(p, 0).wait_recv()
+            for k in range(1, outer):
+                self.second(p, k).wait_recv()
+            self.third(p).start()
+        p = t - lags[2]
+        if 0 <= p < count:
+            self.third(p).wait_recv()
+            self.fourth(p).start()
+        p = t - lags[3]
+        if 0 <= p < count:
+            self.fourth(p).wait_recv()
+
+    def end(self):
+        for p in range(len(self.pieces)):
+            for k in range(self.outer):
+                self.first(p, k).wait_send()
+            for k in range(1, self.outer):
+                self.second(p, k).wait_send()
+            self.third(p).wait_send()
+            self.fourth(p).wait_send()
+
+    @staticmethod
+    def semaphores(outer, arrays, pieces):
+        return [
+            pltpu.SemaphoreType.DMA((arrays,)),
+            pltpu.SemaphoreType.DMA((pieces, 2 * outer + 1)),
+            pltpu.SemaphoreType.DMA((pieces, 2 * outer + 1)),
+        ]
+
+
+def add_slots(target, other):
+    lead = target.shape[:-2]
+
+    def body(k, carry):
+        index = []
+        for size in reversed(lead):
+            index.append(lax.rem(k, size))
+            k = k // size
+        index = tuple(reversed(index))
+        value = target[index].astype(jnp.float32) + other[index].astype(jnp.float32)
+        target[index] = value.astype(target.dtype)
+        return carry
+
+    lax.fori_loop(0, math.prod(lead), body, 0)
+
+
+class Scatter:
+    lags = (1, 3, 4, 5)
+
+    def __init__(self, outer, pieces, terms, outs, slots, own_sem, send_sem, recv_sem):
+        self.outer, self.pieces, self.terms, self.outs = outer, pieces, terms, outs
+        n = len(pieces)
+        self.held, self.got = slots[:n], [slots[k * n : (k + 1) * n] for k in range(1, 5)]
+        self.own_sem, self.send_sem, self.recv_sem = own_sem, send_sem, recv_sem
+        self.steps = n + self.lags[3]
+        self.place = place()
+
+    def sems(self, p, k):
+        return self.send_sem.at[p, k], self.recv_sem.at[p, k]
+
+    def own(self, p):
+        i, start, width, order = self.pieces[p]
+        a, y, c, s = self.place
+        block = self.terms[i].at[EVERY, EVERY, c, EVERY, EVERY, pl.ds(start, width)]
+        return pltpu.make_async_copy(block, self.held[p], self.own_sem.at[p])
+
+    def first(self, p):
+        i, start, width, order = self.pieces[p]
+        a, y, c, s = self.place
+        block = self.terms[i].at[EVERY, EVERY, 1 - c, EVERY, EVERY, pl.ds(start, width)]
+        return remote(block, self.got[0][p], *self.sems(p, 0), device(a, y, 1 - c, s))
+
+    def second(self, p):
+        a, y, c, s = self.place
+        if self.pieces[p][3] == 0:
+            src, other = self.held[p].at[:, :, 1 - s], device(a, y, c, 1 - s)
+        else:
+            src, other = self.held[p].at[:, 1 - y], device(a, 1 - y, c, s)
+        return remote(src, self.got[1][p], *self.sems(p, 1), other)
+
+    def third(self, p):
+        a, y, c, s = self.place
+        if self.pieces[p][3] == 0:
+            src, other = self.held[p].at[:, 1 - y, s], device(a, 1 - y, c, s)
+        else:
+            src, other = self.held[p].at[:, y, 1 - s], device(a, y, c, 1 - s)
+        return remote(src, self.got[2][p], *self.sems(p, 2), other)
+
+    def fourth(self, p, k):
+        a, y, c, s = self.place
+        to = lax.rem(a + k, self.outer)
+        src = self.held[p].at[to, y, s]
+        return remote(src, self.got[3][p].at[k - 1], *self.sems(p, 2 + k), device(to, y, c, s))
+
+    def step(self, t):
+        outer, count, lags = self.outer, len(self.pieces), self.lags
+        a, y, c, s = self.place
+        if t < count:
+            self.own(t).start()
+            self.first(t).start()
+        p = t - lags[0]
+        if 0 <= p < count:
+            self.own(p).wait()
+            self.first(p).wait_recv()
+            add_slots(self.held[p], self.got[0][p])
+            self.second(p).start()
+        p = t - lags[1]
+        if 0 <= p < count:
+            self.second(p).wait_recv()
+            mine = (EVERY, EVERY, s) if self.pieces[p][3] == 0 else (EVERY, y)
+            add_slots(self.held[p].at[mine], self.got[1][p])
+            self.third(p).start()
+        p = t - lags[2]
+        if 0 <= p < count:
+            self.third(p).wait_recv()
+            add_slots(self.held[p].at[:, y, s], self.got[2][p])
+            for k in range(1, outer):
+                self.fourth(p, k).start()
+        p = t - lags[3]
+        if 0 <= p < count:
+            i, start, width, order = self.pieces[p]
+            value = self.held[p][a, y, s].astype(jnp.float32)
+            for k in range(1, outer):
+                self.fourth(p, k).wait_recv()
+                value = value + self.got[3][p][k - 1].astype(jnp.float32)
+            self.outs[i][:, pl.ds(start, width)] = value
+
+    def end(self):
+        for p in range(len(self.pieces)):
+            self.first(p).wait_send()
+            self.second(p).wait_send()
+            self.third(p).wait_send()
+            for k in range(1, self.outer):
+                self.fourth(p, k).wait_send()
+
+    @staticmethod
+    def scratch(outer, shapes, pieces):
+        def slot(p, *lead):
+            i, start, width, order = pieces[p]
+            return pltpu.VMEM(lead + (shapes[i][0], width), shapes[i][2])
+
+        n = range(len(pieces))
+        leads = ((outer, 2, 2), (outer, 2, 2), (outer, 2), (outer,), (max(outer - 1, 1),))
+        return [slot(p, *lead) for lead in leads for p in n] + [
+            pltpu.SemaphoreType.DMA((len(pieces),)),
+            pltpu.SemaphoreType.DMA((len(pieces), outer + 2)),
+            pltpu.SemaphoreType.DMA((len(pieces), outer + 2)),
+        ]
+
+
 def gather_kernel(outer, pieces, count, *refs):
-    shards, outs = refs[:count], refs[count : 2 * count]
-    own_sem, send_sem, recv_sem = refs[2 * count :]
-    a, y, c, s = place()
     greet(outer)
-    owns = []
-    for i in range(count):
-        own = pltpu.make_async_copy(shards[i], outs[i].at[a, y, c, s], own_sem.at[i])
-        own.start()
-        owns.append(own)
-
-    def z_copies(p):
-        i, start, width, order = pieces[p]
-        columns = pl.ds(start, width)
-        return [
-            pltpu.make_async_remote_copy(
-                src_ref=shards[i].at[:, columns],
-                dst_ref=outs[i].at[a, y, c, s, :, columns],
-                send_sem=send_sem.at[p, k - 1],
-                recv_sem=recv_sem.at[p, k - 1],
-                device_id=device(lax.rem(a + k, outer), y, c, s),
-                device_id_type=MESH_ID,
-            )
-            for k in range(1, outer)
-        ]
-
-    def later_copy(p, phase):
-        i, start, width, order = pieces[p]
-        columns = pl.ds(start, width)
-        every = slice(None)
-        if phase == 2:
-            index = (every, every, c, every)
-            other = device(a, y, 1 - c, s)
-        elif (phase == 0) == (order == 0):
-            index = (every, y, c, s if phase == 0 else every)
-            other = device(a, 1 - y, c, s)
-        else:
-            index = (every, y if phase == 0 else every, c, s)
-            other = device(a, y, c, 1 - s)
-        block = outs[i].at[index + (every, columns)]
-        return pltpu.make_async_remote_copy(
-            src_ref=block,
-            dst_ref=block,
-            send_sem=send_sem.at[p, outer - 1 + phase],
-            recv_sem=recv_sem.at[p, outer - 1 + phase],
-            device_id=other,
-            device_id_type=MESH_ID,
-        )
-
-    z_all = [z_copies(p) for p in range(len(pieces))]
-    later = [[later_copy(p, phase) for phase in range(3)] for p in range(len(pieces))]
-    lag = (1, 2, 4, 6)
-    for t in range(len(pieces) + lag[3]):
-        if t == 0:
-            for p in range(min(2, len(pieces))):
-                for copy in z_all[p]:
-                    copy.start()
-            for own in owns:
-                own.wait()
-        elif t + 1 < len(pieces):
-            for copy in z_all[t + 1]:
-                copy.start()
-        p = t - lag[0]
-        if 0 <= p < len(pieces):
-            for copy in z_all[p]:
-                copy.wait_recv()
-            later[p][0].start()
-        for phase in range(2):
-            p = t - lag[phase + 1]
-            if 0 <= p < len(pieces):
-                later[p][phase].wait_recv()
-                later[p][phase + 1].start()
-        p = t - lag[3]
-        if 0 <= p < len(pieces):
-            later[p][2].wait_recv()
-    for p in range(len(pieces)):
-        for copy in z_all[p] + later[p]:
-            copy.wait_send()
+    work = Gather(outer, pieces, refs[:count], refs[count : 2 * count], *refs[2 * count :])
+    for t in range(work.steps):
+        work.step(t)
+    work.end()
 
 
 def gather_all(outer, shards, pieces):
@@ -121,167 +281,33 @@
         out_shape=[
             jax.ShapeDtypeStruct((outer, 2, 2, 2) + shard.shape, shard.dtype) for shard in shards
         ],
-        in_specs=[pl.BlockSpec(memory_space=pl.ANY)] * count,
+        in_specs=[pl.BlockSpec(memory_space=pltpu.VMEM)] * count,
         out_specs=[pl.BlockSpec(memory_space=pl.ANY)] * count,
-        scratch_shapes=[
-            pltpu.SemaphoreType.DMA((count,)),
-            pltpu.SemaphoreType.DMA((len(pieces), outer + 2)),
-            pltpu.SemaphoreType.DMA((len(pieces), outer + 2)),
-        ],
-        compiler_params=pltpu.CompilerParams(collective_id=0, has_side_effects=True),
+        scratch_shapes=Gather.semaphores(outer, count, len(pieces)),
+        compiler_params=pltpu.CompilerParams(
+            collective_id=0, has_side_effects=True, vmem_limit_bytes=VMEM_LIMIT
+        ),
     )(*shards)
 
 
 def scatter_kernel(outer, pieces, count, *refs):
-    terms, outs = refs[:count], refs[count : 2 * count]
+    greet(outer)
     rest = refs[2 * count :]
-    n = len(pieces)
-    held, first, second, third, fourth = (rest[k * n : (k + 1) * n] for k in range(5))
-    own_sem, send_sem, recv_sem = rest[5 * n :]
-    a, y, c, s = place()
-    greet(outer)
-    every = slice(None)
-
-    def remote(p, k, src, dst, other):
-        return pltpu.make_async_remote_copy(
-            src_ref=src,
-            dst_ref=dst,
-            send_sem=send_sem.at[p, k],
-            recv_sem=recv_sem.at[p, k],
-            device_id=other,
-            device_id_type=MESH_ID,
-        )
-
-    started = []
-
-    def core_start(p):
-        i, start, width, order = pieces[p]
-        columns = pl.ds(start, width)
-        own = pltpu.make_async_copy(
-            terms[i].at[:, :, c, :, :, columns], held[p], own_sem.at[p]
-        )
-        own.start()
-        copy = remote(
-            p, 0, terms[i].at[:, :, 1 - c, :, :, columns], first[p], device(a, y, 1 - c, s)
-        )
-        copy.start()
-        started.append(copy)
-        return (own, copy)
-
-    def add(target, other):
-        lead = target.shape[:-2]
-        total = math.prod(lead)
-
-        def body(k, carry):
-            index = []
-            for size in reversed(lead):
-                index.append(lax.rem(k, size))
-                k = k // size
-            index = tuple(reversed(index))
-            value = target[index].astype(jnp.float32) + other[index].astype(jnp.float32)
-            target[index] = value.astype(target.dtype)
-            return carry
-
-        lax.fori_loop(0, total, body, 0)
-
-    def first_half(p):
-        order = pieces[p][3]
-        if order == 0:
-            src, other = held[p].at[:, :, 1 - s], device(a, y, c, 1 - s)
-        else:
-            src, other = held[p].at[:, 1 - y], device(a, 1 - y, c, s)
-        copy = remote(p, 1, src, second[p], other)
-        copy.start()
-        started.append(copy)
-        return copy
-
-    def second_half(p):
-        order = pieces[p][3]
-        if order == 0:
-            src, other = held[p].at[:, 1 - y, s], device(a, 1 - y, c, s)
-        else:
-            src, other = held[p].at[:, y, 1 - s], device(a, y, c, 1 - s)
-        copy = remote(p, 2, src, third[p], other)
-        copy.start()
-        started.append(copy)
-        return copy
-
-    def z_start(p):
-        copies = []
-        for k in range(1, outer):
-            to = lax.rem(a + k, outer)
-            copy = remote(
-                p, 2 + k, held[p].at[to, y, s], fourth[p].at[k - 1], device(to, y, c, s)
-            )
-            copy.start()
-            started.append(copy)
-            copies.append(copy)
-        return copies
-
-    def finish(p):
-        i, start, width, order = pieces[p]
-        value = held[p][a, y, s].astype(jnp.float32)
-        for k in range(1, outer):
-            value = value + fourth[p][k - 1].astype(jnp.float32)
-        outs[i][:, pl.ds(start, width)] = value
-
-    core, one, two, z_all = {}, {}, {}, {}
-    for t in range(n + 6):
-        if t == 0:
-            for p in range(min(2, n)):
-                core[p] = core_start(p)
-        elif t + 1 < n:
-            core[t + 1] = core_start(t + 1)
-        p = t - 1
-        if 0 <= p < n:
-            for copy in core[p][:1]:
-                copy.wait()
-            core[p][1].wait_recv()
-            add(held[p], first[p])
-            one[p] = first_half(p)
-        p = t - 3
-        if 0 <= p < n:
-            one[p].wait_recv()
-            if pieces[p][3] == 0:
-                add(held[p].at[:, :, s], second[p])
-            else:
-                add(held[p].at[:, y], second[p])
-            two[p] = second_half(p)
-        p = t - 4
-        if 0 <= p < n:
-            two[p].wait_recv()
-            add(held[p].at[:, y, s], third[p])
-            z_all[p] = z_start(p)
-        p = t - 5
-        if 0 <= p < n:
-            for copy in z_all[p]:
-                copy.wait_recv()
-            finish(p)
-    for copy in started:
-        copy.wait_send()
+    work = Scatter(outer, pieces, refs[:count], refs[count : 2 * count], rest[:-3], *rest[-3:])
+    for t in range(work.steps):
+        work.step(t)
+    work.end()
 
 
 def scatter_all(outer, terms, pieces):
     count = len(terms)
-    shape = lambda p, *lead: pltpu.VMEM(
-        lead + (terms[pieces[p][0]].shape[-2], pieces[p][2]), terms[pieces[p][0]].dtype
-    )
-    n = range(len(pieces))
+    shapes = [term.shape[-2:] + (term.dtype,) for term in terms]
     return pl.pallas_call(
         functools.partial(scatter_kernel, outer, pieces, count),
         out_shape=[jax.ShapeDtypeStruct(term.shape[-2:], jnp.float32) for term in terms],
         in_specs=[pl.BlockSpec(memory_space=pl.ANY)] * count,
         out_specs=[pl.BlockSpec(memory_space=pltpu.VMEM)] * count,
-        scratch_shapes=[shape(p, outer, 2, 2) for p in n]
-        + [shape(p, outer, 2, 2) for p in n]
-        + [shape(p, outer, 2) for p in n]
-        + [shape(p, outer) for p in n]
-        + [shape(p, max(outer - 1, 1)) for p in n]
-        + [
-            pltpu.SemaphoreType.DMA((len(pieces),)),
-            pltpu.SemaphoreType.DMA((len(pieces), outer + 2)),
-            pltpu.SemaphoreType.DMA((len(pieces), outer + 2)),
-        ],
+        scratch_shapes=Scatter.scratch(outer, shapes, pieces),
         compiler_params=pltpu.CompilerParams(
             collective_id=1, has_side_effects=True, vmem_limit_bytes=VMEM_LIMIT
         ),
@@ -784,6 +810,267 @@
     )(x, dq, dk, dv, weight, late, middle_grad, vectors)
 
 
+def spread_vectors(slots, size, fc_size, width):
+    outer = slots.shape[0]
+    zeros = jnp.zeros((8, width - PAIR), jnp.float32)
+    first, second = None, None
+    for d in range(outer * 8):
+        index = (d // 8, (d // 4) % 2, (d // 2) % 2, d % 2)
+        top = jnp.concatenate([slots[index + (slice(0, 8),)], zeros], axis=1)
+        low = jnp.concatenate([slots[index + (slice(8, 16),)], zeros], axis=1)
+        top = pltpu.roll(top, d * size, 1) if d else top
+        row, lane = divmod(d * fc_size, width)
+        low = pltpu.roll(low, lane, 1) if lane else low
+        low = pltpu.roll(low, row, 0) if row else low
+        first = top if first is None else first + top
+        second = low if second is None else second + low
+    return first, second
+
+
+def join_rows(target, slots, columns):
+    outer, rows = slots.shape[0], slots.shape[-2]
+
+    def body(a, carry):
+        for y in range(2):
+            for c in range(2):
+                both = [slots[a, y, c, s, :, columns].astype(jnp.float32) for s in range(2)]
+                start = pl.multiple_of(((a * 2 + y) * 2 + c) * (2 * rows), 2 * rows)
+                joined = jnp.concatenate(both, axis=0).astype(target.dtype)
+                target[pl.ds(start, 2 * rows), columns] = joined
+        return carry
+
+    lax.fori_loop(0, outer, body, 0)
+
+
+VECTORS = 9
+
+
+def forward_kernel(outer, pieces, *refs):
+    tokens_hbm, starts_ref = refs[:2]
+    vector_refs = refs[2 : 2 + VECTORS]
+    shards = refs[2 + VECTORS : 6 + VECTORS]
+    outs = refs[6 + VECTORS : 17 + VECTORS]
+    (
+        normed_hbm, q_hbm, k_hbm, v_hbm, probs_hbm, att_hbm, inverse_hbm, weight_hbm, *slots_hbm,
+    ) = outs
+    vectors = refs[17 + VECTORS]
+    (
+        own, vector_slots, qkv_slots, weight, x, normed, q, k, v, probs, att, inverse,
+        q_cols, k_cols, move_sem, out_sem, probs_sem, own_sem, send_sem, recv_sem,
+    ) = refs[18 + VECTORS :]
+    rows, local, width = q.shape
+    a, y, c, s = place()
+    size, fc_size = vector_refs[0].shape[1], vector_refs[-1].shape[1]
+
+    load = pltpu.make_async_copy(tokens_hbm, x.at[:, pl.ds(TILE, local)], move_sem.at[0])
+    load.start()
+    own[...] = jnp.zeros_like(own)
+    for i, ref in enumerate(vector_refs):
+        own[i : i + 1, : ref.shape[1]] = ref[...].astype(jnp.float32)
+    greet(outer)
+    prev = remote(
+        tokens_hbm.at[:, pl.ds(local - TILE, TILE)],
+        x.at[:, pl.ds(0, TILE)],
+        move_sem.at[1],
+        move_sem.at[2],
+        device(a, y, c, 1 - s),
+    )
+    work = Gather(
+        outer, pieces, (own,) + shards, (vector_slots, qkv_slots) + tuple(slots_hbm), own_sem, send_sem, recv_sem
+    )
+    work.step(0)
+
+    @pl.when(s == 0)
+    def _():
+        prev.start()
+        for r in range(rows):
+            x[r, 0:TILE] = jnp.zeros((TILE, width), x.dtype)
+
+    load.wait()
+    ready = work.lags[3]
+    for t in range(1, ready + 1):
+        work.step(t)
+    first, second = spread_vectors(vector_slots, size, fc_size, width)
+    vectors[0:8], vectors[8:16] = first, second
+
+    @pl.when(s == 1)
+    def _():
+        prev.wait_recv()
+
+    def norm_step(n, carry):
+        r, t = n // (local // TILE + 1), lax.rem(n, local // TILE + 1)
+        span = pl.ds(pl.multiple_of(t * TILE, TILE), TILE)
+        normal, _ = normalize(x[r, span].astype(jnp.float32))
+        normed[r, span] = (normal * vectors[0:1] + vectors[1:2]).astype(jnp.bfloat16)
+        return carry
+
+    lax.fori_loop(0, rows * (local // TILE + 1), norm_step, 0)
+    stores = []
+
+    def store(src, dst):
+        copy = pltpu.make_async_copy(src, dst, out_sem.at[len(stores)])
+        copy.start()
+        stores.append(copy)
+
+    store(normed, normed_hbm)
+    for third in range(3):
+        work.step(ready + 1 + third)
+        columns = slice(third * width, (third + 1) * width)
+        join_rows(weight, qkv_slots, columns)
+
+        def row_step(r, carry):
+            if third == 0:
+                value = dot_nn(normed[r, TILE:], weight[:, columns]) + vectors[2:3]
+                q[r] = value.astype(jnp.bfloat16) * jnp.bfloat16(1.0 / math.sqrt(HD))
+            elif third == 1:
+                k[r] = dot_nn(normed[r], weight[:, columns]).astype(jnp.bfloat16)
+            else:
+                v[r] = (dot_nn(normed[r], weight[:, columns]) + vectors[3:4]).astype(jnp.bfloat16)
+            return carry
+
+        lax.fori_loop(0, rows, row_step, 0)
+        store((q, k, v)[third], (q_hbm, k_hbm, v_hbm)[third])
+    store(weight, weight_hbm)
+    for r in range(rows):
+        mask_columns(starts_ref, r, q_cols.at[r], k_cols.at[r])
+    lane = lane_index(TILE)
+    causal = lax.broadcasted_iota(jnp.int32, (TILE, TILE), 1) <= lax.broadcasted_iota(
+        jnp.int32, (TILE, TILE), 0
+    )
+    ones = jnp.ones((TILE, PAIR), jnp.bfloat16)
+    pairs = width // PAIR
+    done = ready + 4
+
+    def probs_copy(slot, r, j):
+        return pltpu.make_async_copy(probs.at[slot], probs_hbm.at[r, j], probs_sem.at[slot])
+
+    def attend_step(n, carry):
+        r, j = n // pairs, lax.rem(n, pairs)
+        slot = lax.rem(n, 2)
+        pair = pl.ds(pl.multiple_of(j * PAIR, PAIR), PAIR)
+        for i, t in enumerate(range(done, work.steps)):
+
+            @pl.when(n == 2 * i + 1)
+            def _():
+                work.step(t)
+
+        @pl.when(n >= 2)
+        def _():
+            probs_copy(slot, r, j).wait()
+
+        for tile in range(2):
+            span = pl.ds(tile * TILE, TILE)
+            queries = q[r, span, pair]
+            around = [pl.ds((tile + w) * TILE, TILE) for w in range(2)]
+            keys = [
+                jnp.concatenate([k[r, around[w], pair], k_cols[r, tile, w]], axis=1) for w in range(2)
+            ]
+            values = [jnp.concatenate([v[r, around[w], pair], ones], axis=1) for w in range(2)]
+            mixed, shares = [], []
+            for head in range(2):
+                mine = (lane < HD) if head == 0 else (lane >= HD)
+                left = jnp.concatenate(
+                    [jnp.where(mine, queries, jnp.bfloat16(0)), q_cols[r, tile]], axis=1
+                )
+                far = dot_nt(left, keys[0])
+                near = jnp.where(causal, dot_nt(left, keys[1]), -FIRM)
+                top = jnp.max(jnp.maximum(far, near), axis=-1, keepdims=True)
+                far = jnp.exp(far - top).astype(jnp.bfloat16)
+                near = jnp.exp(near - top).astype(jnp.bfloat16)
+                probs[slot, tile, head, 0] = far
+                probs[slot, tile, head, 1] = near
+                total = dot_nn(far, values[0]) + dot_nn(near, values[1])
+                share = 1.0 / total[:, PAIR:]
+                mixed.append(total[:, :PAIR] * share)
+                shares.append(share)
+            att[r, span, pair] = jnp.where(lane < HD, mixed[0], mixed[1]).astype(jnp.bfloat16)
+            inverse[r, span, pair] = jnp.where(lane < HD, shares[0], shares[1])
+        probs_copy(slot, r, j).start()
+        return carry
+
+    steps = rows * pairs
+    lax.fori_loop(0, steps, attend_step, 0)
+    store(att, att_hbm)
+    store(inverse, inverse_hbm)
+    for t in range(done + steps // 2, work.steps):
+        work.step(t)
+    work.end()
+    for n in range(2):
+        probs_copy(n, 0, n).wait()
+    for copy in stores:
+        copy.wait()
+
+    @pl.when(s == 0)
+    def _():
+        prev.wait_send()
+
+
+def forward(outer, tokens, starts, vectors, weights):
+    rows, local, width = tokens.shape
+    devices = outer * 8
+    low, full = jnp.bfloat16, jnp.float32
+    pairs = width // PAIR
+    pieces = [(0, 0, PAIR, 0)]
+    pieces += [(1, i * width, width, (i + 1) % 2) for i in range(3)]
+    for i, weight in enumerate(weights[1:]):
+        parts = max(weight.shape[0] * weight.shape[1] // (weights[0].shape[0] * width), 1)
+        parts = min(parts, weight.shape[1] // PAIR)
+        while weight.shape[1] % (parts * PAIR):
+            parts -= 1
+        step = weight.shape[1] // parts
+        pieces += [(2 + i, j * step, step, (len(pieces) + j) % 2) for j in range(parts)]
+    anywhere = pl.BlockSpec(memory_space=pl.ANY)
+    vmem = pl.BlockSpec(memory_space=pltpu.VMEM)
+    extended = (rows, local + TILE, width)
+    qkv = (devices * weights[0].shape[0], weights[0].shape[1])
+    slots = [(outer, 2, 2, 2) + weight.shape for weight in weights]
+    results = pl.pallas_call(
+        functools.partial(forward_kernel, outer, pieces),
+        in_specs=[anywhere, pl.BlockSpec(memory_space=pltpu.SMEM)] + [vmem] * (VECTORS + 4),
+        out_specs=[anywhere] * 11 + [vmem],
+        out_shape=[
+            jax.ShapeDtypeStruct(extended, low),
+            jax.ShapeDtypeStruct(tokens.shape, low),
+            jax.ShapeDtypeStruct(extended, low),
+            jax.ShapeDtypeStruct(extended, low),
+            jax.ShapeDtypeStruct((rows, pairs, 2, 2, 2, TILE, TILE), low),
+            jax.ShapeDtypeStruct(tokens.shape, low),
+            jax.ShapeDtypeStruct(tokens.shape, full),
+            jax.ShapeDtypeStruct(qkv, low),
+        ]
+        + [jax.ShapeDtypeStruct(slot, low) for slot in slots[1:]]
+        + [jax.ShapeDtypeStruct((16, width), full)],
+        scratch_shapes=[
+            pltpu.VMEM((16, PAIR), full),
+            pltpu.VMEM((outer, 2, 2, 2, 16, PAIR), full),
+            pltpu.VMEM(slots[0], low),
+            pltpu.VMEM(qkv, low),
+            pltpu.VMEM(extended, low),
+            pltpu.VMEM(extended, low),
+            pltpu.VMEM(tokens.shape, low),
+            pltpu.VMEM(extended, low),
+            pltpu.VMEM(extended, low),
+            pltpu.VMEM((2, 2, 2, 2, TILE, TILE), low),
+            pltpu.VMEM(tokens.shape, low),
+            pltpu.VMEM(tokens.shape, full),
+            pltpu.VMEM((rows, 2, TILE, PAIR), low),
+            pltpu.VMEM((rows, 2, 2, TILE, PAIR), low),
+            pltpu.SemaphoreType.DMA((3,)),
+            pltpu.SemaphoreType.DMA((8,)),
+            pltpu.SemaphoreType.DMA((2,)),
+        ]
+        + Gather.semaphores(outer, 5, len(pieces)),
+        compiler_params=pltpu.CompilerParams(
+            collective_id=2, has_side_effects=True, vmem_limit_bytes=VMEM_LIMIT
+        ),
+    )(tokens, starts, *[vector.reshape(1, -1) for vector in vectors], *weights)
+    normed, q, k, v, probs, att, inverse, weight, *slots, whole_vectors = results
+    whole = [weight] + [
+        slot.reshape(devices * w.shape[0], w.shape[1]) for slot, w in zip(slots, weights[1:])
+    ]
+    return whole, whole_vectors, normed, q, k, v, probs, att, inverse
+
+
 def gather_weights(outer, weights, vectors, fc_bias):
     devices = outer * 8
     shards = [pack_vectors(vectors + [fc_bias])]
@@ -838,19 +1125,21 @@
     outer = lax.axis_size("batch") // 4
     rows, local, width = tokens_in.shape
     seq = lax.axis_index("seq")
-    prev = lax.ppermute(tokens_in[:, local - TILE :], "seq", [(0, 1)])
-    (qkv, attn, fc, proj), vectors = gather_weights(
-        outer,
-        [qkv_weight, attn_weight, fc_weight, proj_weight],
-        [norm1_gain, norm1_bias, query_bias, value_bias, attn_bias, norm2_gain, norm2_bias, proj_bias],
-        fc_bias,
-    )
     first = 2 * seq
     padded = jnp.pad(doc_starts, ((0, 0), (1, 0)))
     starts = lax.dynamic_slice_in_dim(padded, first, 3, 1)
     starts = starts - TILE * (first - 1 + jnp.arange(3, dtype=jnp.int32))
-    normed, q, k, v = project(tokens_in, prev, qkv, vectors)
-    probs, att, inverse = attend(starts, q, k, v)
+    weights = [qkv_weight, attn_weight, fc_weight, proj_weight]
+    vectors = [norm1_gain, norm1_bias, query_bias, value_bias, attn_bias, norm2_gain, norm2_bias, proj_bias]
+    if qkv_weight.shape[0] % 8 == 0:
+        (qkv, attn, fc, proj), vectors, normed, q, k, v, probs, att, inverse = forward(
+            outer, tokens_in, starts, vectors + [fc_bias], weights
+        )
+    else:
+        prev = lax.ppermute(tokens_in[:, local - TILE :], "seq", [(0, 1)])
+        (qkv, attn, fc, proj), vectors = gather_weights(outer, weights, vectors, fc_bias)
+        normed, q, k, v = project(tokens_in, prev, qkv, vectors)
+        probs, att, inverse = attend(starts, q, k, v)
     flat = lambda value: value.reshape(rows * local, width)
     out, middle_grad, att_grad, attn_grad, fc_grad, proj_grad, mlp_sums = mlp(
         flat(tokens_in), flat(att), flat(out_grad), attn, fc, proj, vectors

time: 348 us -> 306 us (0.88)
  Pallas kernels: 296 us -> 270 us
  local copies, waits for them, and re-layouts: 22.3 us -> 12.8 us
  starting transfers between devices: 6.17 us -> 1.28 us
    pallas_call x3 -> x1, Pallas kernels: 113 us -> 89.5 us  [forward(): pl.pallas_call(functools.partial(forward_kernel, outer, pieces), in_specs...]
    concatenate x2 -> x0, local copies, waits for them, and re-layouts: 6.12 us -> none  [the longest x1 6.11 us: pack_vectors(): jnp.concatenate([part.astype(jnp.float32) for part in parts], axis=-1)]
    ppermute x1 -> x0, starting transfers between devices: 4.89 us -> none  [shards(): prev = lax.ppermute(tokens_in[:, local - TILE:], 'seq', [(0, 1)])]
    unnamed x17 -> x9, local copies, waits for them, and re-layouts: 9.96 us -> 8.13 us
  transfers between devices with their start and end apart: 2 -> 1, of which waited for: 1 -> 1; matrix products, arithmetic and copies ran while one was open for 3% -> 0% of each run, Pallas kernels for 24% -> 0%
where the time goes in v3:
time: 306 us; the launch traced here: 305 us
  Pallas kernels  270 us (88%)
  waiting for transfers between devices  19 us (6%)
  local copies, waits for them, and re-layouts  12.8 us (4%)
    pallas_call x1, Pallas kernels, forward(): pl.pallas_call(functools.partial(forward_kernel, outer, pieces), in_specs...  89.5 us
    pallas_call x1, Pallas kernels, scatter_all(): pl.pallas_call(functools.partial(scatter_kernel, outer, pieces, count), o...  75.5 us
    pallas_call x1, Pallas kernels, mlp(): pl.pallas_call(mlp_kernel, in_specs=[anywhere] * 6 + [vmem], out_specs=[a...  47.5 us
    pallas_call x1, Pallas kernels, attend_grad(): pl.pallas_call(attend_grad_kernel, grid=(rows, pairs), in_specs=[pl.Block...  34.7 us
    ppermute x1, waiting for transfers between devices, shards(): late = lax.ppermute(prev_grad, 'seq', [(1, 0)])  19 us
    pallas_call x1, Pallas kernels, project_grad(): pl.pallas_call(project_grad_kernel, in_specs=[vmem] * 5, out_specs=[vmem]...  12.7 us
    pallas_call x1, Pallas kernels, tokens_grad_of(): pl.pallas_call(tokens_grad_kernel, grid=(rows, local // TILE), in_specs=[...  10.3 us
    unnamed x9, local copies, waits for them, and re-layouts  8.13 us
  transfers between devices with their start and end apart: 1, of which 1 were waited for; matrix products, arithmetic and copies ran while one was open for 0% of the time, Pallas kernels for 0%

profile of v3, /device:TPU:0, one launch (start us, length us, event | category | flops | bytes accessed | tf_op | source)
XLA Modules:
  0.0 305.4 jit_solution(16934959510242339522)
XLA Ops:
  0.7 1.3 dynamic-slice_subtract_fusion.refs_1_
  2.0 89.5 %shard_map.271 = (bf16[2,768,768]{2,1,0:T(8,128)(2,1)}, bf16[2,512,768]{2,1,0:T(8,128)(2,1)}, bf16[2,768,768]{2,1,0:T(8,128)(2,1)}, bf16[2,768,768]{2,1,0:T(8,12...) custom-call(bf16[2,512,768]{2,1,0:T(8,128)(2,1)} %x_ref.1, ...), custom_call_target="tpu_custom_call" | custom-call | tf_op jit(solution)/shard_map/pallas_call | solution.py:1027
  91.5 47.5 %shard_map.272 = (bf16[1024,768]{1,0:T(8,128)(2,1)}, f32[1024,768]{1,0:T(8,128)}, bf16[1024,768]{1,0:T(8,128)(2,1)}, bf16[768,768]{1,0:T(8,128)(2,1)}, bf16[768,...) custom-call(bf16[1024,768]{1,0:T(8,128)(2,1)} %bitcast.28, bf16[1024,768]{1,0:T(8,128)(2,1)} %bitcast.29, ...), custom_call_target="tpu_custom_call" | custom-call | tf_op jit(solution)/shard_map/pallas_call | solution.py:693
  139.0 34.7 %shard_map.273 = (bf16[2,512,768]{2,1,0:T(8,128)(2,1)}, bf16[2,768,768]{2,1,0:T(8,128)(2,1)}, bf16[2,768,768]{2,1,0:T(8,128)(2,1)}) custom-call(bf16[2,6,2,2,2,256,256]{6,5,4,3,2,1,0:T(8,128)(2,1)} %get-tuple-element.53.probs_ref, bf16[2,512,768]{2,1,0:T(8,128)(2,1)} %get-tuple-element.54.q_ref, bf16[2,768,768]{2,1,0:T(8,128)(2,1)} %get-tuple-element.55.k_ref, ...), custom_call_target="tpu_custom_call" | custom-call | tf_op jit(solution)/shard_map/pallas_call | solution.py:562
  173.7 0.0 copy-start.1
  173.7 12.7 %shard_map.274 = (bf16[768,2304]{1,0:T(8,128)(2,1)}, bf16[2,256,768]{2,1,0:T(8,128)(2,1)}, f32[8,768]{1,0:T(8,128)}) custom-call(bf16[2,768,768]{2,1,0:T(8,128)(2,1)} %get-tuple-element.63.normed, bf16[2,512,768]{2,1,0:T(8,128)(2,1)} %get-tuple-element.59.dq, bf16[2,768,768]{2,1,0:T(8,128)(2,1)} %get-tuple-element.60.dk, ...), custom_call_target="tpu_custom_call" | custom-call | tf_op jit(solution)/shard_map/pallas_call | solution.py:756
  186.4 1.3 collective-permute-start
  187.7 0.0 copy-done.1
  187.8 0.1 reshape.133
  187.8 0.7 slice.40
  188.6 19.0 %collective-permute-done.late = bf16[2,256,768]{2,1,0:T(8,128)(2,1)S(1)} collective-permute-done((bf16[2,256,768]{2,1,0:T(8,128)(2,1)}, bf16[2,256,768]{2,1,0:T(8,128)(2,1)S(1)}, u32[]{:S(2)}, u32[]{:S(2)}) %collective-permute-start) | collective-permute-done | bytes 786464 | tf_op jit(solution)/shard_map/ppermute | solution.py:1150
  207.6 0.0 copy-start
  207.6 0.9 copy-done
  208.5 10.3 %shard_map.275 = (f32[2,512,768]{2,1,0:T(8,128)}, f32[8,768]{1,0:T(8,128)}) custom-call(bf16[2,512,768]{2,1,0:T(8,128)(2,1)} %x_ref.1, bf16[2,512,768]{2,1,0:T(8,128)(2,1)} %get-tuple-element.59.dq, bf16[2,768,768]{2,1,0:T(8,128)(2,1)} %get-tuple-element.60.dk, bf16[2,768,768]{2,1,0:T(8,128)(2,1)} %get-tuple-element.61.dv, ...), custom_call_target="tpu_custom_call" | custom-call | tf_op jit(solution)/shard_map/pallas_call | solution.py:791
  218.8 0.7 slice.39
  219.5 0.1 reshape.131
  219.6 0.1 copy.32
  219.7 0.1 reshape.132
  219.8 0.1 fusion
  219.9 0.7 copy.33
  220.6 75.5 %shard_map.276 = (f32[8,128]{1,0:T(8,128)}, f32[24,2304]{1,0:T(8,128)}, f32[24,768]{1,0:T(8,128)}, f32[24,3072]{1,0:T(8,128)}, f32[96,768]{1,0:T(8,128)}) custom-call(f32[4,2,2,2,8,128]{5,4,3,2,1,0:T(8,128)} %bitcast.40, bf16[4,2,2,2,24,2304]{5,4,3,2,1,0:T(8,128)(2,1)} %bitcast.34, bf16[4,2,2,2,24,768]{5,4,3,2,1,0:T(8,128)(2,1)} %bitcast.38, ...), custom_call_target="tpu_custom_call" | custom-call | tf_op jit(solution)/shard_map/pallas_call | solution.py:305
  296.1 1.2 slice.50
  297.3 1.6 fusion.2
  298.9 1.6 copy.38
  300.5 1.5 copy.39
  302.1 1.7 copy.40
  303.7 1.7 copy.41
  (3 shorter events, 0.0 us)
Async XLA Ops:
  173.7 14.0 %copy-start.1 = (f32[8,768]{1,0:T(8,128)S(1)}, f32[8,768]{1,0:T(8,128)}, u32[]{:S(2)}) copy-start(f32[8,768]{1,0:T(8,128)} %get-tuple-element.69) | copy-start | bytes 73732
  186.4 21.1 %collective-permute-start = (bf16[2,256,768]{2,1,0:T(8,128)(2,1)}, bf16[2,256,768]{2,1,0:T(8,128)(2,1)S(1)}, u32[]{:S(2)}, u32[]{:S(2)}) collective-permute-start(bf16[2,256,768]{2,1,0:T(8,128)(2,1)} %get-tuple-element.64), channel_id=1, source_target_pairs={{1,0},{3,2},{5,4},{7,6},{9,8},{11,10},{13,12},{15,14},{17,16},{19,... | collective-permute-start | bytes 2359304 | tf_op jit(solution)/shard_map/ppermute | solution.py:1150
  207.6 0.9 copy-start

commit v4 on v3

--- a/solution.py
+++ b/solution.py
@@ -163,14 +163,14 @@
 
 
 class Scatter:
-    lags = (1, 3, 4, 5)
-
-    def __init__(self, outer, pieces, terms, outs, slots, own_sem, send_sem, recv_sem):
+    def __init__(self, outer, pieces, terms, outs, slots, own_sem, send_sem, recv_sem, times=None, places=None):
         self.outer, self.pieces, self.terms, self.outs = outer, pieces, terms, outs
         n = len(pieces)
         self.held, self.got = slots[:n], [slots[k * n : (k + 1) * n] for k in range(1, 5)]
         self.own_sem, self.send_sem, self.recv_sem = own_sem, send_sem, recv_sem
-        self.steps = n + self.lags[3]
+        self.times = times or [(p, p + 1, p + 3, p + 4, p + 5) for p in range(n)]
+        self.places = places or {}
+        self.steps = max(time[4] for time in self.times) + 1
         self.place = place()
 
     def sems(self, p, k):
@@ -211,37 +211,35 @@
         return remote(src, self.got[3][p].at[k - 1], *self.sems(p, 2 + k), device(to, y, c, s))
 
     def step(self, t):
-        outer, count, lags = self.outer, len(self.pieces), self.lags
+        outer = self.outer
         a, y, c, s = self.place
-        if t < count:
-            self.own(t).start()
-            self.first(t).start()
-        p = t - lags[0]
-        if 0 <= p < count:
-            self.own(p).wait()
-            self.first(p).wait_recv()
-            add_slots(self.held[p], self.got[0][p])
-            self.second(p).start()
-        p = t - lags[1]
-        if 0 <= p < count:
-            self.second(p).wait_recv()
-            mine = (EVERY, EVERY, s) if self.pieces[p][3] == 0 else (EVERY, y)
-            add_slots(self.held[p].at[mine], self.got[1][p])
-            self.third(p).start()
-        p = t - lags[2]
-        if 0 <= p < count:
-            self.third(p).wait_recv()
-            add_slots(self.held[p].at[:, y, s], self.got[2][p])
-            for k in range(1, outer):
-                self.fourth(p, k).start()
-        p = t - lags[3]
-        if 0 <= p < count:
-            i, start, width, order = self.pieces[p]
-            value = self.held[p][a, y, s].astype(jnp.float32)
-            for k in range(1, outer):
-                self.fourth(p, k).wait_recv()
-                value = value + self.got[3][p][k - 1].astype(jnp.float32)
-            self.outs[i][:, pl.ds(start, width)] = value
+        for p, times in enumerate(self.times):
+            if t == times[4]:
+                i, start, width, order = self.pieces[p]
+                value = self.held[p][a, y, s].astype(jnp.float32)
+                for k in range(1, outer):
+                    self.fourth(p, k).wait_recv()
+                    value = value + self.got[3][p][k - 1].astype(jnp.float32)
+                for offset, size, to in self.places.get(p, [(0, width, start)]):
+                    self.outs[i][:, to : to + size] = value[:, offset : offset + size]
+            if t == times[3]:
+                self.third(p).wait_recv()
+                add_slots(self.held[p].at[:, y, s], self.got[2][p])
+                for k in range(1, outer):
+                    self.fourth(p, k).start()
+            if t == times[2]:
+                self.second(p).wait_recv()
+                mine = (EVERY, EVERY, s) if self.pieces[p][3] == 0 else (EVERY, y)
+                add_slots(self.held[p].at[mine], self.got[1][p])
+                self.third(p).start()
+            if t == times[1]:
+                self.own(p).wait()
+                self.first(p).wait_recv()
+                add_slots(self.held[p], self.got[0][p])
+                self.second(p).start()
+            if t == times[0]:
+                self.own(p).start()
+                self.first(p).start()
 
     def end(self):
         for p in range(len(self.pieces)):
@@ -1071,6 +1069,521 @@
     return whole, whole_vectors, normed, q, k, v, probs, att, inverse
 
 
+def shares_out(rows, columns):
+    return jax.ShapeDtypeStruct((rows, columns), jnp.float32)
+
+
+def column_pieces(array, columns, parts, orders):
+    step = columns // parts
+    return [(array, j * step, step, orders[j % len(orders)]) for j in range(parts)]
+
+
+def mlp_scatter_kernel(
+    outer, pieces, times,
+    x_hbm, att_hbm, dy_hbm, attn_hbm, fc_hbm, proj_hbm, vectors,
+    out_hbm, middle_grad_hbm, att_grad_hbm, attn_grad_hbm, fc_grad_hbm, sums_ref, proj_share,
+    x, att, dy, attn, fc, proj, hidden, slope, normed, branch, middle, att_grad,
+    attn_grad, proj_terms, in_sem, out_sem, *rest,
+):
+    tokens, width = x.shape
+    chunks = fc.shape[1] // CHUNK
+    tiles = tokens // MLP_TILE
+    loads = [
+        pltpu.make_async_copy(src, dst, in_sem.at[i])
+        for i, (src, dst) in enumerate(
+            ((att_hbm, att), (attn_hbm, attn), (x_hbm, x), (fc_hbm, fc), (dy_hbm, dy), (proj_hbm, proj))
+        )
+    ]
+    for load in loads:
+        load.start()
+    greet(outer)
+    work = Scatter(outer, pieces, (proj_terms,), (proj_share,), rest[:-3], *rest[-3:], times)
+    sums_ref[...] = jnp.zeros_like(sums_ref)
+    for load in loads[:3]:
+        load.wait()
+
+    def forward_step(t, carry):
+        span = pl.ds(pl.multiple_of(t * MLP_TILE, MLP_TILE), MLP_TILE)
+        value = x[span].astype(jnp.float32) + dot_nn(att[span], attn[...]) + vectors[4:5]
+        middle[span] = value
+        normal, _ = normalize(value)
+        low = (normal * vectors[5:6] + vectors[6:7]).astype(jnp.bfloat16)
+        normed[span] = low
+
+        @pl.when(t == 0)
+        def _():
+            loads[3].wait()
+
+        for j in range(chunks):
+            columns = pl.ds(j * CHUNK, CHUNK)
+            pre = dot_nn(low, fc[:, columns]) + vectors[8 + j : 9 + j]
+            value, back = gelu_pair(pre)
+            hidden[span, columns] = value.astype(jnp.bfloat16)
+            slope[span, columns] = back.astype(jnp.bfloat16)
+        return carry
+
+    lax.fori_loop(0, tiles, forward_step, 0)
+    loads[4].wait()
+    share = proj_terms.shape[-2]
+    each = CHUNK // (8 * share)
+    for j in range(chunks):
+        columns = pl.ds(j * CHUNK, CHUNK)
+        grad = dot_tn(hidden[:, columns], dy[...]).astype(jnp.bfloat16)
+        proj_terms[j * each : (j + 1) * each] = grad.reshape((each, 2, 2, 2, share, width))
+    loads[5].wait()
+
+    def backward_step(t, carry):
+        span = pl.ds(pl.multiple_of(t * MLP_TILE, MLP_TILE), MLP_TILE)
+        for i in range(work.steps):
+            if i < 2 * tiles and i % 2 == 0:
+
+                @pl.when(t == i // 2)
+                def _():
+                    work.step(i)
+
+        upstream = dy[span]
+        result = middle[span] + vectors[7:8]
+        back = None
+        for j in range(chunks):
+            columns = pl.ds(j * CHUNK, CHUNK)
+            grad = dot_nt(upstream, proj[columns]) * slope[span, columns].astype(jnp.float32)
+            grad = grad.astype(jnp.bfloat16)
+            slope[span, columns] = grad
+            sums_ref[4 + j : 5 + j] += column_sum(grad.astype(jnp.float32))
+            part = dot_nt(grad, fc[:, columns])
+            back = part if back is None else back + part
+            if j == chunks // 2 - 1:
+                for i in range(1, 2 * tiles, 2):
+
+                    @pl.when(t == i // 2)
+                    def _():
+                        work.step(i)
+
+            result = result + dot_nn(hidden[span, columns], proj[columns])
+        x[span] = result.astype(jnp.bfloat16)
+        normal, scale = normalize(middle[span])
+        upstream = upstream.astype(jnp.float32)
+        sums_ref[0:1] += column_sum(upstream)
+        sums_ref[1:2] += column_sum(back * normal)
+        sums_ref[2:3] += column_sum(back)
+        total = upstream + norm_grad(back, vectors[5:6], normal, scale)
+        middle[span] = total
+        total = total.astype(jnp.bfloat16)
+        branch[span] = total
+        sums_ref[3:4] += column_sum(total.astype(jnp.float32))
+        att_grad[span] = dot_nt(total, attn[...]).astype(jnp.bfloat16)
+        return carry
+
+    lax.fori_loop(0, tiles, backward_step, 0)
+    stores = []
+
+    def store(src, dst):
+        copy = pltpu.make_async_copy(src, dst, out_sem.at[len(stores)])
+        copy.start()
+        stores.append(copy)
+
+    store(x, out_hbm)
+    store(middle, middle_grad_hbm)
+    store(att_grad, att_grad_hbm)
+    t = 2 * tiles
+    for j in range(chunks):
+        columns = pl.ds(j * CHUNK, CHUNK)
+        grad = dot_tn(normed[...], slope[:, columns]).astype(jnp.bfloat16)
+        hidden[0:width, columns] = grad
+        store(hidden.at[pl.ds(0, width), columns], fc_grad_hbm.at[:, columns])
+        if t < work.steps:
+            work.step(t)
+            t += 1
+    attn_grad[...] = dot_tn(att[...], branch[...]).astype(jnp.bfloat16)
+    store(attn_grad, attn_grad_hbm)
+    while t < work.steps:
+        work.step(t)
+        t += 1
+    work.end()
+    for copy in stores:
+        copy.wait()
+
+
+def mlp_scatter(outer, x, att, dy, attn, fc, proj, vectors):
+    tokens, width = x.shape
+    hidden = fc.shape[1]
+    share = hidden // (outer * 8)
+    low, full = jnp.bfloat16, jnp.float32
+    anywhere = pl.BlockSpec(memory_space=pl.ANY)
+    vmem = pl.BlockSpec(memory_space=pltpu.VMEM)
+    pieces = column_pieces(0, width, 3, (0, 1))
+    times = [(0, 1, 5, 8, 11), (0, 1, 5, 8, 11), (1, 3, 9, 11, 13)]
+    return pl.pallas_call(
+        functools.partial(mlp_scatter_kernel, outer, pieces, times),
+        in_specs=[anywhere] * 6 + [vmem],
+        out_specs=[anywhere] * 5 + [vmem] * 2,
+        out_shape=[
+            jax.ShapeDtypeStruct((tokens, width), low),
+            jax.ShapeDtypeStruct((tokens, width), full),
+            jax.ShapeDtypeStruct((tokens, width), low),
+            jax.ShapeDtypeStruct(attn.shape, low),
+            jax.ShapeDtypeStruct(fc.shape, low),
+            jax.ShapeDtypeStruct((8, width), full),
+            shares_out(share, width),
+        ],
+        scratch_shapes=[
+            pltpu.VMEM((tokens, width), low),
+            pltpu.VMEM((tokens, width), low),
+            pltpu.VMEM((tokens, width), low),
+            pltpu.VMEM(attn.shape, low),
+            pltpu.VMEM(fc.shape, low),
+            pltpu.VMEM(proj.shape, low),
+            pltpu.VMEM((tokens, hidden), low),
+            pltpu.VMEM((tokens, hidden), low),
+            pltpu.VMEM((tokens, width), low),
+            pltpu.VMEM((tokens, width), low),
+            pltpu.VMEM((tokens, width), full),
+            pltpu.VMEM((tokens, width), low),
+            pltpu.VMEM(attn.shape, low),
+            pltpu.VMEM((outer, 2, 2, 2, share, width), low),
+            pltpu.SemaphoreType.DMA((6,)),
+            pltpu.SemaphoreType.DMA((12,)),
+        ]
+        + Scatter.scratch(outer, [(share, width, low)], pieces),
+        compiler_params=pltpu.CompilerParams(
+            collective_id=3, has_side_effects=True, vmem_limit_bytes=VMEM_LIMIT
+        ),
+    )(x, att, dy, attn, fc, proj, vectors)
+
+
+def pack_columns(values, start, lanes):
+    width = values.shape[1]
+    moved = pltpu.roll(values, (width - start) % width, 1) if start % width else values
+    return jnp.where(lane_index(values.shape[0]) < lanes, moved[:, :PAIR], 0.0)
+
+
+def backward_kernel(
+    outer, pieces, times, places, count,
+    probs_hbm, q_hbm, k_hbm, v_hbm, normed_hbm, grad_hbm, att_hbm, inverse_hbm, x_hbm, middle_hbm,
+    weight_hbm, vectors, mlp_sums, *refs,
+):
+    terms, refs = refs[:count], refs[count:]
+    tokens_grad_hbm, refs = refs[0], refs[1:]
+    shares, refs = refs[: count + 2], refs[count + 2 :]
+    (
+        q, k, v, normed, grad, att, inverse, x, middle, weight, probs, dq, dk, dv, dq_part, dk_sum,
+        dv_sum, prev, late, qkv_terms, vector_terms, sums, in_sem, probs_sem, out_sem, late_sem, *rest,
+    ) = refs
+    rows, local, width = q.shape
+    pairs = width // PAIR
+    a, y, c, s = place()
+    loads = [
+        pltpu.make_async_copy(src, dst, in_sem.at[i])
+        for i, (src, dst) in enumerate(
+            (
+                (q_hbm, q), (k_hbm, k), (v_hbm, v), (grad_hbm, grad), (att_hbm, att), (inverse_hbm, inverse),
+                (weight_hbm, weight), (normed_hbm, normed), (x_hbm, x), (middle_hbm, middle),
+            )
+        )
+    ]
+
+    def far_copy(slot, r, j):
+        return pltpu.make_async_copy(
+            probs_hbm.at[r, j, 0, :, 0], probs.at[slot, 0, :, 0], probs_sem.at[slot]
+        )
+
+    def near_copy(slot, r, j):
+        return pltpu.make_async_copy(
+            probs_hbm.at[r, j, :, :, 1], probs.at[slot, :, :, 1], probs_sem.at[slot]
+        )
+
+    def cross_copy(slot, r, j):
+        return pltpu.make_async_copy(
+            probs_hbm.at[r, j, 1, :, 0], probs.at[slot, 1, :, 0], probs_sem.at[2 + slot]
+        )
+
+    for load in loads[:6]:
+        load.start()
+    far_copy(0, 0, 0).start()
+    for load in loads[6:]:
+        load.start()
+    greet(outer)
+    work = Scatter(
+        outer, pieces, terms + (qkv_terms, vector_terms), shares, rest[:-3], *rest[-3:], times, places
+    )
+    sums[...] = jnp.zeros_like(sums)
+    for load in loads[:6]:
+        load.wait()
+    lane = lane_index(TILE)
+    ones = jnp.ones((TILE, PAIR), jnp.bfloat16)
+
+    def sides(r, pair, tile):
+        span = pl.ds(tile * TILE, TILE)
+        scaled = (grad[r, span, pair].astype(jnp.float32) * inverse[r, span, pair]).astype(jnp.bfloat16)
+        product = scaled.astype(jnp.float32) * att[r, span, pair].astype(jnp.float32)
+        queries = q[r, span, pair]
+        both = []
+        for head in range(2):
+            mine = (lane < HD) if head == 0 else (lane >= HD)
+            delta = -jnp.sum(jnp.where(mine, product, 0.0), axis=-1, keepdims=True)
+            high = delta.astype(jnp.bfloat16).astype(jnp.float32)
+            extra = jnp.where(lane == 0, high, jnp.where(lane == 1, delta - high, 0.0))
+            grads = jnp.where(mine, scaled, jnp.bfloat16(0))
+            mine_queries = jnp.where(mine, queries, jnp.bfloat16(0))
+            both.append(
+                (jnp.concatenate([grads, extra.astype(jnp.bfloat16)], axis=1), grads, mine_queries)
+            )
+        return both
+
+    def unit(r, pair, side, chances, place_of):
+        at = pl.ds(place_of * TILE, TILE)
+        left, grads, mine_queries = side
+        right = jnp.concatenate([v[r, at, pair], ones], axis=1)
+        d_score = (chances.astype(jnp.float32) * dot_nt(left, right)).astype(jnp.bfloat16)
+        return (
+            dot_nn(d_score, k[r, at, pair]),
+            dot_tn(d_score, mine_queries),
+            dot_tn(chances, grads),
+        )
+
+    def far_step(n, carry):
+        r, j = n // pairs, lax.rem(n, pairs)
+        slot = lax.rem(n, 2)
+        pair = pl.ds(pl.multiple_of(j * PAIR, PAIR), PAIR)
+        for t in range(rows * pairs):
+
+            @pl.when(n == t)
+            def _():
+                work.step(t)
+
+        far_copy(slot, r, j).wait()
+
+        @pl.when(n + 1 < rows * pairs)
+        def _():
+            far_copy(1 - slot, (n + 1) // pairs, lax.rem(n + 1, pairs)).start()
+
+        first = unit(r, pair, sides(r, pair, 0)[0], probs[slot, 0, 0, 0], 0)
+        second = unit(r, pair, sides(r, pair, 0)[1], probs[slot, 0, 1, 0], 0)
+        dq_part[r, :, pair] = jnp.where(lane < HD, first[0], second[0])
+        dk[r, 0:TILE, pair] = (first[1] + second[1]).astype(jnp.bfloat16)
+        dv[r, 0:TILE, pair] = (first[2] + second[2]).astype(jnp.bfloat16)
+        return carry
+
+    far_steps = rows * pairs
+    lax.fori_loop(0, far_steps, far_step, 0)
+    near_copy(0, 0, 0).start()
+    cross_copy(0, 0, 0).start()
+    for load in loads[6:8]:
+        load.wait()
+    third = [slice(i * width, (i + 1) * width) for i in range(3)]
+    for r in range(rows):
+        head = slice(0, TILE)
+        prev[r] = (
+            dot_nt(dk[r, head], weight[:, third[1]]) + dot_nt(dv[r, head], weight[:, third[2]])
+        ).astype(jnp.bfloat16)
+    late_copy = remote(prev, late, late_sem.at[0], late_sem.at[1], device(a, y, c, 1 - s))
+
+    @pl.when(s == 1)
+    def _():
+        late_copy.start()
+        late[...] = jnp.zeros_like(late)
+
+    def near_step(n, carry):
+        j, r = n // rows, lax.rem(n, rows)
+        slot = lax.rem(n, 2)
+        pair = pl.ds(pl.multiple_of(j * PAIR, PAIR), PAIR)
+        for t in range(rows * pairs):
+
+            @pl.when(n == t)
+            def _():
+                work.step(far_steps + t)
+
+        near_copy(slot, r, j).wait()
+        cross_copy(slot, r, j).wait()
+
+        @pl.when(n + 1 < rows * pairs)
+        def _():
+            near_copy(1 - slot, lax.rem(n + 1, rows), (n + 1) // rows).start()
+            cross_copy(1 - slot, lax.rem(n + 1, rows), (n + 1) // rows).start()
+
+        scale = 1.0 / math.sqrt(HD)
+        parts = []
+        for head, side in enumerate(sides(r, pair, 0)):
+            parts.append(unit(r, pair, side, probs[slot, 0, head, 1], 1))
+        total = dq_part[r, :, pair] + jnp.where(lane < HD, parts[0][0], parts[1][0])
+        dq[r, 0:TILE, pair] = (total * scale).astype(jnp.bfloat16)
+        dk_sum[...] = parts[0][1] + parts[1][1]
+        dv_sum[...] = parts[0][2] + parts[1][2]
+        queries = []
+        for head, side in enumerate(sides(r, pair, 1)):
+            cross = unit(r, pair, side, probs[slot, 1, head, 0], 1)
+            dk_sum[...] += cross[1]
+            dv_sum[...] += cross[2]
+            near = unit(r, pair, side, probs[slot, 1, head, 1], 2)
+            queries.append(cross[0] + near[0])
+            if head == 0:
+                dk[r, 2 * TILE : 3 * TILE, pair] = near[1].astype(jnp.bfloat16)
+                dv[r, 2 * TILE : 3 * TILE, pair] = near[2].astype(jnp.bfloat16)
+            else:
+                last = dk[r, 2 * TILE : 3 * TILE, pair].astype(jnp.float32) + near[1]
+                dk[r, 2 * TILE : 3 * TILE, pair] = last.astype(jnp.bfloat16)
+                last = dv[r, 2 * TILE : 3 * TILE, pair].astype(jnp.float32) + near[2]
+                dv[r, 2 * TILE : 3 * TILE, pair] = last.astype(jnp.bfloat16)
+        total = jnp.where(lane < HD, queries[0], queries[1])
+        dq[r, TILE : 2 * TILE, pair] = (total * scale).astype(jnp.bfloat16)
+        dk[r, TILE : 2 * TILE, pair] = dk_sum[...].astype(jnp.bfloat16)
+        dv[r, TILE : 2 * TILE, pair] = dv_sum[...].astype(jnp.bfloat16)
+
+        @pl.when((r == rows - 1) & (lax.rem(j, 2) == 1))
+        def _():
+            block = pl.ds(pl.multiple_of((j // 2) * (2 * PAIR), 2 * PAIR), 2 * PAIR)
+            share = qkv_terms.shape[-2]
+            for i, grads in enumerate((dq, dk, dv)):
+                total = None
+                for row in range(rows):
+                    left = normed[row, TILE:] if i == 0 else normed[row]
+                    part = dot_tn(left, grads[row, :, block])
+                    total = part if total is None else total + part
+                to = pl.ds(pl.multiple_of((j // 2) * width + i * 2 * PAIR, 2 * PAIR), 2 * PAIR)
+                qkv_terms[:, :, :, :, :, to] = total.astype(jnp.bfloat16).reshape(
+                    (outer, 2, 2, 2, share, 2 * PAIR)
+                )
+
+        return carry
+
+    near_steps = rows * pairs
+    lax.fori_loop(0, near_steps, near_step, 0)
+    at = far_steps + near_steps
+    for load in loads[8:]:
+        load.wait()
+    stores = []
+    tiles = local // TILE
+    for t in range(tiles):
+        if t == tiles - 1:
+
+            @pl.when(s == 0)
+            def _():
+                late_copy.wait_recv()
+
+        for r in range(rows):
+            work.step(at)
+            at += 1
+            span = slice(t * TILE, (t + 1) * TILE)
+            keys = slice((t + 1) * TILE, (t + 2) * TILE)
+            back = dot_nt(dq[r, span], weight[:, third[0]])
+            back = back + dot_nt(dk[r, keys], weight[:, third[1]])
+            back = back + dot_nt(dv[r, keys], weight[:, third[2]])
+            if t == tiles - 1:
+                back = back + late[r].astype(jnp.float32)
+            normal, scale = normalize(x[r, span].astype(jnp.float32))
+            sums[0:1] += column_sum(back * normal)
+            sums[1:2] += column_sum(back)
+            middle[r, span] = middle[r, span] + norm_grad(back, vectors[0:1], normal, scale)
+            store = pltpu.make_async_copy(
+                middle.at[r, pl.ds(t * TILE, TILE)],
+                tokens_grad_hbm.at[r, pl.ds(t * TILE, TILE)],
+                out_sem.at[t * rows + r],
+            )
+            store.start()
+            stores.append(store)
+    for r in range(rows):
+        sums[2:3] += column_sum(dq[r].astype(jnp.float32))
+        sums[3:4] += column_sum(dv[r].astype(jnp.float32))
+    sums[4:8] = mlp_sums[0:4]
+    size = width // (outer * 8)
+    fc_size = 4 * size
+    total, fc_total = sums[...], mlp_sums[...]
+    for d in range(outer * 8):
+        row, start = divmod(d * fc_size, width)
+        index = (d // 8, (d // 4) % 2, (d // 2) % 2, d % 2)
+        vector_terms[index + (slice(0, 8),)] = pack_columns(total, d * size, size)
+        vector_terms[index + (slice(8, 16),)] = pack_columns(
+            jnp.broadcast_to(fc_total[4 + row : 5 + row], (8, width)), start, fc_size
+        )
+    for t in range(at, work.steps):
+        work.step(t)
+    work.end()
+    for store in stores:
+        store.wait()
+
+    @pl.when(s == 1)
+    def _():
+        late_copy.wait_send()
+
+
+def backward(outer, probs, q, k, v, normed, grad, att, inverse, x, middle_grad, weight, vectors, mlp_sums, fc_grad, attn_grad):
+    rows, local, width = q.shape
+    devices = outer * 8
+    low, full = jnp.bfloat16, jnp.float32
+    share = weight.shape[0] // devices
+    anywhere = pl.BlockSpec(memory_space=pl.ANY)
+    vmem = pl.BlockSpec(memory_space=pltpu.VMEM)
+    terms = [
+        fc_grad.reshape((outer, 2, 2, 2, share, fc_grad.shape[1])),
+        attn_grad.reshape((outer, 2, 2, 2, share, width)),
+    ]
+    blocks = weight.shape[1] // width
+    pieces = column_pieces(0, fc_grad.shape[1], 4, (1, 0, 1, 1)) + [(1, 0, width, 0)]
+    pieces += column_pieces(2, weight.shape[1], 3, (1, 0, 1)) + [(3, 0, PAIR, 0)]
+    part = width // 3
+    places = {
+        5 + b: [(i * part, part, i * width + b * part) for i in range(blocks)] for b in range(3)
+    }
+    times = BACKWARD_TIMES
+    shapes = [(share, fc_grad.shape[1], low), (share, width, low), (share, weight.shape[1], low), (16, PAIR, full)]
+    extended = (rows, local + TILE, width)
+    results = pl.pallas_call(
+        functools.partial(backward_kernel, outer, pieces, times, places, 2),
+        in_specs=[anywhere] * 11 + [vmem] * 2 + [anywhere] * 2,
+        out_specs=[anywhere] + [vmem] * 4,
+        out_shape=[jax.ShapeDtypeStruct(x.shape, full)]
+        + [shares_out(shape[0], shape[1]) for shape in shapes],
+        scratch_shapes=[
+            pltpu.VMEM(q.shape, low),
+            pltpu.VMEM(extended, low),
+            pltpu.VMEM(extended, low),
+            pltpu.VMEM(extended, low),
+            pltpu.VMEM(q.shape, low),
+            pltpu.VMEM(q.shape, low),
+            pltpu.VMEM(q.shape, full),
+            pltpu.VMEM(q.shape, low),
+            pltpu.VMEM(q.shape, full),
+            pltpu.VMEM(weight.shape, low),
+            pltpu.VMEM((2, 2, 2, 2, TILE, TILE), low),
+            pltpu.VMEM(q.shape, low),
+            pltpu.VMEM(extended, low),
+            pltpu.VMEM(extended, low),
+            pltpu.VMEM((rows, TILE, width), full),
+            pltpu.VMEM((TILE, PAIR), full),
+            pltpu.VMEM((TILE, PAIR), full),
+            pltpu.VMEM((rows, TILE, width), low),
+            pltpu.VMEM((rows, TILE, width), low),
+            pltpu.VMEM((outer, 2, 2, 2, share, weight.shape[1]), low),
+            pltpu.VMEM((outer, 2, 2, 2, 16, PAIR), full),
+            pltpu.VMEM((8, width), full),
+            pltpu.SemaphoreType.DMA((10,)),
+            pltpu.SemaphoreType.DMA((4,)),
+            pltpu.SemaphoreType.DMA((rows * local // TILE,)),
+            pltpu.SemaphoreType.DMA((2,)),
+        ]
+        + Scatter.scratch(outer, shapes, pieces),
+        compiler_params=pltpu.CompilerParams(
+            collective_id=4, has_side_effects=True, vmem_limit_bytes=VMEM_LIMIT
+        ),
+    )(probs, q, k, v, normed, grad, att, inverse, x, middle_grad, weight, vectors, mlp_sums, *terms)
+    tokens_grad, fc_share, attn_share, qkv_share, packed = results
+    size = width // devices
+    return tokens_grad, fc_share, attn_share, qkv_share, packed[:8, :size], packed[8, : 4 * size]
+
+
+BACKWARD_TIMES = [
+    (0, 4, 14, 17, 20),
+    (0, 4, 14, 17, 20),
+    (6, 11, 18, 21, 24),
+    (6, 11, 18, 21, 24),
+    (14, 16, 21, 23, 25),
+    (16, 18, 23, 25, 27),
+    (20, 22, 25, 27, 29),
+    (24, 25, 27, 28, 29),
+    (28, 29, 30, 31, 32),
+]
+
+
 def gather_weights(outer, weights, vectors, fc_bias):
     devices = outer * 8
     shards = [pack_vectors(vectors + [fc_bias])]
@@ -1141,20 +1654,31 @@
         normed, q, k, v = project(tokens_in, prev, qkv, vectors)
         probs, att, inverse = attend(starts, q, k, v)
     flat = lambda value: value.reshape(rows * local, width)
-    out, middle_grad, att_grad, attn_grad, fc_grad, proj_grad, mlp_sums = mlp(
-        flat(tokens_in), flat(att), flat(out_grad), attn, fc, proj, vectors
-    )
     block = lambda value: value.reshape(rows, local, width)
-    dq, dk, dv = attend_grad(probs, q, k, v, block(att_grad), att, inverse)
-    qkv_grad, prev_grad, project_sums = project_grad(normed, dq, dk, dv, qkv)
-    late = lax.ppermute(prev_grad, "seq", [(1, 0)])
-    tokens_grad, norm_sums = tokens_grad_of(
-        tokens_in, dq, dk, dv, qkv, late, block(middle_grad), vectors
-    )
-    sums = jnp.concatenate([norm_sums[:2], project_sums[:2], mlp_sums[:4]], axis=0)
-    weights, shares, fc_share = scatter_grads(
-        outer, [qkv_grad, attn_grad, fc_grad, proj_grad], sums, mlp_sums[4:]
-    )
+    if qkv_weight.shape[0] % 8 == 0:
+        out, middle_grad, att_grad, attn_grad, fc_grad, mlp_sums, proj_share = mlp_scatter(
+            outer, flat(tokens_in), flat(att), flat(out_grad), attn, fc, proj, vectors
+        )
+        tokens_grad, fc_share, attn_share, qkv_share, packed, fc_bias_share = backward(
+            outer, probs, q, k, v, normed, block(att_grad), att, inverse, tokens_in, block(middle_grad),
+            qkv, vectors, mlp_sums, fc_grad, attn_grad,
+        )
+        weights = [qkv_share, attn_share, fc_share, proj_share]
+        shares = [packed[i] for i in range(8)]
+    else:
+        out, middle_grad, att_grad, attn_grad, fc_grad, proj_grad, mlp_sums = mlp(
+            flat(tokens_in), flat(att), flat(out_grad), attn, fc, proj, vectors
+        )
+        dq, dk, dv = attend_grad(probs, q, k, v, block(att_grad), att, inverse)
+        qkv_grad, prev_grad, project_sums = project_grad(normed, dq, dk, dv, qkv)
+        late = lax.ppermute(prev_grad, "seq", [(1, 0)])
+        tokens_grad, norm_sums = tokens_grad_of(
+            tokens_in, dq, dk, dv, qkv, late, block(middle_grad), vectors
+        )
+        sums = jnp.concatenate([norm_sums[:2], project_sums[:2], mlp_sums[:4]], axis=0)
+        weights, shares, fc_bias_share = scatter_grads(
+            outer, [qkv_grad, attn_grad, fc_grad, proj_grad], sums, mlp_sums[4:]
+        )
     gain1, bias1, query, value, proj_b, gain2, bias2, attn_b = shares
     return (
         out.reshape(rows, local, width),
@@ -1169,7 +1693,7 @@
         gain2,
         bias2,
         weights[2],
-        fc_share,
+        fc_bias_share,
         weights[3],
         proj_b,
     )

time: 306 us -> 268 us (0.88)
  waiting for transfers between devices: 19 us -> 0 us
  Pallas kernels: 270 us -> 257 us
  local copies, waits for them, and re-layouts: 12.8 us -> 8.42 us
    ppermute x1 -> x0, waiting for transfers between devices: 19 us -> none  [shards(): late = lax.ppermute(prev_grad, 'seq', [(1, 0)])]
    pallas_call x5 -> x2, Pallas kernels: 181 us -> 168 us  [the longest x1 103 us: backward(): pl.pallas_call(functools.partial(backward_kernel, outer, pieces, times, p...]
    slice x5 -> x0, local copies, waits for them, and re-layouts: 4.3 us -> none  [the longest x1 1.57 us: scatter_grads(): vectors = [flat[i * size:(i + 1) * size] for i in range(count)]]
    unnamed x9 -> x18, local copies, waits for them, and re-layouts: 8.13 us -> 5.58 us
  transfers between devices with their start and end apart: 1 -> 0, of which waited for: 1 -> 0; matrix products, arithmetic and copies ran while one was open for 0% -> 0% of each run, Pallas kernels for 0% -> 0%
where the time goes in v4:
time: 268 us
  Pallas kernels  257 us (96%)
  local copies, waits for them, and re-layouts  8.42 us (3%)
    pallas_call x1, Pallas kernels, backward(): pl.pallas_call(functools.partial(backward_kernel, outer, pieces, times, p...  103 us
    pallas_call x1, Pallas kernels, forward(): pl.pallas_call(functools.partial(forward_kernel, outer, pieces), in_specs...  89.6 us
    pallas_call x1, Pallas kernels, mlp_scatter(): pl.pallas_call(functools.partial(mlp_scatter_kernel, outer, pieces, times...  64.6 us
    unnamed x18, local copies, waits for them, and re-layouts  5.58 us

profile of v4, /device:TPU:0, one launch (start us, length us, event | category | flops | bytes accessed | tf_op | source)
XLA Modules:
  0.0 267.6 jit_solution(10827517612948703498)
XLA Ops:
  0.7 1.3 dynamic-slice_subtract_fusion.refs_1_
  2.0 89.6 %shard_map.271 = (bf16[2,768,768]{2,1,0:T(8,128)(2,1)}, bf16[2,512,768]{2,1,0:T(8,128)(2,1)}, bf16[2,768,768]{2,1,0:T(8,128)(2,1)}, bf16[2,768,768]{2,1,0:T(8,12...) custom-call(bf16[2,512,768]{2,1,0:T(8,128)(2,1)} %x_hbm.1, ...), custom_call_target="tpu_custom_call" | custom-call | tf_op jit(solution)/shard_map/pallas_call | solution.py:1025
  91.6 64.6 %shard_map.272 = (bf16[1024,768]{1,0:T(8,128)(2,1)}, f32[1024,768]{1,0:T(8,128)}, bf16[1024,768]{1,0:T(8,128)(2,1)}, bf16[768,768]{1,0:T(8,128)(2,1)}, bf16[768,...) custom-call(bf16[1024,768]{1,0:T(8,128)(2,1)} %bitcast.38, bf16[1024,768]{1,0:T(8,128)(2,1)} %bitcast.39, ...), custom_call_target="tpu_custom_call" | custom-call | tf_op jit(solution)/shard_map/pallas_call | solution.py:1216
  156.2 0.0 copy-start.1
  156.2 103.0 %shard_map.273 = (f32[2,512,768]{2,1,0:T(8,128)}, f32[24,3072]{1,0:T(8,128)}, f32[24,768]{1,0:T(8,128)}, f32[24,2304]{1,0:T(8,128)}, f32[16,128]{1,0:T(8,128)}) custom-call(bf16[2,6,2,2,2,256,256]{6,5,4,3,2,1,0:T(8,128)(2,1)} %get-tuple-element.45.probs_hbm, bf16[2,512,768]{2,1,0:T(8,128)(2,1)} %get-tuple-element.46.q_hbm, ...), custom_call_target="tpu_custom_call" | custom-call | tf_op jit(solution)/shard_map/pallas_call | solution.py:1530
  259.2 0.0 copy-start
  259.2 1.3 slice_bitcast_fusion.1
  260.5 1.5 slice_bitcast_fusion
  262.0 0.0 copy-done.1
  262.0 1.1 copy.37
  263.2 0.0 copy-done
  263.2 0.0 copy-start.4
  263.2 0.0 copy-start.5
  263.2 0.0 copy-start.3
  263.2 0.0 copy-start.2
  263.2 1.7 copy.38
  264.8 0.0 copy-done.4
  264.9 0.7 copy.39
  265.5 0.0 copy-done.5
  265.5 0.6 copy.40
  266.2 0.0 copy-done.3
  266.2 0.7 copy.41
  266.9 0.0 copy-done.2
  266.9 0.7 copy.42
  (1 shorter events, 0.0 us)
Async XLA Ops:
  156.2 105.8 %copy-start.1 = (bf16[1024,768]{1,0:T(8,128)(2,1)S(1)}, bf16[1024,768]{1,0:T(8,128)(2,1)}, u32[]{:S(2)}) copy-start(bf16[1024,768]{1,0:T(8,128)(2,1)} %get-tuple-element.44) | copy-start | bytes 4718596
  259.2 4.0 %copy-start = (f32[2,512,768]{2,1,0:T(8,128)S(1)}, f32[2,512,768]{2,1,0:T(8,128)}, u32[]{:S(2)}) copy-start(f32[2,512,768]{2,1,0:T(8,128)} %get-tuple-element.87) | copy-start | bytes 9437188
  263.2 1.7 copy-start.4
  263.2 2.4 copy-start.5
  263.2 3.0 %copy-start.3 = (f32[24,3072]{1,0:T(8,128)S(1)}, f32[24,3072]{1,0:T(8,128)}, u32[]{:S(2)}) copy-start(f32[24,3072]{1,0:T(8,128)} %get-tuple-element.97) | copy-start | bytes 884740
  263.2 3.7 %copy-start.2 = (f32[96,768]{1,0:T(8,128)S(1)}, f32[96,768]{1,0:T(8,128)}, u32[]{:S(2)}) copy-start(f32[96,768]{1,0:T(8,128)} %get-tuple-element.99) | copy-start | bytes 884740
